TPU v7x, 256 devices: a whole 4x4x8 slice. The times are simulated.
256 devices in a mesh: dp: 16 (over y, x), shard: 16 (over z, core).
Axes of the slice: x: 4, y: 4, z: 8, core: 2. Of those that a mesh axis runs over, the one named last changes fastest.
Arguments:
- features: bfloat16 [131072, 128], P('dp'), may hold values from -160 to 160
- anchors: float32 [2048, 128], P('shard'), may hold values from -6 to 6
- metric: float32 [4, 128], replicated, may hold values from 0.5 to 1.5
- classifier: float32 [128, 172], replicated, may hold values from -0.5 to 0.5
- labels: int32 [131072], P('dp'), may hold values from 0 to 171
- train_mask: int32 [131072], P('dp'), may hold values 0 or 1
Outputs:
- embedding: bfloat16 [131072, 128], P(('dp', 'shard'))
- loss: float32 [], replicated
- grad_classifier: float32 [128, 172], replicated
- grad_anchors: float32 [2048, 128], P('shard')
- grad_metric: float32 [4, 128], replicated
All inputs are finite; a program needn't handle non-finite values. No bound on the sum of `train_mask` on one device may be relied on, other than what follows from the above.
Results may differ from a plain program's by a relative error of at most 0.009.
Values may be sent and summed in bfloat16 or wider, within the bound.
No kernel may reach another device: no remote copies, remote signals or barrier semaphores. Data moves between devices by JAX's collectives and lax.ppermute only.
A program may use at most 128 MiB of HBM per device.

v0:
```python
import jax
import jax.numpy as jnp
from jax import lax
from jax.sharding import PartitionSpec as P

threshold = 0.2
degree_floor = 0.25


def directions(values, metric):
    scaled = values.astype(jnp.float32)[:, None, :] * metric[None, :, :]
    unit_norm = jnp.sqrt(jnp.sum(scaled * scaled, axis=-1, keepdims=True) + 1e-06)
    return (scaled / unit_norm, unit_norm)


def project_back(dir_grad, unit_dirs, unit_norm):
    return (
        dir_grad - unit_dirs * jnp.sum(unit_dirs * dir_grad, axis=-1, keepdims=True)
    ) / unit_norm


def node_head(field_sum, node_raw, own_labels, own_mask, classifier):
    node_degree = node_raw + degree_floor
    node_field = field_sum / node_degree[:, None]
    logits = jnp.dot(
        node_field, classifier, precision=lax.Precision.HIGHEST, preferred_element_type=jnp.float32
    )
    classes = lax.broadcasted_iota(jnp.int32, (1, classifier.shape[1]), 1)
    target = (own_labels[:, None] == classes).astype(jnp.float32)
    residual = own_mask.astype(jnp.float32)[:, None] * (logits - target)
    loss_part = 0.5 * jnp.sum(residual * residual)
    class_part = lax.dot_general(
        node_field,
        residual,
        (((0,), (0,)), ((), ())),
        precision=lax.Precision.HIGHEST,
        preferred_element_type=jnp.float32,
    )
    field_grad = lax.dot_general(
        residual,
        classifier,
        (((1,), (1,)), ((), ())),
        precision=lax.Precision.HIGHEST,
        preferred_element_type=jnp.float32,
    )
    node_grads = (field_grad / node_degree[:, None]).astype(jnp.bfloat16)
    degree_grads = (-jnp.sum(field_grad * node_field, axis=1) / node_degree).astype(jnp.bfloat16)
    return (node_field.astype(jnp.bfloat16), loss_part, class_part, node_grads, degree_grads)


def body(features, anchors, metric, classifier, labels, train_mask):
    row_count, feat_width = features.shape
    head_count = metric.shape[0]
    share_rows = row_count // lax.axis_size("shard")
    share_start = lax.axis_index("shard") * share_rows
    anchor_unit, anchor_norm = directions(anchors, metric)
    anchor_dirs = anchor_unit.reshape(anchors.shape[0], -1).astype(jnp.bfloat16)
    unit_dirs, unit_norm = directions(features, metric)
    node_dirs = unit_dirs.reshape(features.shape[0], -1).astype(jnp.bfloat16)
    score = (
        lax.dot_general(
            node_dirs, anchor_dirs, (((1,), (1,)), ((), ())), preferred_element_type=jnp.float32
        )
        / head_count
    )
    excess = jnp.maximum(score - threshold, jnp.float32(0.0))
    link_weights = excess * excess
    link_b = link_weights.astype(jnp.bfloat16)
    total_part = lax.dot_general(
        link_b, features, (((0,), (0,)), ((), ())), preferred_element_type=jnp.float32
    )
    degree_part = jnp.sum(link_weights, axis=0)
    anchor_total, anchor_raw = lax.psum((total_part, degree_part), "dp")
    anchor_degree = anchor_raw + degree_floor
    anchor_means = (anchor_total / anchor_degree[:, None]).astype(jnp.bfloat16)
    field_part = jnp.dot(link_b, anchor_means, preferred_element_type=jnp.float32)
    row_part = jnp.sum(link_weights, axis=1)
    field_sum, node_raw = lax.psum((field_part, row_part), "shard")
    embedded, loss_part, class_part, all_node_grads, all_degree_grads = node_head(
        field_sum, node_raw, labels, train_mask, classifier
    )
    embedding = lax.dynamic_slice_in_dim(embedded, share_start, share_rows, 0)
    mean_part = lax.dot_general(
        link_b, all_node_grads, (((0,), (0,)), ((), ())), preferred_element_type=jnp.float32
    )
    mean_grads, grad_classifier, loss_sum = lax.psum((mean_part, class_part, loss_part), "dp")
    total_grads = (mean_grads / anchor_degree[:, None]).astype(jnp.bfloat16)
    anchor_degree_grads = -jnp.sum(mean_grads * anchor_total, axis=1) / (
        anchor_degree * anchor_degree
    )
    link_grads = lax.dot_general(
        all_node_grads, anchor_means, (((1,), (1,)), ((), ())), preferred_element_type=jnp.float32
    )
    link_grads = link_grads + lax.dot_general(
        features, total_grads, (((1,), (1,)), ((), ())), preferred_element_type=jnp.float32
    )
    link_grads = (
        link_grads + all_degree_grads.astype(jnp.float32)[:, None] + anchor_degree_grads[None, :]
    )
    score_grads = (link_grads * (2.0 / head_count) * excess).astype(jnp.bfloat16)
    anchor_dir_grads = lax.dot_general(
        score_grads, node_dirs, (((0,), (0,)), ((), ())), preferred_element_type=jnp.float32
    )
    anchor_dir_grads = anchor_dir_grads.reshape(anchors.shape[0], head_count, feat_width)
    node_dir_grads = jnp.dot(score_grads, anchor_dirs, preferred_element_type=jnp.float32).reshape(
        features.shape[0], head_count, feat_width
    )
    anchor_g = project_back(anchor_dir_grads, anchor_unit, anchor_norm)
    node_g = project_back(node_dir_grads, unit_dirs, unit_norm)
    anchor_grad_part = jnp.sum(anchor_g * metric[None, :, :], axis=1)
    metric_part = jnp.sum(anchor_g * anchors[:, None, :], axis=0) + jnp.sum(
        node_g * features.astype(jnp.float32)[:, None, :], axis=0
    )
    grad_anchors = lax.psum(anchor_grad_part, "dp")
    grad_metric = lax.psum(metric_part, ("dp", "shard"))
    loss = loss_sum / (2.0 * row_count * lax.axis_size("dp"))
    return (embedding, loss, grad_classifier, grad_anchors, grad_metric)


def solution(mesh):
    return jax.shard_map(
        body,
        mesh=mesh,
        in_specs=(P("dp", None), P("shard", None), P(), P(), P("dp"), P("dp")),
        out_specs=(P(("dp", "shard"), None), P(), P(), P("shard", None), P()),
        check_vma=False,
    )
```

profile of v0, /device:TPU:1, one launch (start us, length us, event | category | flops | bytes accessed | tf_op | source)
XLA Modules:
  0.0 552.2 jit_solution(16510715723667247967)
XLA Ops:
  7.2 0.0 copy-start
  7.2 0.0 copy-start.12
  7.2 0.0 all-reduce.6.cloned.1.call-start
  7.2 1.0 fusion.29
  8.3 0.0 copy-start.9
  8.3 1.9 convert_element_type.46
  10.2 4.4 fusion.2
  14.6 0.1 add_sqrt_fusion
  14.7 0.0 copy-start.5
  14.7 6.7 %multiply_reduce_fusion.4 = (f32[8192]{0:T(1024)S(1)}, f32[128]{0:T(128)S(1)}, f32[8192,128]{1,0:T(8,128)S(1)}) fusion(f32[128,4]{0,1:T(4,128)S(1)} %add_sqrt_fusion.1, f32[4,128]{1,0:T(4,128)S(1)} %copy-done.12, f32[128,128]{1,0:T(8,128)S(1)} %copy-done.9, f32[8192,4]{0,1:T(4,128)S(1)} %add_sqrt_fusion, f32[8192,128]{1,0:T(8,128)S(1)} %convert_element_type.46), kind=kOutput, calls=%fused_computation.36 | convolution fusion | flops 1092804480 | bytes 8622592 | tf_op jit(solution)/shard_map/dot_general | solution.py:61
  21.4 2.0 copy-done.2
  23.4 1.4 fusion.45
  24.8 0.0 all-reduce.6.cloned.1.call-update
  24.8 0.0 all-reduce.8.cloned.1.call-start
  24.9 34.4 %psum.64 = f32[128]{0:T(128)S(1)} all-reduce(f32[128]{0:T(128)S(1)} %get-tuple-element.6), channel_id=1, replica_groups=mesh['dp'=16,'shard'=16] {'dp'}, use_global_device_ids=true, to_apply=%region_4.0 | all-reduce | flops 128 | bytes 1024 | tf_op jit(solution)/shard_map/psum | solution.py:73
  59.3 58.9 %all-reduce.6.cloned.1.call-done = f32[128,128]{1,0:T(8,128)} async-done(((f32[128,128]{1,0:T(8,128)}), f32[128,128]{1,0:T(8,128)}) %all-reduce.6.cloned.1.call-update) | async-done | bytes 65552 | tf_op jit(solution)/shard_map/psum | solution.py:73
  118.3 4.9 fusion.43
  123.2 0.0 all-reduce.8.cloned.1.call-update
  123.2 0.0 copy-start.11
  123.2 0.0 all-reduce.10.cloned.1.call-start
  123.3 3.4 copy.27
  126.7 0.1 copy.29
  126.8 7.7 %fusion.3 = bf16[8192,512]{0,1:T(8,128)(2,1)} fusion(f32[8192,4]{0,1:T(4,128)S(1)} %add_sqrt_fusion, f32[8192,128]{0,1:T(8,128)} %copy.27, f32[512]{0:T(512)S(1)} %bitcast.71), kind=kLoop, calls=%fused_computation.6 | loop fusion | flops 12582912 | bytes 12716032 | tf_op jit(solution)/shard_map/convert_element_type | solution.py:59
  134.5 0.1 fusion.30
  134.7 45.5 %psum.66 = f32[8192]{0:T(1024)S(1)} all-reduce(f32[8192]{0:T(1024)S(1)} %get-tuple-element.5), channel_id=1, replica_groups=mesh['dp'=16,'shard'=16] {'shard'}, use_global_device_ids=true, to_apply=%region_7.0 | all-reduce | flops 8192 | bytes 65536 | tf_op jit(solution)/shard_map/psum | solution.py:78
  180.2 65.2 %all-reduce.8.cloned.1.call-done = f32[8192,128]{1,0:T(8,128)} async-done(((f32[8192,128]{1,0:T(8,128)}), f32[8192,128]{1,0:T(8,128)}) %all-reduce.8.cloned.1.call-update) | async-done | bytes 4194320 | tf_op jit(solution)/shard_map/psum | solution.py:78
  245.4 5.0 broadcast_divide_fusion
  250.4 7.0 %multiply_reduce_fusion.2 = (f32[]{:T(128)}, f32[8192,172]{0,1:T(8,128)S(1)}) fusion(s32[8192]{0:T(1024)S(1)} %copy-done.10, f32[8192,128]{1,0:T(8,128)S(1)} %broadcast_divide_fusion, f32[128,172]{0,1:T(8,128)S(1)} %copy-done, f32[8192]{0:T(1024)S(1)} %convert_element_type.52), kind=kOutput, calls=%fused_computation.32 | convolution fusion | flops 2172715008 | bytes 9984004 | tf_op jit(solution)/shard_map/dot_general | solution.py:25
  257.4 17.0 %multiply_reduce_fusion.3 = (f32[8192]{0:T(1024)S(1)}, bf16[8192,128]{1,0:T(8,128)(2,1)}) fusion(f32[8192,128]{1,0:T(8,128)S(1)} %broadcast_divide_fusion, f32[8192]{0:T(1024)S(1)} %broadcast_add_fusion, f32[8192,172]{0,1:T(8,128)S(1)} %get-tuple-element.15, f32[128,172]{0,1:T(8,128)S(1)} %copy-done), kind=kOutput, calls=%fused_computation.34 | convolution fusion | flops 2168446976 | bytes 12081152 | tf_op jit(solution)/shard_map/dot_general | solution.py:39
  275.0 9.2 %fusion.48 = f32[128,172]{0,1:T(8,128)} fusion(f32[8192,128]{1,0:T(8,128)} %copy-done.3, f32[8192,172]{0,1:T(8,128)} %copy-done.4), kind=kOutput, calls=%fused_computation.78 | convolution fusion | flops 2164260864 | bytes 9918464 | tf_op jit(solution)/shard_map/dot_general | solution.py:32
  284.3 33.7 %psum.67 = f32[]{:T(128)} all-reduce(f32[]{:T(128)S(6)} %mul.141), channel_id=1, replica_groups=mesh['dp'=16,'shard'=16] {'dp'}, use_global_device_ids=true, to_apply=%region_9.0 | all-reduce | flops 1 | bytes 8 | tf_op jit(solution)/shard_map/psum | solution.py:86
  318.0 4.2 fusion.44
  322.2 0.0 all-reduce.10.cloned.1.call-update
  322.2 0.0 all-reduce.12.cloned.1.call-start
  323.0 4.4 fusion.42
  327.3 1.6 dynamic-slice_convert_fusion
  328.9 85.9 %all-reduce.10.cloned.1.call-done = f32[128,128]{1,0:T(8,128)} async-done(((f32[128,128]{1,0:T(8,128)}), f32[128,128]{1,0:T(8,128)}) %all-reduce.10.cloned.1.call-update) | async-done | bytes 65552 | tf_op jit(solution)/shard_map/psum | solution.py:86
  414.8 0.9 multiply_reduce_fusion.9
  415.8 5.5 fusion.15
  421.3 13.5 %multiply_reduce_fusion.6 = (f32[4,128]{1,0:T(4,128)S(1)}, f32[128,128]{1,0:T(8,128)}) fusion(f32[128,128]{1,0:T(8,128)S(1)} %copy-done.9, f32[4,128]{1,0:T(4,128)S(1)} %copy-done.12, f32[128,4]{0,1:T(4,128)S(1)} %add_sqrt_fusion.1, bf16[8192,128,1]{1,0,2:T(8,128)(2,1)} %fusion.15, bf16[4,128,8192]{2,1,0:T(8,128)(2,1)} %bitcast.68), kind=kOutput, calls=%fused_computation.51 | convolution fusion | flops 2148253696 | bytes 10622976 | tf_op jit(solution)/shard_map/mul | solution.py:18
  434.8 13.2 %fusion = f32[8192,4,128]{2,0,1:T(8,128)} fusion(f32[8192,4]{0,1:T(4,128)S(1)} %add_sqrt_fusion, f32[4,128]{1,0:T(4,128)S(1)} %copy-done.12, f32[8192,128]{1,0:T(8,128)} %copy-done.6, bf16[8192,128,1]{1,0,2:T(8,128)(2,1)S(1)} %copy-done.7, bf16[4,128,128]{2,1,0:T(8,128)(2,1)S(1)} %bitcast.69), kind=kOutput, calls=%fused_computation | convolution fusion | flops 1086357632 | bytes 23332864 | tf_op jit(solution)/shard_map/mul | solution.py:18
  448.0 0.0 all-reduce.12.cloned.1.call-update
  448.0 0.0 copy-start.1
  448.0 10.3 %multiply_reduce_fusion = f32[4,128]{1,0:T(4,128)S(1)} fusion(f32[8192,4,128]{2,0,1:T(8,128)} %fusion, f32[8192,4]{0,1:T(4,128)S(1)} %add_sqrt_fusion, f32[4,128]{1,0:T(4,128)S(1)} %copy-done.12, f32[8192,128]{1,0:T(8,128)} %copy-done.6, bf16[8192,128,1]{1,0,2:T(8,128)(2,1)S(1)} %copy-done.7, bf16[4,128,128]{2,1,0:T(8,128)(2,1)S(1)} %bitcast.70), kind=kOutput, calls=%fused_computation.8 | convolution fusion | flops 1103101440 | bytes 23334912 | tf_op jit(solution)/shard_map/dot_general | solution.py:105
  458.4 77.1 %psum.71 = f32[4,128]{1,0:T(4,128)} all-reduce(f32[4,128]{1,0:T(4,128)S(1)} %add.92), channel_id=1, replica_groups=mesh['dp'=16,'shard'=16] {'dp','shard'}, use_global_device_ids=true, to_apply=%region_20.0 | all-reduce | flops 512 | bytes 4096 | tf_op jit(solution)/shard_map/psum | solution.py:115
  535.4 5.6 %all-reduce.12.cloned.1.call-done = (f32[128,172]{0,1:T(8,128)}, f32[128,128]{1,0:T(8,128)}) async-done(((f32[128,172]{0,1:T(8,128)}, f32[128,128]{1,0:T(8,128)}), (f32[128,172]{0,1:T(8,128)}, f32[128,128]{1,0:T(8,128)})) %all-reduce.12.cloned.1.call-update) | async-done | bytes 153616 | tf_op jit(solution)/shard_map/psum | solution.py:86
  541.0 1.5 copy.36
  542.5 1.5 copy.37
  (26 shorter events, 0.1 us)
Async XLA Ops:
  7.2 243.2 %copy-start = (f32[128,172]{0,1:T(8,128)S(1)}, f32[128,172]{0,1:T(8,128)}, u32[]{:S(2)}) copy-start(f32[128,172]{0,1:T(8,128)} %param.9) | copy-start | bytes 264196
  7.2 3.0 copy-start.12
  7.2 111.1 %all-reduce.6.cloned.1.call-start = ((), (), s32[]{:S(2)}) async-start(), calls=%async_computation | async-start | bytes 131072 | tf_op jit(solution)/shard_map/psum | solution.py:73
  8.3 6.5 %copy-start.9 = (f32[128,128]{1,0:T(8,128)S(1)}, f32[128,128]{1,0:T(8,128)}, u32[]{:S(2)}) copy-start(f32[128,128]{1,0:T(8,128)} %param.7) | copy-start | bytes 196612
  10.2 11.2 %copy-start.6 = (f32[8192,128]{1,0:T(8,128)}, f32[8192,128]{1,0:T(8,128)S(1)}, u32[]{:S(2)}) copy-start(f32[8192,128]{1,0:T(8,128)S(1)} %convert_element_type.46) | copy-start | bytes 12582916
  14.7 8.7 %copy-start.5 = (bf16[8192,128]{1,0:T(8,128)(2,1)S(1)}, bf16[8192,128]{1,0:T(8,128)(2,1)}, u32[]{:S(2)}) copy-start(bf16[8192,128]{1,0:T(8,128)(2,1)} %param.6) | copy-start | bytes 6291460
  21.4 2.0 copy-start.2
  24.8 220.5 %all-reduce.8.cloned.1.call-start = ((), (), s32[]{:S(2)}) async-start(), calls=%async_computation.1 | async-start | bytes 8388608 | tf_op jit(solution)/shard_map/psum | solution.py:78
  123.2 3.6 copy-start.11
  123.2 291.6 %all-reduce.10.cloned.1.call-start = ((), (), s32[]{:S(2)}) async-start(), calls=%async_computation.2 | async-start | bytes 131072 | tf_op jit(solution)/shard_map/psum | solution.py:86
  180.2 70.2 %copy-start.10 = (s32[8192]{0:T(1024)S(1)}, s32[8192]{0:T(1024)}, u32[]{:S(2)}) copy-start(s32[8192]{0:T(1024)} %param.10) | copy-start | bytes 98308
  250.4 7.0 %copy-start.3 = (f32[8192,128]{1,0:T(8,128)}, f32[8192,128]{1,0:T(8,128)S(1)}, u32[]{:S(2)}) copy-start(f32[8192,128]{1,0:T(8,128)S(1)} %broadcast_divide_fusion) | copy-start | bytes 12582916
  257.4 17.0 %copy-start.4 = (f32[8192,172]{0,1:T(8,128)}, f32[8192,172]{0,1:T(8,128)S(1)}, u32[]{:S(2)}) copy-start(f32[8192,172]{0,1:T(8,128)S(1)} %get-tuple-element.15) | copy-start | bytes 16908292
  284.3 38.7 %copy-start.8 = (f32[128,128]{1,0:T(8,128)S(1)}, f32[128,128]{1,0:T(8,128)}, u32[]{:S(2)}) copy-start(f32[128,128]{1,0:T(8,128)} %all-reduce.6.cloned.1.call-done) | copy-start | bytes 196612
  322.2 218.8 %all-reduce.12.cloned.1.call-start = ((), (), s32[]{:S(2)}) async-start(), calls=%async_computation.3 | async-start | bytes 311296 | tf_op jit(solution)/shard_map/psum | solution.py:86
  421.3 13.5 %copy-start.7 = (bf16[8192,128,1]{1,0,2:T(8,128)(2,1)S(1)}, bf16[8192,128,1]{1,0,2:T(8,128)(2,1)}, u32[]{:S(2)}) copy-start(bf16[8192,128,1]{1,0,2:T(8,128)(2,1)} %fusion.15) | copy-start | bytes 6291460
  448.0 96.0 %copy-start.1 = (f32[128,172]{0,1:T(8,128)S(1)}, f32[128,172]{0,1:T(8,128)}, u32[]{:S(2)}) copy-start(f32[128,172]{0,1:T(8,128)} %param.9) | copy-start | bytes 264196
Sparse Core Ops, SparseCore 0:
  25.0 93.2 all-reduce.5
  123.3 122.0 all-reduce.7
  322.4 92.4 all-reduce.9
  448.1 92.8 all-reduce.11
where the time goes:
time: 561 us; the launch traced here: 552 us
  waiting for transfers between devices  216 us (39%)
  blocking collectives  191 us (34%)
  matrix products  97.3 us (17%)
  other arithmetic  21.3 us (4%)
  between operations  16.9 us (3%)
  local copies, waits for them, and re-layouts  10.1 us (2%)
    psum x2, waiting for transfers between devices, body(): lax.psum((mean_part, class_part, loss_part), 'dp')  91.4 us
    psum x1, blocking collectives, body(): grad_metric = lax.psum(metric_part, ('dp', 'shard'))  77.1 us
    psum x1, waiting for transfers between devices, body(): field_sum, node_raw = lax.psum((field_part, row_part), 'shard')  65.2 us
    psum x1, waiting for transfers between devices, body(): anchor_total, anchor_raw = lax.psum((total_part, degree_part), 'dp')  58.9 us
    psum x1, blocking collectives, body(): field_sum, node_raw = lax.psum((field_part, row_part), 'shard')  45.5 us
    psum x1, blocking collectives, body(): anchor_total, anchor_raw = lax.psum((total_part, degree_part), 'dp')  34.4 us
    psum x1, blocking collectives, body(): lax.psum((mean_part, class_part, loss_part), 'dp')  33.7 us
    mul x2, matrix products, project_back(): unit_dirs * jnp.sum(unit_dirs * dir_grad, axis=-1, keepdims=True)  26.7 us
  transfers between devices with their start and end apart: 4, of which 4 were waited for; matrix products, arithmetic and copies ran while one was open for 5% of the time, Pallas kernels for 0%

commit v1 on v0

v1 whole, which is shorter than its diff:
```python
import jax
import jax.numpy as jnp
from jax import lax
from jax.experimental import pallas as pl
from jax.experimental.pallas import tpu as pltpu
from jax.sharding import Mesh
from jax.sharding import PartitionSpec as P

f32, bf16 = jnp.float32, jnp.bfloat16

threshold = 0.2
degree_floor = 0.25
F = 128
HEADS = 4
CLASSES = 172
CPAD = 256
OWN = 512
APD = 128
NZ = 8
VMEM = 48 * 1024 * 1024

NN = ((1,), (0,))
NT = ((1,), (1,))
TN = ((0,), (0,))


def mm(a, b, dims, precision=None):
    return lax.dot_general(a, b, (dims, ((), ())), precision=precision, preferred_element_type=f32)


def params(**kw):
    return pltpu.CompilerParams(vmem_limit_bytes=VMEM, **kw)


def vspec():
    return pl.BlockSpec(memory_space=pltpu.VMEM)


def column(row):
    return jnp.broadcast_to(row, (row.shape[1], row.shape[1])).T


def anchor_rows(anchors, metric, h):
    m = metric[h : h + 1, :]
    u = anchors * m
    r = lax.rsqrt(jnp.sum(u * u, axis=1, keepdims=True) + 1e-06)
    return u, r, m


def scaled_dirs(anchors, metric):
    rows = []
    for h in range(HEADS):
        u, r, m = anchor_rows(anchors, metric, h)
        rows.append((u * r * (m * (1.0 / HEADS))).astype(bf16))
    return jnp.concatenate(rows, axis=0)


def head_scores(am, ft, rinv):
    prod = mm(am, ft, NN)
    return [prod[h * APD : (h + 1) * APD, :] * rinv[h : h + 1, :] for h in range(HEADS)]


def excess_of(parts):
    score = (parts[0] + parts[1]) + (parts[2] + parts[3])
    return jnp.maximum(score - threshold, 0.0)


LINK_BLOCK = 1024
CHUNK = 256


def link_kernel(f_ref, a_ref, m_ref, ft_ref, rinv_ref, lb_ref, am_ref, msg_ref, tot, raw, m2c):
    i = pl.program_id(0)

    @pl.when(i == 0)
    def _():
        am_ref[...] = scaled_dirs(a_ref[...], m_ref[...])
        for h in range(HEADS):
            m = m_ref[h : h + 1, :]
            m2c[h] = column(m * m)
        tot[...] = jnp.zeros_like(tot)
        raw[...] = jnp.zeros_like(raw)

    for j in range(LINK_BLOCK // CHUNK):
        cols = slice(j * CHUNK, (j + 1) * CHUNK)
        ft = f_ref[cols, :].astype(f32).T
        ft_b = ft.astype(bf16)
        ft_ref[:, cols] = ft_b
        sq = ft * ft
        norms = []
        for h in range(HEADS):
            m2 = jnp.concatenate([m2c[h]] * (CHUNK // F), axis=1)
            norms.append(jnp.sum(sq * m2, axis=0, keepdims=True))
        rinv = lax.rsqrt(jnp.concatenate(norms + norms, axis=0) + 1e-06)
        rinv_ref[:, cols] = rinv
        e = excess_of(head_scores(am_ref[...], ft_b, rinv))
        link = e * e
        lb_ref[:, cols] = link.astype(bf16)
        raw[...] += sum(link[:, k * F : (k + 1) * F] for k in range(CHUNK // F))
    tot[...] += mm(lb_ref[...], f_ref[...], NN)

    @pl.when(i == pl.num_programs(0) - 1)
    def _():
        msg_ref[0:APD, :] = tot[...].astype(bf16)
        t = raw[...].T
        msg_ref[APD : APD + 16, :] = sum(t[16 * k : 16 * k + 16, :] for k in range(8)).astype(bf16)


def link_call(features, anchors, metric):
    n = features.shape[0]
    const = lambda i: (0, 0)
    return pl.pallas_call(
        link_kernel,
        grid=(n // LINK_BLOCK,),
        in_specs=[
            pl.BlockSpec((LINK_BLOCK, F), lambda i: (i, 0)),
            pl.BlockSpec((APD, F), const),
            pl.BlockSpec((HEADS, F), const),
        ],
        out_specs=[
            pl.BlockSpec((F, LINK_BLOCK), lambda i: (0, i)),
            pl.BlockSpec((8, LINK_BLOCK), lambda i: (0, i)),
            pl.BlockSpec((APD, LINK_BLOCK), lambda i: (0, i)),
            pl.BlockSpec((HEADS * APD, F), const),
            pl.BlockSpec((APD + 16, F), const),
        ],
        out_shape=[
            jax.ShapeDtypeStruct((F, n), bf16),
            jax.ShapeDtypeStruct((8, n), f32),
            jax.ShapeDtypeStruct((APD, n), bf16),
            jax.ShapeDtypeStruct((HEADS * APD, F), bf16),
            jax.ShapeDtypeStruct((APD + 16, F), bf16),
        ],
        scratch_shapes=[
            pltpu.VMEM((APD, F), f32),
            pltpu.VMEM((APD, F), f32),
            pltpu.VMEM((HEADS, F, F), f32),
        ],
        compiler_params=params(),
    )(features, anchors, metric)


def four(a, b, c, d):
    return (a[...].astype(f32) + b[...].astype(f32)) + (c[...].astype(f32) + d[...].astype(f32))


def mean_kernel(a, b, c, d, total_ref, degree_ref, means_ref):
    s = four(a, b, c, d)
    total = s[0:APD, :]
    degree = column(jnp.sum(s[APD:, :], axis=0, keepdims=True) + degree_floor)
    total_ref[...] = total
    degree_ref[...] = degree
    means = (total / degree).astype(bf16)
    for z in range(NZ):
        means_ref[z] = means


def mean_call(parts):
    return pl.pallas_call(
        mean_kernel,
        in_specs=[vspec()] * 4,
        out_specs=[vspec()] * 3,
        out_shape=[
            jax.ShapeDtypeStruct((APD, F), f32),
            jax.ShapeDtypeStruct((APD, F), f32),
            jax.ShapeDtypeStruct((NZ, APD, F), bf16),
        ],
        compiler_params=params(),
    )(*parts)


def head_kernel(s_ref, all_ref, m_ref, ft_ref, rinv_ref, ma_ref, mb_ref, cls_ref, lab_ref, mask_ref, emb_ref, msg_ref):
    core = lax.rem(s_ref[0], 2)
    metric = m_ref[...]
    ft = ft_ref[...]
    rinv = rinv_ref[...]

    def links(z, which, means_ref, field, raw):
        shard = 2 * z + which
        rows = pl.ds(pl.multiple_of(shard * APD, APD), APD)
        am = scaled_dirs(all_ref[rows, :], metric)
        e = excess_of(head_scores(am, ft, rinv))
        link = e * e
        field = field + mm(means_ref[z], link.astype(bf16), TN)
        raw = raw + sum(link[8 * k : 8 * k + 8, :] for k in range(APD // 8))
        return field, raw

    def step(z, carry):
        field, raw = links(z, core, ma_ref, *carry)
        return links(z, 1 - core, mb_ref, field, raw)

    field, raw = lax.fori_loop(0, NZ, step, (jnp.zeros((F, OWN), f32), jnp.zeros((8, OWN), f32)))
    inv_degree = 1.0 / (jnp.sum(raw, axis=0, keepdims=True) + degree_floor)
    field = field * inv_degree
    emb_ref[...] = field.T.astype(bf16)
    highest = lax.Precision.HIGHEST
    cls_t = cls_ref[...]
    logits = mm(cls_t, field, NN, highest)
    ids = lax.broadcasted_iota(jnp.int32, (CPAD, OWN), 0)
    target = jnp.where(ids == lab_ref[...], 1.0, 0.0)
    residual = mask_ref[...].astype(f32) * (logits - target)
    loss_row = jnp.sum(residual * residual, axis=0, keepdims=True)
    loss_row = sum(loss_row[:, k * F : (k + 1) * F] for k in range(OWN // F))
    class_part = mm(residual, field, NT, highest).astype(bf16)
    field_grad = mm(cls_t.T, residual, NN, highest)
    node_grads = (field_grad * inv_degree).astype(bf16)
    degree_grads = -jnp.sum(field_grad * field, axis=0, keepdims=True) * inv_degree
    small = jnp.concatenate(
        [degree_grads[:, k * F : (k + 1) * F] for k in range(OWN // F)] + [loss_row, jnp.zeros((11, F), f32)], axis=0
    ).astype(bf16)
    empty = jnp.zeros((16, F), bf16)
    for z in range(NZ):
        msg_ref[z, 0:F, :] = node_grads
        msg_ref[z, F : F + 16, 0:F] = class_part[32 * z : 32 * z + 16, :]
        msg_ref[z, F : F + 16, F : 2 * F] = class_part[32 * z + 16 : 32 * z + 32, :]
        msg_ref[z, F : F + 16, 2 * F : 3 * F] = small
        msg_ref[z, F : F + 16, 3 * F : 4 * F] = empty


def head_call(shard, anchors_all, metric, ft, rinv, means_a, means_b, cls_t, labels, mask):
    zero2 = lambda i, s: (0, 0)
    zero3 = lambda i, s: (0, 0, 0)
    own = lambda i, s: (0, s[0])
    return pl.pallas_call(
        head_kernel,
        grid_spec=pltpu.PrefetchScalarGridSpec(
            num_scalar_prefetch=1,
            grid=(1,),
            in_specs=[
                pl.BlockSpec(anchors_all.shape, zero2),
                pl.BlockSpec((HEADS, F), zero2),
                pl.BlockSpec((F, OWN), own),
                pl.BlockSpec((8, OWN), own),
                pl.BlockSpec((NZ, APD, F), zero3),
                pl.BlockSpec((NZ, APD, F), zero3),
                pl.BlockSpec((CPAD, F), zero2),
                pl.BlockSpec((1, OWN), own),
                pl.BlockSpec((1, OWN), own),
            ],
            out_specs=[
                pl.BlockSpec((OWN, F), zero2),
                pl.BlockSpec((NZ, F + 16, OWN), zero3),
            ],
        ),
        out_shape=[
            jax.ShapeDtypeStruct((OWN, F), bf16),
            jax.ShapeDtypeStruct((NZ, F + 16, OWN), bf16),
        ],
        compiler_params=params(),
    )(shard, anchors_all, metric, ft, rinv, means_a, means_b, cls_t, labels, mask)


def mean_grad_kernel(s_ref, lb_ref, ga_ref, gb_ref, msg_ref, loss_ref):
    core = lax.rem(s_ref[0], 2)
    grads = jnp.zeros((APD, F), f32)
    for z in range(NZ):
        for which, ref in ((core, ga_ref), (1 - core, gb_ref)):
            cols = pl.ds(pl.multiple_of((2 * z + which) * OWN, OWN), OWN)
            grads = grads + mm(lb_ref[:, cols], ref[z, 0:F, :], NT)
    msg_ref[0:APD, :] = grads.astype(bf16)
    extra = []
    for ref in (ga_ref, gb_ref):
        s = ref[0, F : F + 16, :].astype(f32)
        for z in range(1, NZ):
            s = s + ref[z, F : F + 16, :].astype(f32)
        extra.append(s)
    extra = extra[0] + extra[1]
    msg_ref[APD : APD + 16, :] = extra[:, 0:F].astype(bf16)
    msg_ref[APD + 16 : APD + 32, :] = extra[:, F : 2 * F].astype(bf16)
    loss_ref[...] = extra[0:8, 2 * F : 3 * F]


def mean_grad_call(shard, lb, grads_a, grads_b):
    return pl.pallas_call(
        mean_grad_kernel,
        in_specs=[pl.BlockSpec(memory_space=pltpu.SMEM)] + [vspec()] * 3,
        out_specs=[vspec()] * 2,
        out_shape=[
            jax.ShapeDtypeStruct((APD + 32, F), bf16),
            jax.ShapeDtypeStruct((8, F), f32),
        ],
        compiler_params=params(),
    )(shard, lb, grads_a, grads_b)


def score_kernel(
    s_ref, f0_ref, f1_ref, ft0_ref, ft1_ref, r0_ref, r1_ref, ga_ref, gb_ref, am_ref, a_ref, m_ref, means_ref, total_ref, degree_ref, loss_ref,
    p0, p1, p2, p3, msg_ref, cls_ref, acc, vacc, tg, adg, sgr
):
    i = pl.program_id(0)

    @pl.when(i == 0)
    def _():
        s = four(p0, p1, p2, p3)
        cls_ref[...] = s[APD:, :]
        grads = s[0:APD, :]
        inv = 1.0 / degree_ref[...]
        tg[...] = (grads * inv).astype(bf16)
        dots = jnp.sum(grads * total_ref[...], axis=1, keepdims=True)
        adg[...] = -dots * (inv * inv)
        acc[...] = jnp.zeros_like(acc)
        vacc[...] = jnp.zeros_like(vacc)

    am = am_ref[...]
    for f_ref, ft_ref, r_ref, g_ref in ((f0_ref, ft0_ref, r0_ref, ga_ref), (f1_ref, ft1_ref, r1_ref, gb_ref)):
        rows = []
        for j in range(OWN // CHUNK):
            cols = slice(j * CHUNK, (j + 1) * CHUNK)
            ft = ft_ref[:, cols]
            rinv = r_ref[:, cols]
            dg = jnp.concatenate([g_ref[0, F : F + 16, 2 * F : 3 * F].astype(f32)[k : k + 1, :] for k in range(2 * j, 2 * j + 2)], axis=1)
            parts = head_scores(am, ft, rinv)
            e = excess_of(parts)
            link_grads = mm(means_ref[...], g_ref[0, 0:F, cols], NN) + mm(tg[...], ft, NN)
            link_grads = link_grads + dg + jnp.concatenate([adg[...]] * (CHUNK // F), axis=1)
            sg = link_grads * (2.0 / HEADS) * e
            ws = []
            for h in range(HEADS):
                r = rinv[h : h + 1, :]
                sgr[h * APD : (h + 1) * APD, cols] = (sg * r).astype(bf16)
                ws.append(jnp.sum(sg * parts[h], axis=0, keepdims=True) * (r * r))
            w = jnp.concatenate(ws, axis=0)
            hi = w.astype(bf16).astype(f32)
            rows.append(jnp.concatenate([hi, w - hi], axis=0))
        v = jnp.concatenate(rows, axis=1).astype(bf16)
        fb = f_ref[...]
        acc[...] += mm(sgr[...], fb, NN)
        sq = fb.astype(f32)
        sq = sq * sq
        sq_hi = sq.astype(bf16)
        sq_lo = (sq - sq_hi.astype(f32)).astype(bf16)
        vacc[...] += mm(v, sq_hi, NN) + mm(v, sq_lo, NN)

    @pl.when(i == pl.num_programs(0) - 1)
    def _():
        anchors = a_ref[...]
        metric = m_ref[...]
        out = jnp.zeros((APD, F), f32)
        rows = []
        for h in range(HEADS):
            u, r, m = anchor_rows(anchors, metric, h)
            unit = u * r
            raw = acc[h * APD : (h + 1) * APD, :]
            grad = raw * m
            g = (grad - unit * jnp.sum(unit * grad, axis=1, keepdims=True)) * r
            out = out + g * m
            dirs = am_ref[h * APD : (h + 1) * APD, :].astype(f32)
            along = vacc[h : h + 1, :] + vacc[HEADS + h : HEADS + h + 1, :]
            row = jnp.sum(g * anchors, axis=0, keepdims=True)
            row = row + jnp.sum(dirs * raw, axis=0, keepdims=True) * (HEADS / m)
            rows.append(row - (m * HEADS) * along)
        msg_ref[0:APD, :] = out.astype(bf16)
        rows.append(loss_ref[4:5, :])
        rows.append(jnp.zeros((11, F), f32))
        msg_ref[APD : APD + 16, :] = jnp.concatenate(rows, axis=0).astype(bf16)


def score_call(shard, features, ft, rinv, grads_a, grads_b, am, anchors, metric, means, total, degree, loss, parts):
    n = features.shape[0]
    near = lambda i, s: 2 * i + s[0] % 2
    far = lambda i, s: 2 * i + 1 - s[0] % 2
    c2 = lambda i, s: (0, 0)
    whole = lambda x: pl.BlockSpec(x.shape, c2)
    return pl.pallas_call(
        score_kernel,
        grid_spec=pltpu.PrefetchScalarGridSpec(
            num_scalar_prefetch=1,
            grid=(NZ,),
            in_specs=[
                pl.BlockSpec((OWN, F), lambda i, s: (near(i, s), 0)),
                pl.BlockSpec((OWN, F), lambda i, s: (far(i, s), 0)),
                pl.BlockSpec((F, OWN), lambda i, s: (0, near(i, s))),
                pl.BlockSpec((F, OWN), lambda i, s: (0, far(i, s))),
                pl.BlockSpec((8, OWN), lambda i, s: (0, near(i, s))),
                pl.BlockSpec((8, OWN), lambda i, s: (0, far(i, s))),
                pl.BlockSpec((1, F + 16, OWN), lambda i, s: (i, 0, 0)),
                pl.BlockSpec((1, F + 16, OWN), lambda i, s: (i, 0, 0)),
                whole(am),
                whole(anchors),
                whole(metric),
                whole(means),
                whole(total),
                whole(degree),
                whole(loss),
            ]
            + [whole(p) for p in parts],
            out_specs=[pl.BlockSpec((APD + 16, F), c2), pl.BlockSpec((32, F), c2)],
            scratch_shapes=[
                pltpu.VMEM((HEADS * APD, F), f32),
                pltpu.VMEM((8, F), f32),
                pltpu.VMEM((APD, F), bf16),
                pltpu.VMEM((APD, F), f32),
                pltpu.VMEM((HEADS * APD, OWN), bf16),
            ],
        ),
        out_shape=[
            jax.ShapeDtypeStruct((APD + 16, F), bf16),
            jax.ShapeDtypeStruct((32, F), f32),
        ],
        compiler_params=params(),
    )(shard, features, features, ft, ft, rinv, rinv, grads_a, grads_b, am, anchors, metric, means, total, degree, loss, *parts)


def last_kernel(scale, p0, p1, p2, p3, cls_ref, out_ref, loss_ref, msg_ref):
    s = four(p0, p1, p2, p3)
    out_ref[...] = s[0:APD, :]
    loss_ref[...] = jnp.sum(s[APD + 4 : APD + 5, :], axis=1, keepdims=True) * scale
    for k in range(2 * NZ):
        msg_ref[k, 0:8, :] = s[APD : APD + 8, :]
        msg_ref[k, 8:40, :] = cls_ref[...]


def last_call(parts, cls, scale):
    return pl.pallas_call(
        lambda *refs: last_kernel(scale, *refs),
        in_specs=[vspec()] * 5,
        out_specs=[vspec()] * 3,
        out_shape=[
            jax.ShapeDtypeStruct((APD, F), f32),
            jax.ShapeDtypeStruct((1, 1), f32),
            jax.ShapeDtypeStruct((2 * NZ, 40, F), f32),
        ],
        compiler_params=params(),
    )(*parts, cls)


def finish_kernel(x_ref, metric_ref, cls_ref):
    s = x_ref[0, 0:8, :]
    for k in range(1, 2 * NZ):
        s = s + x_ref[k, 0:8, :]
    metric_ref[...] = s[0:HEADS, :]
    for z in range(NZ):
        rows = min(32, CLASSES - 32 * z)
        if rows > 0:
            cls_ref[32 * z : 32 * z + rows, :] = x_ref[2 * z, 8 : 8 + rows, :]


def finish_call(x):
    return pl.pallas_call(
        finish_kernel,
        in_specs=[vspec()],
        out_specs=[vspec()] * 2,
        out_shape=[jax.ShapeDtypeStruct((HEADS, F), f32), jax.ShapeDtypeStruct((CLASSES, F), f32)],
        compiler_params=params(),
    )(x)


def swap(x):
    return lax.ppermute(x, "c", [(0, 1), (1, 0)])


def shared(x, axis):
    others = [lax.ppermute(x, axis, [(i, i ^ k) for i in range(4)]) for k in (1, 2, 3)]
    return [x] + others


def sum4(parts):
    a, b, c, d = (p.astype(f32) for p in parts)
    return ((a + b) + (c + d)).astype(bf16)


def over_dp(x):
    return shared(sum4(shared(x, "x")), "y")


def body(features, anchors, metric, classifier, labels, train_mask):
    n = features.shape[0]
    shard = (lax.axis_index("z") * 2 + lax.axis_index("c")).astype(jnp.int32).reshape(1)
    anchors_all = lax.all_gather(anchors, ("z", "c"), tiled=True)
    cls_t = jnp.pad(classifier.T, ((0, CPAD - CLASSES), (0, 0)))
    ft, rinv, lb, am, msg = link_call(features, anchors, metric)
    total, degree, means8 = mean_call(over_dp(msg))
    means_a = lax.all_to_all(means8, "z", 0, 0, tiled=True)
    means_b = swap(means_a)
    embedding, msg = head_call(
        shard, anchors_all, metric, ft, rinv, means_a, means_b, cls_t, labels.reshape(1, n), train_mask.reshape(1, n)
    )
    grads_a = lax.all_to_all(msg, "z", 0, 0, tiled=True)
    grads_b = swap(grads_a)
    msg, loss = mean_grad_call(shard, lb, grads_a, grads_b)
    msg, cls = score_call(
        shard, features, ft, rinv, grads_a, grads_b, am, anchors, metric, means8[0], total, degree, loss, over_dp(msg)
    )
    grad_anchors, loss, msg = last_call(over_dp(msg), cls, 1.0 / (4.0 * n * 16))
    grad_metric, grad_cls = finish_call(lax.all_to_all(msg, ("z", "c"), 0, 0, tiled=True))
    return (embedding, loss.reshape(()), grad_cls.T, grad_anchors, grad_metric)


def solution(mesh):
    grid = Mesh(mesh.devices.reshape(4, 4, 8, 2), ("y", "x", "z", "c"))
    dp, sh = ("y", "x"), ("z", "c")
    return jax.shard_map(
        body,
        mesh=grid,
        in_specs=(P(dp, None), P(sh, None), P(), P(), P(dp), P(dp)),
        out_specs=(P(dp + sh, None), P(), P(), P(sh, None), P()),
        check_vma=False,
    )
```

time: 561 us -> 174 us (0.31); the launches traced: 552 us -> 173 us
  waiting for transfers between devices: 216 us -> 20.5 us
  blocking collectives: 191 us -> 73.4 us
  matrix products: 97.3 us -> 0 us
  Pallas kernels: 0 us -> 32.6 us
  starting transfers between devices: 0.16 us -> 26.3 us
  other arithmetic: 21.3 us -> 0.07 us
    psum x4 -> x0, waiting for transfers between devices: 216 us -> none  [the longest x2 91.4 us: body(): lax.psum((mean_part, class_part, loss_part), 'dp')]
    psum x4 -> x0, blocking collectives: 191 us -> none  [the longest x1 77.1 us: body(): grad_metric = lax.psum(metric_part, ('dp', 'shard'))]
    all_to_all x0 -> x3, blocking collectives: none -> 73.4 us  [the longest x1 34.5 us: body(): grads_a = lax.all_to_all(msg, 'z', 0, 0, tiled=True)]
    dot_general x10 -> x0, matrix products: 70.6 us -> none  [the longest x1 17 us: node_head(): lax.dot_general(residual, classifier, (((1,), (1,)), ((), ())), precision...]
    pallas_call x0 -> x7, Pallas kernels: none -> 32.6 us  [the longest x1 12.7 us: score_call(): pl.pallas_call(score_kernel, grid_spec=pltpu.PrefetchScalarGridSpec(num_s...]
    mul x2 -> x0, matrix products: 26.7 us -> none  [project_back(): unit_dirs * jnp.sum(unit_dirs * dir_grad, axis=-1, keepdims=True)]
    ppermute x0 -> x20, starting transfers between devices: none -> 26.2 us  [the longest x18 20.7 us: shared(): lax.ppermute(x, axis, [(i, i ^ k) for i in range(4)])]
    ppermute x0 -> x20, waiting for transfers between devices: none -> 19.8 us  [the longest x18 17.1 us: shared(): lax.ppermute(x, axis, [(i, i ^ k) for i in range(4)])]
  transfers between devices with their start and end apart: 4 -> 21, of which waited for: 4 -> 14; matrix products, arithmetic and copies ran while one was open for 5% -> 1% of each run, Pallas kernels for 0% -> 5%
where the time goes in v1:
time: 174 us; the launch traced here: 173 us
  blocking collectives  73.4 us (42%)
  Pallas kernels  32.6 us (19%)
  starting transfers between devices  26.3 us (15%)
  waiting for transfers between devices  20.5 us (12%)
  between operations  14.1 us (8%)
  local copies, waits for them, and re-layouts  6.51 us (4%)
    all_to_all x1, blocking collectives, body(): grads_a = lax.all_to_all(msg, 'z', 0, 0, tiled=True)  34.5 us
    all_to_all x1, blocking collectives, body(): lax.all_to_all(msg, ('z', 'c'), 0, 0, tiled=True)  21.5 us
    ppermute x18, starting transfers between devices, shared(): lax.ppermute(x, axis, [(i, i ^ k) for i in range(4)])  20.7 us
    all_to_all x1, blocking collectives, body(): means_a = lax.all_to_all(means8, 'z', 0, 0, tiled=True)  17.3 us
    ppermute x18, waiting for transfers between devices, shared(): lax.ppermute(x, axis, [(i, i ^ k) for i in range(4)])  17.1 us
    pallas_call x1, Pallas kernels, score_call(): pl.pallas_call(score_kernel, grid_spec=pltpu.PrefetchScalarGridSpec(num_s...  12.7 us
    pallas_call x1, Pallas kernels, head_call(): pl.pallas_call(head_kernel, grid_spec=pltpu.PrefetchScalarGridSpec(num_sc...  9.42 us
    pallas_call x1, Pallas kernels, link_call(): pl.pallas_call(link_kernel, grid=(n // LINK_BLOCK,), in_specs=[pl.BlockSp...  8.38 us
  transfers between devices with their start and end apart: 21, of which 14 were waited for; matrix products, arithmetic and copies ran while one was open for 1% of the time, Pallas kernels for 5%

profile of v1, /device:TPU:1, one launch (start us, length us, event | category | flops | bytes accessed | tf_op | source)
XLA Modules:
  0.0 173.5 jit_solution(389185528263886489)
XLA Ops:
  7.2 0.7 all-gather.2.cloned.1.call-update
  7.9 0.8 copy-done.5
  8.8 0.7 copy-done.9
  9.4 8.4 %shard_map.101 = (bf16[128,8192]{1,0:T(8,128)(2,1)S(1)}, f32[8,8192]{1,0:T(8,128)S(1)}, bf16[128,8192]{1,0:T(8,128)(2,1)S(1)}, bf16[512,128]{1,0:T(8,128)(2,1)S(1)}, bf16[144,128]{1,0:T(8,128)(2,1)S(1)}) custom-call(bf16[8192,128]{1,0:T(8,128)(2,1)} %f1_ref.1, f32[128,128]{1,0:T(8,128)S(1)} %copy-done.5, f32[4,128]{1,0:T(4,128)S(1)} %copy-done.9), custom_call_target="tpu_custom_call" | custom-call | tf_op jit(solution)/shard_map/pallas_call | solution.py:112
  17.8 1.3 copy-done.2
  19.2 3.3 %collective-permute-start.2 = (bf16[144,128]{1,0:T(8,128)(2,1)S(1)}, bf16[144,128]{1,0:T(8,128)(2,1)S(1)}, u32[]{:S(2)}, u32[]{:S(2)}) collective-permute-start(bf16[144,128]{1,0:T(8,128)(2,1)S(1)} %get-tuple-element.26), channel_id=1, source_target_pairs={{0,48},{16,32},{32,16},{48,0},{1,49},{17,33},{33,17},{49,1},{2,50}... | collective-permute-start | bytes 110600 | tf_op jit(solution)/shard_map/ppermute | solution.py:453
  22.5 0.5 collective-permute-start.1
  23.1 0.8 collective-permute-done.2
  23.8 3.0 %collective-permute-done.1 = bf16[144,128]{1,0:T(8,128)(2,1)S(1)} collective-permute-done((bf16[144,128]{1,0:T(8,128)(2,1)S(1)}, bf16[144,128]{1,0:T(8,128)(2,1)S(1)}, u32[]{:S(2)}, u32[]{:S(2)}) %collective-permute-start.1) | collective-permute-done | bytes 36896 | tf_op jit(solution)/shard_map/ppermute | solution.py:453
  26.8 2.8 %collective-permute-start.5 = (bf16[144,128]{1,0:T(8,128)(2,1)S(1)}, bf16[144,128]{1,0:T(8,128)(2,1)S(1)}, u32[]{:S(2)}, u32[]{:S(2)}) collective-permute-start(bf16[144,128]{1,0:T(8,128)(2,1)S(1)} %add_convert_fusion.2.a), channel_id=1, source_target_pairs={{0,192},{64,128},{128,64},{192,0},{1,193},{65,129},{129,65},{193,1... | collective-permute-start | bytes 110600 | tf_op jit(solution)/shard_map/ppermute | solution.py:453
  29.6 0.3 collective-permute-start.4
  30.3 0.7 collective-permute-done.5.d
  31.0 3.0 %collective-permute-done.4.c = bf16[144,128]{1,0:T(8,128)(2,1)S(1)} collective-permute-done((bf16[144,128]{1,0:T(8,128)(2,1)S(1)}, bf16[144,128]{1,0:T(8,128)(2,1)S(1)}, u32[]{:S(2)}, u32[]{:S(2)}) %collective-permute-start.4) | collective-permute-done | bytes 36896 | tf_op jit(solution)/shard_map/ppermute | solution.py:453
  34.1 17.3 %all_to_all.15.ma_ref = bf16[8,128,128]{2,1,0:T(8,128)(2,1)S(1)} all-to-all(bf16[8,128,128]{2,1,0:T(8,128)(2,1)S(1)} %get-tuple-element.27), channel_id=1, replica_groups=mesh['y'=4,'x'=4,'z'=8,'c'=2] {'z'}, dimensions={0} | all-to-all | bytes 524288 | tf_op jit(solution)/shard_map/all_to_all | solution.py:473
  51.4 5.1 %collective-permute-start.6 = (bf16[8,128,128]{2,1,0:T(8,128)(2,1)S(1)}, bf16[8,128,128]{2,1,0:T(8,128)(2,1)S(1)}, u32[]{:S(2)}, u32[]{:S(2)}) collective-permute-start(bf16[8,128,128]{2,1,0:T(8,128)(2,1)S(1)} %all_to_all.15.ma_ref), channel_id=1, source_target_pairs={{0,1},{1,0},{2,3},{3,2},{4,5},{5,4},{6,7},{7,6},{8,9},{9,8},{10,11... | collective-permute-start | bytes 786440 | tf_op jit(solution)/shard_map/ppermute | solution.py:449
  56.4 0.9 pad.4.cls_ref
  57.6 1.2 copy-done.4
  58.8 0.8 copy-done.7
  59.6 0.8 copy-done.8
  60.4 9.4 %shard_map.103 = (bf16[512,128]{1,0:T(8,128)(2,1)}, bf16[8,144,512]{2,1,0:T(8,128)(2,1)S(1)}) custom-call(s32[1]{0:T(128)} %bitcast.s_ref, f32[2048,128]{1,0:T(8,128)S(1)} %copy-done.4, f32[4,128]{1,0:T(4,128)S(1)} %copy-done.10, bf16[128,8192]{1,0:T(8,128)(2,1)S(1)} %get-tuple-element.24.ft_ref.ft0_ref.ft1_ref, ...), custom_call_target="tpu_custom_call" | custom-call | tf_op jit(solution)/shard_map/pallas_call | solution.py:224
  69.8 34.5 %all_to_all.16.ga_ref = bf16[8,144,512]{2,1,0:T(8,128)(2,1)S(1)} all-to-all(bf16[8,144,512]{2,1,0:T(8,128)(2,1)S(1)} %get-tuple-element.29), channel_id=1, replica_groups=mesh['y'=4,'x'=4,'z'=8,'c'=2] {'z'}, dimensions={0} | all-to-all | bytes 2359296 | tf_op jit(solution)/shard_map/all_to_all | solution.py:478
  104.3 0.5 collective-permute-start.7
  104.8 2.5 %collective-permute-done.7.gb_ref = bf16[8,144,512]{2,1,0:T(8,128)(2,1)S(1)} collective-permute-done((bf16[8,144,512]{2,1,0:T(8,128)(2,1)S(1)}, bf16[8,144,512]{2,1,0:T(8,128)(2,1)S(1)}, u32[]{:S(2)}, u32[]{:S(2)}) %collective-permute-start.7) | collective-permute-done | bytes 1179680 | tf_op jit(solution)/shard_map/ppermute | solution.py:449
  107.3 0.7 shard_map.104
  108.0 1.3 collective-permute-start.10
  109.3 0.7 collective-permute-start.9
  110.0 1.3 collective-permute-start.8
  111.3 0.8 collective-permute-done.10
  112.2 1.5 collective-permute-done.9
  113.7 1.3 collective-permute-start.13
  115.0 0.6 collective-permute-start.12
  115.6 1.4 collective-permute-start.11
  117.0 0.8 collective-permute-done.13.p3
  117.8 1.5 collective-permute-done.12.p2
  119.4 12.7 %shard_map.105 = (bf16[144,128]{1,0:T(8,128)(2,1)S(1)}, f32[32,128]{1,0:T(8,128)S(1)}) custom-call(s32[1]{0:T(128)} %bitcast.s_ref, bf16[8192,128]{1,0:T(8,128)(2,1)S(1)} %copy-done, bf16[8192,128]{1,0:T(8,128)(2,1)S(1)} %copy-done, bf16[128,8192]{1,0:T(8,128)(2,1)} %copy-done.1, bf16[128,8192]{1,0:T(8,128)(2,1)} %copy-done.1, ...), custom_call_target="tpu_custom_call" | custom-call | tf_op jit(solution)/shard_map/pallas_call | solution.py:364
  132.0 1.8 %collective-permute-start.16 = (bf16[144,128]{1,0:T(8,128)(2,1)S(1)}, bf16[144,128]{1,0:T(8,128)(2,1)S(1)}, u32[]{:S(2)}, u32[]{:S(2)}) collective-permute-start(bf16[144,128]{1,0:T(8,128)(2,1)S(1)} %get-tuple-element.36), channel_id=1, source_target_pairs={{0,48},{16,32},{32,16},{48,0},{1,49},{17,33},{33,17},{49,1},{2,50}... | collective-permute-start | bytes 110600 | tf_op jit(solution)/shard_map/ppermute | solution.py:453
  133.9 0.7 collective-permute-start.15
  134.6 0.8 collective-permute-start.14
  135.4 0.8 collective-permute-done.16
  136.1 2.0 %collective-permute-done.15 = bf16[144,128]{1,0:T(8,128)(2,1)S(1)} collective-permute-done((bf16[144,128]{1,0:T(8,128)(2,1)S(1)}, bf16[144,128]{1,0:T(8,128)(2,1)S(1)}, u32[]{:S(2)}, u32[]{:S(2)}) %collective-permute-start.15) | collective-permute-done | bytes 36896 | tf_op jit(solution)/shard_map/ppermute | solution.py:453
  138.2 1.3 collective-permute-start.19
  139.5 0.8 collective-permute-start.18
  140.3 1.2 collective-permute-start.17
  141.5 0.8 collective-permute-done.19.refs_3_
  142.3 1.5 collective-permute-done.18.refs_2_
  143.8 0.7 shard_map.106
  144.5 21.5 %all_to_all.17.x_ref = f32[16,40,128]{2,1,0:T(8,128)S(1)} all-to-all(f32[16,40,128]{2,1,0:T(8,128)S(1)} %get-tuple-element.39), channel_id=1, replica_groups=mesh['y'=4,'x'=4,'z'=8,'c'=2] {'z','c'}, dimensions={0} | all-to-all | bytes 655360 | tf_op jit(solution)/shard_map/all_to_all | solution.py:485
  166.0 0.6 shard_map.107
  (32 shorter events, 0.9 us)
Async XLA Ops:
  7.2 50.5 %copy-start.10 = (f32[4,128]{1,0:T(4,128)S(1)}, f32[4,128]{1,0:T(4,128)}, u32[]{:S(2)}) copy-start(f32[4,128]{1,0:T(4,128)} %m_ref.5) | copy-start | bytes 6148
  7.2 50.4 %all-gather.2.cloned.1.call-start = ((), (), s32[]{:S(2)}) async-start(), calls=%async_computation.3 | async-start | bytes 1114112 | tf_op jit(solution)/shard_map/all_gather | solution.py:469
  7.9 0.8 copy-start.5
  8.8 0.7 copy-start.9
  17.8 1.3 copy-start.2
  19.2 50.6 %copy-start.1 = (bf16[128,8192]{1,0:T(8,128)(2,1)}, bf16[128,8192]{1,0:T(8,128)(2,1)S(1)}, u32[]{:S(2)}) copy-start(bf16[128,8192]{1,0:T(8,128)(2,1)S(1)} %get-tuple-element.24.ft_ref.ft0_ref.ft1_ref) | copy-start | bytes 6291460
  19.2 4.7 %collective-permute-start.2 = (bf16[144,128]{1,0:T(8,128)(2,1)S(1)}, bf16[144,128]{1,0:T(8,128)(2,1)S(1)}, u32[]{:S(2)}, u32[]{:S(2)}) collective-permute-start(bf16[144,128]{1,0:T(8,128)(2,1)S(1)} %get-tuple-element.26), channel_id=1, source_target_pairs={{0,48},{16,32},{32,16},{48,0},{1,49},{17,33},{33,17},{49,1},{2,50}... | collective-permute-start | bytes 110600 | tf_op jit(solution)/shard_map/ppermute | solution.py:453
  22.5 4.3 %collective-permute-start.1 = (bf16[144,128]{1,0:T(8,128)(2,1)S(1)}, bf16[144,128]{1,0:T(8,128)(2,1)S(1)}, u32[]{:S(2)}, u32[]{:S(2)}) collective-permute-start(bf16[144,128]{1,0:T(8,128)(2,1)S(1)} %get-tuple-element.26), channel_id=1, source_target_pairs={{0,32},{16,48},{32,0},{48,16},{1,33},{17,49},{33,1},{49,17},{2,34}... | collective-permute-start | bytes 110600 | tf_op jit(solution)/shard_map/ppermute | solution.py:453
  23.0 3.8 %collective-permute-start = (bf16[144,128]{1,0:T(8,128)(2,1)S(1)}, bf16[144,128]{1,0:T(8,128)(2,1)S(1)}, u32[]{:S(2)}, u32[]{:S(2)}) collective-permute-start(bf16[144,128]{1,0:T(8,128)(2,1)S(1)} %get-tuple-element.26), channel_id=1, source_target_pairs={{0,16},{16,0},{32,48},{48,32},{1,17},{17,1},{33,49},{49,33},{2,18}... | collective-permute-start | bytes 110600 | tf_op jit(solution)/shard_map/ppermute | solution.py:453
  26.8 4.1 %collective-permute-start.5 = (bf16[144,128]{1,0:T(8,128)(2,1)S(1)}, bf16[144,128]{1,0:T(8,128)(2,1)S(1)}, u32[]{:S(2)}, u32[]{:S(2)}) collective-permute-start(bf16[144,128]{1,0:T(8,128)(2,1)S(1)} %add_convert_fusion.2.a), channel_id=1, source_target_pairs={{0,192},{64,128},{128,64},{192,0},{1,193},{65,129},{129,65},{193,1... | collective-permute-start | bytes 110600 | tf_op jit(solution)/shard_map/ppermute | solution.py:453
  29.6 4.3 %collective-permute-start.4 = (bf16[144,128]{1,0:T(8,128)(2,1)S(1)}, bf16[144,128]{1,0:T(8,128)(2,1)S(1)}, u32[]{:S(2)}, u32[]{:S(2)}) collective-permute-start(bf16[144,128]{1,0:T(8,128)(2,1)S(1)} %add_convert_fusion.2.a), channel_id=1, source_target_pairs={{0,128},{64,192},{128,0},{192,64},{1,129},{65,193},{129,1},{193,65... | collective-permute-start | bytes 110600 | tf_op jit(solution)/shard_map/ppermute | solution.py:453
  30.0 4.0 %collective-permute-start.3 = (bf16[144,128]{1,0:T(8,128)(2,1)S(1)}, bf16[144,128]{1,0:T(8,128)(2,1)S(1)}, u32[]{:S(2)}, u32[]{:S(2)}) collective-permute-start(bf16[144,128]{1,0:T(8,128)(2,1)S(1)} %add_convert_fusion.2.a), channel_id=1, source_target_pairs={{0,64},{64,0},{128,192},{192,128},{1,65},{65,1},{129,193},{193,129... | collective-permute-start | bytes 110600 | tf_op jit(solution)/shard_map/ppermute | solution.py:453
  51.4 6.2 %collective-permute-start.6 = (bf16[8,128,128]{2,1,0:T(8,128)(2,1)S(1)}, bf16[8,128,128]{2,1,0:T(8,128)(2,1)S(1)}, u32[]{:S(2)}, u32[]{:S(2)}) collective-permute-start(bf16[8,128,128]{2,1,0:T(8,128)(2,1)S(1)} %all_to_all.15.ma_ref), channel_id=1, source_target_pairs={{0,1},{1,0},{2,3},{3,2},{4,5},{5,4},{6,7},{7,6},{8,9},{9,8},{10,11... | collective-permute-start | bytes 786440 | tf_op jit(solution)/shard_map/ppermute | solution.py:449
  57.6 1.2 copy-start.4
  58.8 0.8 copy-start.7
  59.6 0.8 copy-start.8
  69.8 37.5 %copy-start.3 = (bf16[128,8192]{1,0:T(8,128)(2,1)S(1)}, bf16[128,8192]{1,0:T(8,128)(2,1)}, u32[]{:S(2)}) copy-start(bf16[128,8192]{1,0:T(8,128)(2,1)} %copy-done.2) | copy-start | bytes 6291460
  104.3 3.0 %collective-permute-start.7 = (bf16[8,144,512]{2,1,0:T(8,128)(2,1)S(1)}, bf16[8,144,512]{2,1,0:T(8,128)(2,1)S(1)}, u32[]{:S(2)}, u32[]{:S(2)}) collective-permute-start(bf16[8,144,512]{2,1,0:T(8,128)(2,1)S(1)} %all_to_all.16.ga_ref), channel_id=1, source_target_pairs={{0,1},{1,0},{2,3},{3,2},{4,5},{5,4},{6,7},{7,6},{8,9},{9,8},{10,11... | collective-permute-start | bytes 3538952 | tf_op jit(solution)/shard_map/ppermute | solution.py:449
  107.3 12.1 %copy-start = (bf16[8192,128]{1,0:T(8,128)(2,1)S(1)}, bf16[8192,128]{1,0:T(8,128)(2,1)}, u32[]{:S(2)}) copy-start(bf16[8192,128]{1,0:T(8,128)(2,1)} %f1_ref.1) | copy-start | bytes 6291460
  107.3 12.1 %copy-start.6 = (f32[128,128]{1,0:T(8,128)S(1)}, f32[128,128]{1,0:T(8,128)}, u32[]{:S(2)}) copy-start(f32[128,128]{1,0:T(8,128)} %a_ref.3) | copy-start | bytes 196612
  108.0 4.2 %collective-permute-start.10 = (bf16[160,128]{1,0:T(8,128)(2,1)S(1)}, bf16[160,128]{1,0:T(8,128)(2,1)S(1)}, u32[]{:S(2)}, u32[]{:S(2)}) collective-permute-start(bf16[160,128]{1,0:T(8,128)(2,1)S(1)} %get-tuple-element.35), channel_id=1, source_target_pairs={{0,48},{16,32},{32,16},{48,0},{1,49},{17,33},{33,17},{49,1},{2,50}... | collective-permute-start | bytes 122888 | tf_op jit(solution)/shard_map/ppermute | solution.py:453
  109.3 4.4 %collective-permute-start.9 = (bf16[160,128]{1,0:T(8,128)(2,1)S(1)}, bf16[160,128]{1,0:T(8,128)(2,1)S(1)}, u32[]{:S(2)}, u32[]{:S(2)}) collective-permute-start(bf16[160,128]{1,0:T(8,128)(2,1)S(1)} %get-tuple-element.35), channel_id=1, source_target_pairs={{0,32},{16,48},{32,0},{48,16},{1,33},{17,49},{33,1},{49,17},{2,34}... | collective-permute-start | bytes 122888 | tf_op jit(solution)/shard_map/ppermute | solution.py:453
  110.0 3.6 %collective-permute-start.8 = (bf16[160,128]{1,0:T(8,128)(2,1)S(1)}, bf16[160,128]{1,0:T(8,128)(2,1)S(1)}, u32[]{:S(2)}, u32[]{:S(2)}) collective-permute-start(bf16[160,128]{1,0:T(8,128)(2,1)S(1)} %get-tuple-element.35), channel_id=1, source_target_pairs={{0,16},{16,0},{32,48},{48,32},{1,17},{17,1},{33,49},{49,33},{2,18}... | collective-permute-start | bytes 122888 | tf_op jit(solution)/shard_map/ppermute | solution.py:453
  113.7 4.2 %collective-permute-start.13 = (bf16[160,128]{1,0:T(8,128)(2,1)S(1)}, bf16[160,128]{1,0:T(8,128)(2,1)S(1)}, u32[]{:S(2)}, u32[]{:S(2)}) collective-permute-start(bf16[160,128]{1,0:T(8,128)(2,1)S(1)} %add_convert_fusion.p0), channel_id=1, source_target_pairs={{0,192},{64,128},{128,64},{192,0},{1,193},{65,129},{129,65},{193,1... | collective-permute-start | bytes 122888 | tf_op jit(solution)/shard_map/ppermute | solution.py:453
  115.0 4.4 %collective-permute-start.12 = (bf16[160,128]{1,0:T(8,128)(2,1)S(1)}, bf16[160,128]{1,0:T(8,128)(2,1)S(1)}, u32[]{:S(2)}, u32[]{:S(2)}) collective-permute-start(bf16[160,128]{1,0:T(8,128)(2,1)S(1)} %add_convert_fusion.p0), channel_id=1, source_target_pairs={{0,128},{64,192},{128,0},{192,64},{1,129},{65,193},{129,1},{193,65... | collective-permute-start | bytes 122888 | tf_op jit(solution)/shard_map/ppermute | solution.py:453
  115.6 3.7 %collective-permute-start.11 = (bf16[160,128]{1,0:T(8,128)(2,1)S(1)}, bf16[160,128]{1,0:T(8,128)(2,1)S(1)}, u32[]{:S(2)}, u32[]{:S(2)}) collective-permute-start(bf16[160,128]{1,0:T(8,128)(2,1)S(1)} %add_convert_fusion.p0), channel_id=1, source_target_pairs={{0,64},{64,0},{128,192},{192,128},{1,65},{65,1},{129,193},{193,129... | collective-permute-start | bytes 122888 | tf_op jit(solution)/shard_map/ppermute | solution.py:453
  132.0 4.1 %collective-permute-start.16 = (bf16[144,128]{1,0:T(8,128)(2,1)S(1)}, bf16[144,128]{1,0:T(8,128)(2,1)S(1)}, u32[]{:S(2)}, u32[]{:S(2)}) collective-permute-start(bf16[144,128]{1,0:T(8,128)(2,1)S(1)} %get-tuple-element.36), channel_id=1, source_target_pairs={{0,48},{16,32},{32,16},{48,0},{1,49},{17,33},{33,17},{49,1},{2,50}... | collective-permute-start | bytes 110600 | tf_op jit(solution)/shard_map/ppermute | solution.py:453
  133.9 4.3 %collective-permute-start.15 = (bf16[144,128]{1,0:T(8,128)(2,1)S(1)}, bf16[144,128]{1,0:T(8,128)(2,1)S(1)}, u32[]{:S(2)}, u32[]{:S(2)}) collective-permute-start(bf16[144,128]{1,0:T(8,128)(2,1)S(1)} %get-tuple-element.36), channel_id=1, source_target_pairs={{0,32},{16,48},{32,0},{48,16},{1,33},{17,49},{33,1},{49,17},{2,34}... | collective-permute-start | bytes 110600 | tf_op jit(solution)/shard_map/ppermute | solution.py:453
  134.6 3.6 %collective-permute-start.14 = (bf16[144,128]{1,0:T(8,128)(2,1)S(1)}, bf16[144,128]{1,0:T(8,128)(2,1)S(1)}, u32[]{:S(2)}, u32[]{:S(2)}) collective-permute-start(bf16[144,128]{1,0:T(8,128)(2,1)S(1)} %get-tuple-element.36), channel_id=1, source_target_pairs={{0,16},{16,0},{32,48},{48,32},{1,17},{17,1},{33,49},{49,33},{2,18}... | collective-permute-start | bytes 110600 | tf_op jit(solution)/shard_map/ppermute | solution.py:453
  138.2 4.1 %collective-permute-start.19 = (bf16[144,128]{1,0:T(8,128)(2,1)S(1)}, bf16[144,128]{1,0:T(8,128)(2,1)S(1)}, u32[]{:S(2)}, u32[]{:S(2)}) collective-permute-start(bf16[144,128]{1,0:T(8,128)(2,1)S(1)} %add_convert_fusion.1.refs_0_), channel_id=1, source_target_pairs={{0,192},{64,128},{128,64},{192,0},{1,193},{65,129},{129,65},{193,1... | collective-permute-start | bytes 110600 | tf_op jit(solution)/shard_map/ppermute | solution.py:453
  139.5 4.3 %collective-permute-start.18 = (bf16[144,128]{1,0:T(8,128)(2,1)S(1)}, bf16[144,128]{1,0:T(8,128)(2,1)S(1)}, u32[]{:S(2)}, u32[]{:S(2)}) collective-permute-start(bf16[144,128]{1,0:T(8,128)(2,1)S(1)} %add_convert_fusion.1.refs_0_), channel_id=1, source_target_pairs={{0,128},{64,192},{128,0},{192,64},{1,129},{65,193},{129,1},{193,65... | collective-permute-start | bytes 110600 | tf_op jit(solution)/shard_map/ppermute | solution.py:453
  140.3 3.5 %collective-permute-start.17 = (bf16[144,128]{1,0:T(8,128)(2,1)S(1)}, bf16[144,128]{1,0:T(8,128)(2,1)S(1)}, u32[]{:S(2)}, u32[]{:S(2)}) collective-permute-start(bf16[144,128]{1,0:T(8,128)(2,1)S(1)} %add_convert_fusion.1.refs_0_), channel_id=1, source_target_pairs={{0,64},{64,0},{128,192},{192,128},{1,65},{65,1},{129,193},{193,129... | collective-permute-start | bytes 110600 | tf_op jit(solution)/shard_map/ppermute | solution.py:453
Sparse Core Ops, SparseCore 0:
  9.8 44.5 all-gather.1

commit v2 on v1

--- a/solution.py
+++ b/solution.py
@@ -17,7 +17,7 @@
 OWN = 512
 APD = 128
 NZ = 8
-VMEM = 48 * 1024 * 1024
+MIB = 1024 * 1024
 
 NN = ((1,), (0,))
 NT = ((1,), (1,))
@@ -28,8 +28,8 @@
     return lax.dot_general(a, b, (dims, ((), ())), precision=precision, preferred_element_type=f32)
 
 
-def params(**kw):
-    return pltpu.CompilerParams(vmem_limit_bytes=VMEM, **kw)
+def params(mib=20):
+    return pltpu.CompilerParams(vmem_limit_bytes=mib * MIB)
 
 
 def vspec():
@@ -169,7 +169,7 @@
     )(*parts)
 
 
-def head_kernel(s_ref, all_ref, m_ref, ft_ref, rinv_ref, ma_ref, mb_ref, cls_ref, lab_ref, mask_ref, emb_ref, msg_ref):
+def head_kernel(s_ref, all_ref, m_ref, ft_ref, rinv_ref, ma_ref, mb_ref, cls_ref, lab_ref, mask_ref, emb_ref, up_ref, down_ref, part_ref, loss_ref):
     core = lax.rem(s_ref[0], 2)
     metric = m_ref[...]
     ft = ft_ref[...]
@@ -201,20 +201,17 @@
     residual = mask_ref[...].astype(f32) * (logits - target)
     loss_row = jnp.sum(residual * residual, axis=0, keepdims=True)
     loss_row = sum(loss_row[:, k * F : (k + 1) * F] for k in range(OWN // F))
-    class_part = mm(residual, field, NT, highest).astype(bf16)
+    loss_ref[...] = jnp.concatenate([loss_row, jnp.zeros((7, F), f32)], axis=0)
+    class_part = mm(residual, field, NT, highest)
+    z = s_ref[0] // 2
+    for k in range(NZ):
+        part_ref[lax.rem(k - z + NZ, NZ)] = jnp.concatenate([class_part[32 * k + 8 * q : 32 * k + 8 * q + 8, :] for q in range(4)], axis=1)
     field_grad = mm(cls_t.T, residual, NN, highest)
     node_grads = (field_grad * inv_degree).astype(bf16)
     degree_grads = -jnp.sum(field_grad * field, axis=0, keepdims=True) * inv_degree
-    small = jnp.concatenate(
-        [degree_grads[:, k * F : (k + 1) * F] for k in range(OWN // F)] + [loss_row, jnp.zeros((11, F), f32)], axis=0
-    ).astype(bf16)
-    empty = jnp.zeros((16, F), bf16)
-    for z in range(NZ):
-        msg_ref[z, 0:F, :] = node_grads
-        msg_ref[z, F : F + 16, 0:F] = class_part[32 * z : 32 * z + 16, :]
-        msg_ref[z, F : F + 16, F : 2 * F] = class_part[32 * z + 16 : 32 * z + 32, :]
-        msg_ref[z, F : F + 16, 2 * F : 3 * F] = small
-        msg_ref[z, F : F + 16, 3 * F : 4 * F] = empty
+    for ref, k in ((up_ref, 4), (down_ref, 5)):
+        ref[0:F, :] = node_grads
+        ref[F : F + 16, :] = jnp.concatenate([degree_grads, jnp.zeros((7, OWN), f32), part_ref[k]], axis=0).astype(bf16)
 
 
 def head_call(shard, anchors_all, metric, ft, rinv, means_a, means_b, cls_t, labels, mask):
@@ -239,61 +236,58 @@
             ],
             out_specs=[
                 pl.BlockSpec((OWN, F), zero2),
-                pl.BlockSpec((NZ, F + 16, OWN), zero3),
+                pl.BlockSpec((F + 16, OWN), zero2),
+                pl.BlockSpec((F + 16, OWN), zero2),
+                pl.BlockSpec((NZ, 8, OWN), zero3),
+                pl.BlockSpec((8, F), zero2),
             ],
         ),
         out_shape=[
             jax.ShapeDtypeStruct((OWN, F), bf16),
-            jax.ShapeDtypeStruct((NZ, F + 16, OWN), bf16),
+            jax.ShapeDtypeStruct((F + 16, OWN), bf16),
+            jax.ShapeDtypeStruct((F + 16, OWN), bf16),
+            jax.ShapeDtypeStruct((NZ, 8, OWN), f32),
+            jax.ShapeDtypeStruct((8, F), f32),
         ],
         compiler_params=params(),
     )(shard, anchors_all, metric, ft, rinv, means_a, means_b, cls_t, labels, mask)
 
 
-def mean_grad_kernel(s_ref, lb_ref, ga_ref, gb_ref, msg_ref, loss_ref):
+def mean_grad_kernel(s_ref, lb_ref, *refs):
+    blocks, (msg_ref, all_ref) = refs[: 2 * NZ], refs[2 * NZ :]
     core = lax.rem(s_ref[0], 2)
+    z = s_ref[0] // 2
     grads = jnp.zeros((APD, F), f32)
-    for z in range(NZ):
-        for which, ref in ((core, ga_ref), (1 - core, gb_ref)):
-            cols = pl.ds(pl.multiple_of((2 * z + which) * OWN, OWN), OWN)
-            grads = grads + mm(lb_ref[:, cols], ref[z, 0:F, :], NT)
-    msg_ref[0:APD, :] = grads.astype(bf16)
-    extra = []
-    for ref in (ga_ref, gb_ref):
-        s = ref[0, F : F + 16, :].astype(f32)
-        for z in range(1, NZ):
-            s = s + ref[z, F : F + 16, :].astype(f32)
-        extra.append(s)
-    extra = extra[0] + extra[1]
-    msg_ref[APD : APD + 16, :] = extra[:, 0:F].astype(bf16)
-    msg_ref[APD + 16 : APD + 32, :] = extra[:, F : 2 * F].astype(bf16)
-    loss_ref[...] = extra[0:8, 2 * F : 3 * F]
-
-
-def mean_grad_call(shard, lb, grads_a, grads_b):
+    for k, ref in enumerate(blocks):
+        shard = 2 * lax.rem(z + k // 2, NZ) + (core if k % 2 == 0 else 1 - core)
+        cols = pl.ds(pl.multiple_of(shard * OWN, OWN), OWN)
+        all_ref[:, cols] = ref[...]
+        grads = grads + mm(lb_ref[:, cols], ref[0:F, :], NT)
+    msg_ref[...] = grads.astype(bf16)
+
+
+def mean_grad_call(shard, lb, blocks):
     return pl.pallas_call(
         mean_grad_kernel,
-        in_specs=[pl.BlockSpec(memory_space=pltpu.SMEM)] + [vspec()] * 3,
+        in_specs=[pl.BlockSpec(memory_space=pltpu.SMEM)] + [vspec()] * (1 + len(blocks)),
         out_specs=[vspec()] * 2,
         out_shape=[
-            jax.ShapeDtypeStruct((APD + 32, F), bf16),
-            jax.ShapeDtypeStruct((8, F), f32),
-        ],
-        compiler_params=params(),
-    )(shard, lb, grads_a, grads_b)
+            jax.ShapeDtypeStruct((APD, F), bf16),
+            jax.ShapeDtypeStruct((F + 16, lb.shape[1]), bf16),
+        ],
+        compiler_params=params(),
+    )(shard, lb, *blocks)
 
 
 def score_kernel(
-    s_ref, f0_ref, f1_ref, ft0_ref, ft1_ref, r0_ref, r1_ref, ga_ref, gb_ref, am_ref, a_ref, m_ref, means_ref, total_ref, degree_ref, loss_ref,
-    p0, p1, p2, p3, msg_ref, cls_ref, acc, vacc, tg, adg, sgr
+    f_ref, ft_ref, r_ref, g_ref, am_ref, a_ref, m_ref, means_ref, total_ref, degree_ref, loss_ref,
+    p0, p1, p2, p3, msg_ref, acc, vacc, tg, adg, sgr
 ):
     i = pl.program_id(0)
 
     @pl.when(i == 0)
     def _():
-        s = four(p0, p1, p2, p3)
-        cls_ref[...] = s[APD:, :]
-        grads = s[0:APD, :]
+        grads = four(p0, p1, p2, p3)
         inv = 1.0 / degree_ref[...]
         tg[...] = (grads * inv).astype(bf16)
         dots = jnp.sum(grads * total_ref[...], axis=1, keepdims=True)
@@ -302,34 +296,33 @@
         vacc[...] = jnp.zeros_like(vacc)
 
     am = am_ref[...]
-    for f_ref, ft_ref, r_ref, g_ref in ((f0_ref, ft0_ref, r0_ref, ga_ref), (f1_ref, ft1_ref, r1_ref, gb_ref)):
-        rows = []
-        for j in range(OWN // CHUNK):
-            cols = slice(j * CHUNK, (j + 1) * CHUNK)
-            ft = ft_ref[:, cols]
-            rinv = r_ref[:, cols]
-            dg = jnp.concatenate([g_ref[0, F : F + 16, 2 * F : 3 * F].astype(f32)[k : k + 1, :] for k in range(2 * j, 2 * j + 2)], axis=1)
-            parts = head_scores(am, ft, rinv)
-            e = excess_of(parts)
-            link_grads = mm(means_ref[...], g_ref[0, 0:F, cols], NN) + mm(tg[...], ft, NN)
-            link_grads = link_grads + dg + jnp.concatenate([adg[...]] * (CHUNK // F), axis=1)
-            sg = link_grads * (2.0 / HEADS) * e
-            ws = []
-            for h in range(HEADS):
-                r = rinv[h : h + 1, :]
-                sgr[h * APD : (h + 1) * APD, cols] = (sg * r).astype(bf16)
-                ws.append(jnp.sum(sg * parts[h], axis=0, keepdims=True) * (r * r))
-            w = jnp.concatenate(ws, axis=0)
-            hi = w.astype(bf16).astype(f32)
-            rows.append(jnp.concatenate([hi, w - hi], axis=0))
-        v = jnp.concatenate(rows, axis=1).astype(bf16)
-        fb = f_ref[...]
-        acc[...] += mm(sgr[...], fb, NN)
-        sq = fb.astype(f32)
-        sq = sq * sq
-        sq_hi = sq.astype(bf16)
-        sq_lo = (sq - sq_hi.astype(f32)).astype(bf16)
-        vacc[...] += mm(v, sq_hi, NN) + mm(v, sq_lo, NN)
+    rows = []
+    for j in range(SCORE_BLOCK // CHUNK):
+        cols = slice(j * CHUNK, (j + 1) * CHUNK)
+        ft = ft_ref[:, cols]
+        rinv = r_ref[:, cols]
+        dg = g_ref[F : F + 16, cols].astype(f32)[0:1, :]
+        parts = head_scores(am, ft, rinv)
+        e = excess_of(parts)
+        link_grads = mm(means_ref[...], g_ref[0:F, cols], NN) + mm(tg[...], ft, NN)
+        link_grads = link_grads + dg + jnp.concatenate([adg[...]] * (CHUNK // F), axis=1)
+        sg = link_grads * (2.0 / HEADS) * e
+        ws = []
+        for h in range(HEADS):
+            r = rinv[h : h + 1, :]
+            sgr[h * APD : (h + 1) * APD, cols] = (sg * r).astype(bf16)
+            ws.append(jnp.sum(sg * parts[h], axis=0, keepdims=True) * (r * r))
+        w = jnp.concatenate(ws, axis=0)
+        hi = w.astype(bf16).astype(f32)
+        rows.append(jnp.concatenate([hi, w - hi], axis=0))
+    v = jnp.concatenate(rows, axis=1).astype(bf16)
+    fb = f_ref[...]
+    acc[...] += mm(sgr[...], fb, NN)
+    sq = fb.astype(f32)
+    sq = sq * sq
+    sq_hi = sq.astype(bf16)
+    sq_lo = (sq - sq_hi.astype(f32)).astype(bf16)
+    vacc[...] += mm(v, sq_hi, NN) + mm(v, sq_lo, NN)
 
     @pl.when(i == pl.num_programs(0) - 1)
     def _():
@@ -350,97 +343,79 @@
             row = row + jnp.sum(dirs * raw, axis=0, keepdims=True) * (HEADS / m)
             rows.append(row - (m * HEADS) * along)
         msg_ref[0:APD, :] = out.astype(bf16)
-        rows.append(loss_ref[4:5, :])
+        rows.append(loss_ref[0:1, :])
         rows.append(jnp.zeros((11, F), f32))
         msg_ref[APD : APD + 16, :] = jnp.concatenate(rows, axis=0).astype(bf16)
 
 
-def score_call(shard, features, ft, rinv, grads_a, grads_b, am, anchors, metric, means, total, degree, loss, parts):
+SCORE_BLOCK = 1024
+
+
+def score_call(features, ft, rinv, grads, am, anchors, metric, means, total, degree, loss, parts):
     n = features.shape[0]
-    near = lambda i, s: 2 * i + s[0] % 2
-    far = lambda i, s: 2 * i + 1 - s[0] % 2
-    c2 = lambda i, s: (0, 0)
+    c2 = lambda i: (0, 0)
     whole = lambda x: pl.BlockSpec(x.shape, c2)
+    wide = lambda x: pl.BlockSpec((x.shape[0], SCORE_BLOCK), lambda i: (0, i))
     return pl.pallas_call(
         score_kernel,
-        grid_spec=pltpu.PrefetchScalarGridSpec(
-            num_scalar_prefetch=1,
-            grid=(NZ,),
-            in_specs=[
-                pl.BlockSpec((OWN, F), lambda i, s: (near(i, s), 0)),
-                pl.BlockSpec((OWN, F), lambda i, s: (far(i, s), 0)),
-                pl.BlockSpec((F, OWN), lambda i, s: (0, near(i, s))),
-                pl.BlockSpec((F, OWN), lambda i, s: (0, far(i, s))),
-                pl.BlockSpec((8, OWN), lambda i, s: (0, near(i, s))),
-                pl.BlockSpec((8, OWN), lambda i, s: (0, far(i, s))),
-                pl.BlockSpec((1, F + 16, OWN), lambda i, s: (i, 0, 0)),
-                pl.BlockSpec((1, F + 16, OWN), lambda i, s: (i, 0, 0)),
-                whole(am),
-                whole(anchors),
-                whole(metric),
-                whole(means),
-                whole(total),
-                whole(degree),
-                whole(loss),
-            ]
-            + [whole(p) for p in parts],
-            out_specs=[pl.BlockSpec((APD + 16, F), c2), pl.BlockSpec((32, F), c2)],
-            scratch_shapes=[
-                pltpu.VMEM((HEADS * APD, F), f32),
-                pltpu.VMEM((8, F), f32),
-                pltpu.VMEM((APD, F), bf16),
-                pltpu.VMEM((APD, F), f32),
-                pltpu.VMEM((HEADS * APD, OWN), bf16),
-            ],
-        ),
-        out_shape=[
-            jax.ShapeDtypeStruct((APD + 16, F), bf16),
-            jax.ShapeDtypeStruct((32, F), f32),
-        ],
-        compiler_params=params(),
-    )(shard, features, features, ft, ft, rinv, rinv, grads_a, grads_b, am, anchors, metric, means, total, degree, loss, *parts)
-
-
-def last_kernel(scale, p0, p1, p2, p3, cls_ref, out_ref, loss_ref, msg_ref):
+        grid=(n // SCORE_BLOCK,),
+        in_specs=[pl.BlockSpec((SCORE_BLOCK, F), lambda i: (i, 0)), wide(ft), wide(rinv), wide(grads)]
+        + [whole(x) for x in (am, anchors, metric, means, total, degree, loss, *parts)],
+        out_specs=pl.BlockSpec((APD + 16, F), c2),
+        out_shape=jax.ShapeDtypeStruct((APD + 16, F), bf16),
+        scratch_shapes=[
+            pltpu.VMEM((HEADS * APD, F), f32),
+            pltpu.VMEM((8, F), f32),
+            pltpu.VMEM((APD, F), bf16),
+            pltpu.VMEM((APD, F), f32),
+            pltpu.VMEM((HEADS * APD, SCORE_BLOCK), bf16),
+        ],
+        compiler_params=params(),
+    )(features, ft, rinv, grads, am, anchors, metric, means, total, degree, loss, *parts)
+
+
+def last_kernel(p0, p1, p2, p3, out_ref, small_ref):
     s = four(p0, p1, p2, p3)
     out_ref[...] = s[0:APD, :]
-    loss_ref[...] = jnp.sum(s[APD + 4 : APD + 5, :], axis=1, keepdims=True) * scale
-    for k in range(2 * NZ):
-        msg_ref[k, 0:8, :] = s[APD : APD + 8, :]
-        msg_ref[k, 8:40, :] = cls_ref[...]
-
-
-def last_call(parts, cls, scale):
-    return pl.pallas_call(
-        lambda *refs: last_kernel(scale, *refs),
-        in_specs=[vspec()] * 5,
-        out_specs=[vspec()] * 3,
+    small_ref[0:8, :] = s[APD : APD + 8, :]
+    small_ref[8:40, :] = s[APD + 16 : APD + 48, :]
+
+
+def last_call(parts):
+    return pl.pallas_call(
+        last_kernel,
+        in_specs=[vspec()] * 4,
+        out_specs=[vspec()] * 2,
         out_shape=[
             jax.ShapeDtypeStruct((APD, F), f32),
-            jax.ShapeDtypeStruct((1, 1), f32),
-            jax.ShapeDtypeStruct((2 * NZ, 40, F), f32),
-        ],
-        compiler_params=params(),
-    )(*parts, cls)
-
-
-def finish_kernel(x_ref, metric_ref, cls_ref):
+            jax.ShapeDtypeStruct((40, F), f32),
+        ],
+        compiler_params=params(),
+    )(*parts)
+
+
+def finish_kernel(scale, x_ref, metric_ref, loss_ref, cls_ref):
     s = x_ref[0, 0:8, :]
-    for k in range(1, 2 * NZ):
+    for k in range(1, NZ):
         s = s + x_ref[k, 0:8, :]
     metric_ref[...] = s[0:HEADS, :]
+    loss_ref[...] = jnp.sum(s[HEADS : HEADS + 1, :], axis=1, keepdims=True) * scale
     for z in range(NZ):
         rows = min(32, CLASSES - 32 * z)
         if rows > 0:
-            cls_ref[32 * z : 32 * z + rows, :] = x_ref[2 * z, 8 : 8 + rows, :]
-
-
-def finish_call(x):
-    return pl.pallas_call(
-        finish_kernel,
+            cls_ref[32 * z : 32 * z + rows, :] = x_ref[z, 8 : 8 + rows, :]
+
+
+def finish_call(x, scale):
+    return pl.pallas_call(
+        lambda *refs: finish_kernel(scale, *refs),
         in_specs=[vspec()],
-        out_specs=[vspec()] * 2,
-        out_shape=[jax.ShapeDtypeStruct((HEADS, F), f32), jax.ShapeDtypeStruct((CLASSES, F), f32)],
+        out_specs=[vspec()] * 3,
+        out_shape=[
+            jax.ShapeDtypeStruct((HEADS, F), f32),
+            jax.ShapeDtypeStruct((1, 1), f32),
+            jax.ShapeDtypeStruct((CLASSES, F), f32),
+        ],
         compiler_params=params(),
     )(x)
 
@@ -461,6 +436,27 @@
 
 def over_dp(x):
     return shared(sum4(shared(x, "x")), "y")
+
+
+def ring(up, down, part):
+    ups, downs = [(i, (i + 1) % NZ) for i in range(NZ)], [(i, (i - 1) % NZ) for i in range(NZ)]
+
+    def add(x, k):
+        total = x[F + 8 :].astype(f32) + part[k]
+        return jnp.concatenate([x[: F + 8], total.astype(bf16)], axis=0)
+
+    blocks = [up] + [None] * (NZ - 1)
+    for k in range(1, 5):
+        up = lax.ppermute(up, "z", ups)
+        blocks[NZ - k] = up
+        if k < 4:
+            down = lax.ppermute(down, "z", downs)
+            blocks[k] = down
+            up = add(up, 4 - k)
+        if k < 3:
+            down = add(down, 5 + k)
+    total = (up[F + 8 :].astype(f32) + down[F + 8 :].astype(f32)) + part[0]
+    return blocks, jnp.concatenate([total[:, q * F : (q + 1) * F] for q in range(4)], axis=0)
 
 
 def body(features, anchors, metric, classifier, labels, train_mask):
@@ -472,17 +468,18 @@
     total, degree, means8 = mean_call(over_dp(msg))
     means_a = lax.all_to_all(means8, "z", 0, 0, tiled=True)
     means_b = swap(means_a)
-    embedding, msg = head_call(
+    embedding, up, down, part, loss = head_call(
         shard, anchors_all, metric, ft, rinv, means_a, means_b, cls_t, labels.reshape(1, n), train_mask.reshape(1, n)
     )
-    grads_a = lax.all_to_all(msg, "z", 0, 0, tiled=True)
-    grads_b = swap(grads_a)
-    msg, loss = mean_grad_call(shard, lb, grads_a, grads_b)
-    msg, cls = score_call(
-        shard, features, ft, rinv, grads_a, grads_b, am, anchors, metric, means8[0], total, degree, loss, over_dp(msg)
-    )
-    grad_anchors, loss, msg = last_call(over_dp(msg), cls, 1.0 / (4.0 * n * 16))
-    grad_metric, grad_cls = finish_call(lax.all_to_all(msg, ("z", "c"), 0, 0, tiled=True))
+    blocks, cls = ring(up, down, part)
+    blocks = [b for block in blocks for b in (block, swap(block))]
+    msg, grads = mean_grad_call(shard, lb, blocks)
+    msg = score_call(features, ft, rinv, grads, am, anchors, metric, means8[0], total, degree, loss, over_dp(msg))
+    msg = jnp.concatenate([msg, cls.astype(bf16)], axis=0)
+    grad_anchors, small = last_call(over_dp(msg))
+    small = small + swap(small)
+    small = lax.all_to_all(jnp.broadcast_to(small[None], (NZ,) + small.shape), "z", 0, 0, tiled=True)
+    grad_metric, loss, grad_cls = finish_call(small, 1.0 / (4.0 * n * 16))
     return (embedding, loss.reshape(()), grad_cls.T, grad_anchors, grad_metric)
 
 

time: 174 us -> 159 us (0.914)
  blocking collectives: 73.4 us -> 28.8 us
  starting transfers between devices: 26.3 us -> 49.7 us
  waiting for transfers between devices: 20.5 us -> 29 us
  Pallas kernels: 32.6 us -> 28.7 us
    all_to_all x2 -> x1, blocking collectives: 56.1 us -> 11.6 us  [body(): lax.all_to_all(jnp.broadcast_to(small[None], (NZ,) + small.shape), 'z', 0...]
    ppermute x2 -> x10, starting transfers between devices: 5.53 us -> 23 us  [swap(): return lax.ppermute(x, 'c', [(0, 1), (1, 0)])]
    ppermute x0 -> x7, waiting for transfers between devices: none -> 9.08 us  [the longest x4 9.08 us: ring(): up = lax.ppermute(up, 'z', ups)]
    ppermute x0 -> x7, starting transfers between devices: none -> 5.99 us  [the longest x3 3.47 us: ring(): down = lax.ppermute(down, 'z', downs)]
    pallas_call x3, Pallas kernels: 14 us -> 11.3 us  [the longest x1 9.9 us: score_call(): pl.pallas_call(score_kernel, grid=(n // SCORE_BLOCK,), in_specs=[pl.Block...]
    unnamed x22 -> x26, local copies, waits for them, and re-layouts: 5.61 us -> 7.24 us
  transfers between devices with their start and end apart: 21 -> 36, of which waited for: 14 -> 18; matrix products, arithmetic and copies ran while one was open for 1% -> 1% of each run, Pallas kernels for 5% -> 5%
where the time goes in v2:
time: 159 us
  starting transfers between devices  49.7 us (31%)
  waiting for transfers between devices  29 us (18%)
  blocking collectives  28.8 us (18%)
  Pallas kernels  28.7 us (18%)
  between operations  14.3 us (9%)
  local copies, waits for them, and re-layouts  8.21 us (5%)
    ppermute x10, starting transfers between devices, swap(): return lax.ppermute(x, 'c', [(0, 1), (1, 0)])  23 us
    ppermute x18, starting transfers between devices, shared(): lax.ppermute(x, axis, [(i, i ^ k) for i in range(4)])  20.7 us
    all_to_all x1, blocking collectives, body(): means_a = lax.all_to_all(means8, 'z', 0, 0, tiled=True)  17.3 us
    ppermute x18, waiting for transfers between devices, shared(): lax.ppermute(x, axis, [(i, i ^ k) for i in range(4)])  17.1 us
    all_to_all x1, blocking collectives, body(): lax.all_to_all(jnp.broadcast_to(small[None], (NZ,) + small.shape), 'z', 0...  11.6 us
    pallas_call x1, Pallas kernels, score_call(): pl.pallas_call(score_kernel, grid=(n // SCORE_BLOCK,), in_specs=[pl.Block...  9.9 us
    pallas_call x1, Pallas kernels, head_call(): pl.pallas_call(head_kernel, grid_spec=pltpu.PrefetchScalarGridSpec(num_sc...  9.46 us
    ppermute x4, waiting for transfers between devices, ring(): up = lax.ppermute(up, 'z', ups)  9.08 us
  transfers between devices with their start and end apart: 36, of which 18 were waited for; matrix products, arithmetic and copies ran while one was open for 1% of the time, Pallas kernels for 5%

profile of v2, /device:TPU:1, one launch (start us, length us, event | category | flops | bytes accessed | tf_op | source)
XLA Modules:
  0.0 158.9 jit_solution(5172573697151262909)
XLA Ops:
  7.9 1.6 copy-done
  9.5 0.8 copy-done.5
  11.0 7.1 %shard_map.101 = (bf16[128,8192]{1,0:T(8,128)(2,1)S(1)}, f32[8,8192]{1,0:T(8,128)S(1)}, bf16[128,8192]{1,0:T(8,128)(2,1)S(1)}, bf16[512,128]{1,0:T(8,128)(2,1)S(1)}, bf16[144,128]{1,0:T(8,128)(2,1)S(1)}) custom-call(bf16[8192,128]{1,0:T(8,128)(2,1)S(1)} %copy-done, f32[128,128]{1,0:T(8,128)S(1)} %copy-done.5, f32[4,128]{1,0:T(4,128)S(1)} %copy-done.9), custom_call_target="tpu_custom_call" | custom-call | tf_op jit(solution)/shard_map/pallas_call | solution.py:112
  18.1 1.3 copy-done.2
  19.5 3.3 %collective-permute-start.2 = (bf16[144,128]{1,0:T(8,128)(2,1)S(1)}, bf16[144,128]{1,0:T(8,128)(2,1)S(1)}, u32[]{:S(2)}, u32[]{:S(2)}) collective-permute-start(bf16[144,128]{1,0:T(8,128)(2,1)S(1)} %get-tuple-element.27), channel_id=1, source_target_pairs={{0,48},{16,32},{32,16},{48,0},{1,49},{17,33},{33,17},{49,1},{2,50}... | collective-permute-start | bytes 110600 | tf_op jit(solution)/shard_map/ppermute | solution.py:428
  23.3 0.8 collective-permute-done.2
  24.1 3.0 %collective-permute-done.1 = bf16[144,128]{1,0:T(8,128)(2,1)S(1)} collective-permute-done((bf16[144,128]{1,0:T(8,128)(2,1)S(1)}, bf16[144,128]{1,0:T(8,128)(2,1)S(1)}, u32[]{:S(2)}, u32[]{:S(2)}) %collective-permute-start.1) | collective-permute-done | bytes 36896 | tf_op jit(solution)/shard_map/ppermute | solution.py:428
  27.1 2.8 %collective-permute-start.5 = (bf16[144,128]{1,0:T(8,128)(2,1)S(1)}, bf16[144,128]{1,0:T(8,128)(2,1)S(1)}, u32[]{:S(2)}, u32[]{:S(2)}) collective-permute-start(bf16[144,128]{1,0:T(8,128)(2,1)S(1)} %add_convert_fusion.1.a), channel_id=1, source_target_pairs={{0,192},{64,128},{128,64},{192,0},{1,193},{65,129},{129,65},{193,1... | collective-permute-start | bytes 110600 | tf_op jit(solution)/shard_map/ppermute | solution.py:428
  31.3 3.0 %collective-permute-done.4.c = bf16[144,128]{1,0:T(8,128)(2,1)S(1)} collective-permute-done((bf16[144,128]{1,0:T(8,128)(2,1)S(1)}, bf16[144,128]{1,0:T(8,128)(2,1)S(1)}, u32[]{:S(2)}, u32[]{:S(2)}) %collective-permute-start.4) | collective-permute-done | bytes 36896 | tf_op jit(solution)/shard_map/ppermute | solution.py:428
  34.4 17.3 %all_to_all.10.ma_ref = bf16[8,128,128]{2,1,0:T(8,128)(2,1)S(1)} all-to-all(bf16[8,128,128]{2,1,0:T(8,128)(2,1)S(1)} %get-tuple-element.28), channel_id=1, replica_groups=mesh['y'=4,'x'=4,'z'=8,'c'=2] {'z'}, dimensions={0} | all-to-all | bytes 524288 | tf_op jit(solution)/shard_map/all_to_all | solution.py:469
  51.6 5.1 %collective-permute-start.6 = (bf16[8,128,128]{2,1,0:T(8,128)(2,1)S(1)}, bf16[8,128,128]{2,1,0:T(8,128)(2,1)S(1)}, u32[]{:S(2)}, u32[]{:S(2)}) collective-permute-start(bf16[8,128,128]{2,1,0:T(8,128)(2,1)S(1)} %all_to_all.10.ma_ref), channel_id=1, source_target_pairs={{0,1},{1,0},{2,3},{3,2},{4,5},{5,4},{6,7},{7,6},{8,9},{9,8},{10,11... | collective-permute-start | bytes 786440 | tf_op jit(solution)/shard_map/ppermute | solution.py:424
  56.7 0.9 pad.4.cls_ref
  57.9 1.2 copy-done.4
  59.1 0.8 copy-done.7
  59.9 0.8 copy-done.8
  60.7 9.5 %shard_map.103 = (bf16[512,128]{1,0:T(8,128)(2,1)}, bf16[144,512]{1,0:T(8,128)(2,1)S(1)}, bf16[144,512]{1,0:T(8,128)(2,1)S(1)}, f32[8,8,512]{2,1,0:T(8,128)S(1)}, f32[8,128]{1,0:T(8,128)S(1)}) custom-call(s32[1]{0:T(128)} %bitcast.s_ref, f32[2048,128]{1,0:T(8,128)S(1)} %copy-done.4, f32[4,128]{1,0:T(4,128)S(1)} %copy-done.10, ...), custom_call_target="tpu_custom_call" | custom-call | tf_op jit(solution)/shard_map/pallas_call | solution.py:221
  70.1 2.7 %collective-permute-start.8 = (bf16[144,512]{1,0:T(8,128)(2,1)S(1)}, bf16[144,512]{1,0:T(8,128)(2,1)S(1)}, u32[]{:S(2)}, u32[]{:S(2)}) collective-permute-start(bf16[144,512]{1,0:T(8,128)(2,1)S(1)} %get-tuple-element.32), channel_id=1, source_target_pairs={{0,14},{2,0},{4,2},{6,4},{8,6},{10,8},{12,10},{14,12},{1,15},{3,1}... | collective-permute-start | bytes 442376 | tf_op jit(solution)/shard_map/ppermute | solution.py:453
  72.8 3.6 %collective-permute-done.14.refs_14_ = bf16[144,512]{1,0:T(8,128)(2,1)S(1)} collective-permute-done((bf16[144,512]{1,0:T(8,128)(2,1)S(1)}, bf16[144,512]{1,0:T(8,128)(2,1)S(1)}, u32[]{:S(2)}, u32[]{:S(2)}) %collective-permute-start.14) | collective-permute-done | bytes 147488 | tf_op jit(solution)/shard_map/ppermute | solution.py:450
  76.6 5.2 %collective-permute-done.15.refs_12_ = bf16[144,512]{1,0:T(8,128)(2,1)S(1)} collective-permute-done((bf16[144,512]{1,0:T(8,128)(2,1)S(1)}, bf16[144,512]{1,0:T(8,128)(2,1)S(1)}, u32[]{:S(2)}, u32[]{:S(2)}) %collective-permute-start.15) | collective-permute-done | bytes 147488 | tf_op jit(solution)/shard_map/ppermute | solution.py:450
  81.9 1.5 collective-permute-start.16
  83.4 2.9 %collective-permute-start.7 = (bf16[144,512]{1,0:T(8,128)(2,1)S(1)}, bf16[144,512]{1,0:T(8,128)(2,1)S(1)}, u32[]{:S(2)}, u32[]{:S(2)}) collective-permute-start(bf16[144,512]{1,0:T(8,128)(2,1)S(1)} %get-tuple-element.31.refs_0_), channel_id=1, source_target_pairs={{0,1},{1,0},{2,3},{3,2},{4,5},{5,4},{6,7},{7,6},{8,9},{9,8},{10,11... | collective-permute-start | bytes 442376 | tf_op jit(solution)/shard_map/ppermute | solution.py:424
  87.9 0.9 collective-permute-start.17
  88.8 4.1 %collective-permute-start.20 = (bf16[144,512]{1,0:T(8,128)(2,1)S(1)}, bf16[144,512]{1,0:T(8,128)(2,1)S(1)}, u32[]{:S(2)}, u32[]{:S(2)}) collective-permute-start(bf16[144,512]{1,0:T(8,128)(2,1)S(1)} %collective-permute-done.15.refs_12_), channel_id=1, source_target_pairs={{0,1},{1,0},{2,3},{3,2},{4,5},{5,4},{6,7},{7,6},{8,9},{9,8},{10,11... | collective-permute-start | bytes 442376 | tf_op jit(solution)/shard_map/ppermute | solution.py:424
  93.4 2.5 %collective-permute-start.13 = (bf16[144,512]{1,0:T(8,128)(2,1)S(1)}, bf16[144,512]{1,0:T(8,128)(2,1)S(1)}, u32[]{:S(2)}, u32[]{:S(2)}) collective-permute-start(bf16[144,512]{1,0:T(8,128)(2,1)S(1)} %collective-permute-done.12.refs_6_), channel_id=1, source_target_pairs={{0,1},{1,0},{2,3},{3,2},{4,5},{5,4},{6,7},{7,6},{8,9},{9,8},{10,11... | collective-permute-start | bytes 442376 | tf_op jit(solution)/shard_map/ppermute | solution.py:424
  95.9 1.3 collective-permute-start.18
  97.3 1.0 collective-permute-done.18.refs_9_
  98.2 0.8 shard_map.104
  99.0 1.3 collective-permute-start.24
  101.0 1.4 collective-permute-start.22
  103.1 1.5 collective-permute-done.23
  104.6 1.1 collective-permute-start.27
  105.7 0.8 collective-permute-start.26
  106.5 1.4 collective-permute-start.25
  108.7 1.3 collective-permute-done.26.p2
  110.0 9.9 %shard_map.105 = bf16[144,128]{1,0:T(8,128)(2,1)S(1)} custom-call(bf16[8192,128]{1,0:T(8,128)(2,1)S(1)} %copy-done.1, bf16[128,8192]{1,0:T(8,128)(2,1)S(1)} %get-tuple-element.25.ft_ref, f32[8,8192]{1,0:T(8,128)S(1)} %get-tuple-element.26.rinv_ref.r_ref, bf16[144,8192]{1,0:T(8,128)(2,1)S(1)} %get-tuple-element.34.g_ref, ...), custom_call_target="tpu_custom_call" | custom-call | tf_op jit(solution)/shard_map/pallas_call | solution.py:359
  120.0 1.7 %collective-permute-start.30 = (bf16[176,128]{1,0:T(8,128)(2,1)S(1)}, bf16[176,128]{1,0:T(8,128)(2,1)S(1)}, u32[]{:S(2)}, u32[]{:S(2)}) collective-permute-start(bf16[176,128]{1,0:T(8,128)(2,1)S(1)} %constant_dynamic-update-slice_fusion), channel_id=1, source_target_pairs={{0,48},{16,32},{32,16},{48,0},{1,49},{17,33},{33,17},{49,1},{2,50}... | collective-permute-start | bytes 135176 | tf_op jit(solution)/shard_map/ppermute | solution.py:428
  121.6 0.9 collective-permute-start.29
  122.5 0.8 collective-permute-start.28
  123.3 0.9 collective-permute-done.30
  124.2 1.9 %collective-permute-done.29 = bf16[176,128]{1,0:T(8,128)(2,1)S(1)} collective-permute-done((bf16[176,128]{1,0:T(8,128)(2,1)S(1)}, bf16[176,128]{1,0:T(8,128)(2,1)S(1)}, u32[]{:S(2)}, u32[]{:S(2)}) %collective-permute-start.29) | collective-permute-done | bytes 45088 | tf_op jit(solution)/shard_map/ppermute | solution.py:428
  126.1 1.7 %collective-permute-start.33 = (bf16[176,128]{1,0:T(8,128)(2,1)S(1)}, bf16[176,128]{1,0:T(8,128)(2,1)S(1)}, u32[]{:S(2)}, u32[]{:S(2)}) collective-permute-start(bf16[176,128]{1,0:T(8,128)(2,1)S(1)} %add_convert_fusion.p0), channel_id=1, source_target_pairs={{0,192},{64,128},{128,64},{192,0},{1,193},{65,129},{129,65},{193,1... | collective-permute-start | bytes 135176 | tf_op jit(solution)/shard_map/ppermute | solution.py:428
  127.7 0.8 collective-permute-start.32
  128.6 0.9 collective-permute-start.31
  129.4 0.9 collective-permute-done.33.p3
  130.3 1.8 %collective-permute-done.32.p2 = bf16[176,128]{1,0:T(8,128)(2,1)S(1)} collective-permute-done((bf16[176,128]{1,0:T(8,128)(2,1)S(1)}, bf16[176,128]{1,0:T(8,128)(2,1)S(1)}, u32[]{:S(2)}, u32[]{:S(2)}) %collective-permute-start.32) | collective-permute-done | bytes 45088 | tf_op jit(solution)/shard_map/ppermute | solution.py:428
  132.8 6.1 %collective-permute-start.34 = (f32[40,128]{1,0:T(8,128)S(1)}, f32[40,128]{1,0:T(8,128)S(1)}, u32[]{:S(2)}, u32[]{:S(2)}) collective-permute-start(f32[40,128]{1,0:T(8,128)S(1)} %get-tuple-element.40), channel_id=1, source_target_pairs={{0,1},{1,0},{2,3},{3,2},{4,5},{5,4},{6,7},{7,6},{8,9},{9,8},{10,11... | collective-permute-start | bytes 61448 | tf_op jit(solution)/shard_map/ppermute | solution.py:424
  138.9 0.8 collective-permute-done.34
  139.7 11.6 %all_to_all.11.refs_0_ = f32[8,40,128]{2,1,0:T(8,128)S(1)} all-to-all(f32[8,40,128]{2,1,0:T(8,128)S(1)} %broadcast_in_dim.2), channel_id=1, replica_groups=mesh['y'=4,'x'=4,'z'=8,'c'=2] {'z'}, dimensions={0} | all-to-all | bytes 327680 | tf_op jit(solution)/shard_map/all_to_all | solution.py:481
  (82 shorter events, 9.8 us)
Async XLA Ops:
  7.2 50.7 %copy-start.10 = (f32[4,128]{1,0:T(4,128)S(1)}, f32[4,128]{1,0:T(4,128)}, u32[]{:S(2)}) copy-start(f32[4,128]{1,0:T(4,128)} %m_ref.5) | copy-start | bytes 6148
  7.2 50.7 %all-gather.2.cloned.1.call-start = ((), (), s32[]{:S(2)}) async-start(), calls=%async_computation.2 | async-start | bytes 1114112 | tf_op jit(solution)/shard_map/all_gather | solution.py:465
  7.9 1.6 %copy-start = (bf16[8192,128]{1,0:T(8,128)(2,1)S(1)}, bf16[8192,128]{1,0:T(8,128)(2,1)}, u32[]{:S(2)}) copy-start(bf16[8192,128]{1,0:T(8,128)(2,1)} %f_ref.3) | copy-start | bytes 6291460
  9.5 0.8 copy-start.5
  10.3 0.7 copy-start.9
  18.1 1.4 copy-start.2
  19.5 4.7 %collective-permute-start.2 = (bf16[144,128]{1,0:T(8,128)(2,1)S(1)}, bf16[144,128]{1,0:T(8,128)(2,1)S(1)}, u32[]{:S(2)}, u32[]{:S(2)}) collective-permute-start(bf16[144,128]{1,0:T(8,128)(2,1)S(1)} %get-tuple-element.27), channel_id=1, source_target_pairs={{0,48},{16,32},{32,16},{48,0},{1,49},{17,33},{33,17},{49,1},{2,50}... | collective-permute-start | bytes 110600 | tf_op jit(solution)/shard_map/ppermute | solution.py:428
  22.8 4.3 %collective-permute-start.1 = (bf16[144,128]{1,0:T(8,128)(2,1)S(1)}, bf16[144,128]{1,0:T(8,128)(2,1)S(1)}, u32[]{:S(2)}, u32[]{:S(2)}) collective-permute-start(bf16[144,128]{1,0:T(8,128)(2,1)S(1)} %get-tuple-element.27), channel_id=1, source_target_pairs={{0,32},{16,48},{32,0},{48,16},{1,33},{17,49},{33,1},{49,17},{2,34}... | collective-permute-start | bytes 110600 | tf_op jit(solution)/shard_map/ppermute | solution.py:428
  23.3 3.8 %collective-permute-start = (bf16[144,128]{1,0:T(8,128)(2,1)S(1)}, bf16[144,128]{1,0:T(8,128)(2,1)S(1)}, u32[]{:S(2)}, u32[]{:S(2)}) collective-permute-start(bf16[144,128]{1,0:T(8,128)(2,1)S(1)} %get-tuple-element.27), channel_id=1, source_target_pairs={{0,16},{16,0},{32,48},{48,32},{1,17},{17,1},{33,49},{49,33},{2,18}... | collective-permute-start | bytes 110600 | tf_op jit(solution)/shard_map/ppermute | solution.py:428
  27.1 4.1 %collective-permute-start.5 = (bf16[144,128]{1,0:T(8,128)(2,1)S(1)}, bf16[144,128]{1,0:T(8,128)(2,1)S(1)}, u32[]{:S(2)}, u32[]{:S(2)}) collective-permute-start(bf16[144,128]{1,0:T(8,128)(2,1)S(1)} %add_convert_fusion.1.a), channel_id=1, source_target_pairs={{0,192},{64,128},{128,64},{192,0},{1,193},{65,129},{129,65},{193,1... | collective-permute-start | bytes 110600 | tf_op jit(solution)/shard_map/ppermute | solution.py:428
  29.9 4.3 %collective-permute-start.4 = (bf16[144,128]{1,0:T(8,128)(2,1)S(1)}, bf16[144,128]{1,0:T(8,128)(2,1)S(1)}, u32[]{:S(2)}, u32[]{:S(2)}) collective-permute-start(bf16[144,128]{1,0:T(8,128)(2,1)S(1)} %add_convert_fusion.1.a), channel_id=1, source_target_pairs={{0,128},{64,192},{128,0},{192,64},{1,129},{65,193},{129,1},{193,65... | collective-permute-start | bytes 110600 | tf_op jit(solution)/shard_map/ppermute | solution.py:428
  30.3 4.0 %collective-permute-start.3 = (bf16[144,128]{1,0:T(8,128)(2,1)S(1)}, bf16[144,128]{1,0:T(8,128)(2,1)S(1)}, u32[]{:S(2)}, u32[]{:S(2)}) collective-permute-start(bf16[144,128]{1,0:T(8,128)(2,1)S(1)} %add_convert_fusion.1.a), channel_id=1, source_target_pairs={{0,64},{64,0},{128,192},{192,128},{1,65},{65,1},{129,193},{193,129... | collective-permute-start | bytes 110600 | tf_op jit(solution)/shard_map/ppermute | solution.py:428
  51.6 6.3 %collective-permute-start.6 = (bf16[8,128,128]{2,1,0:T(8,128)(2,1)S(1)}, bf16[8,128,128]{2,1,0:T(8,128)(2,1)S(1)}, u32[]{:S(2)}, u32[]{:S(2)}) collective-permute-start(bf16[8,128,128]{2,1,0:T(8,128)(2,1)S(1)} %all_to_all.10.ma_ref), channel_id=1, source_target_pairs={{0,1},{1,0},{2,3},{3,2},{4,5},{5,4},{6,7},{7,6},{8,9},{9,8},{10,11... | collective-permute-start | bytes 786440 | tf_op jit(solution)/shard_map/ppermute | solution.py:424
  57.9 1.2 copy-start.4
  59.1 0.8 copy-start.7
  59.9 0.8 copy-start.8
  70.1 28.1 %copy-start.3 = (bf16[128,8192]{1,0:T(8,128)(2,1)S(1)}, bf16[128,8192]{1,0:T(8,128)(2,1)}, u32[]{:S(2)}) copy-start(bf16[128,8192]{1,0:T(8,128)(2,1)} %copy-done.2) | copy-start | bytes 6291460
  70.1 6.3 %collective-permute-start.14 = (bf16[144,512]{1,0:T(8,128)(2,1)S(1)}, bf16[144,512]{1,0:T(8,128)(2,1)S(1)}, u32[]{:S(2)}, u32[]{:S(2)}) collective-permute-start(bf16[144,512]{1,0:T(8,128)(2,1)S(1)} %get-tuple-element.31.refs_0_), channel_id=1, source_target_pairs={{0,2},{2,4},{4,6},{6,8},{8,10},{10,12},{12,14},{14,0},{1,3},{3,5},... | collective-permute-start | bytes 442376 | tf_op jit(solution)/shard_map/ppermute | solution.py:450
  70.1 6.4 %collective-permute-start.8 = (bf16[144,512]{1,0:T(8,128)(2,1)S(1)}, bf16[144,512]{1,0:T(8,128)(2,1)S(1)}, u32[]{:S(2)}, u32[]{:S(2)}) collective-permute-start(bf16[144,512]{1,0:T(8,128)(2,1)S(1)} %get-tuple-element.32), channel_id=1, source_target_pairs={{0,14},{2,0},{4,2},{6,4},{8,6},{10,8},{12,10},{14,12},{1,15},{3,1}... | collective-permute-start | bytes 442376 | tf_op jit(solution)/shard_map/ppermute | solution.py:453
  76.4 5.3 %collective-permute-start.15 = (bf16[144,512]{1,0:T(8,128)(2,1)S(1)}, bf16[144,512]{1,0:T(8,128)(2,1)S(1)}, u32[]{:S(2)}, u32[]{:S(2)}) collective-permute-start(bf16[144,512]{1,0:T(8,128)(2,1)S(1)} %pad_maximum_fusion.2), channel_id=1, source_target_pairs={{0,2},{2,4},{4,6},{6,8},{8,10},{10,12},{12,14},{14,0},{1,3},{3,5},... | collective-permute-start | bytes 442376 | tf_op jit(solution)/shard_map/ppermute | solution.py:450
  81.7 5.1 %collective-permute-start.10 = (bf16[144,512]{1,0:T(8,128)(2,1)S(1)}, bf16[144,512]{1,0:T(8,128)(2,1)S(1)}, u32[]{:S(2)}, u32[]{:S(2)}) collective-permute-start(bf16[144,512]{1,0:T(8,128)(2,1)S(1)} %pad_maximum_fusion), channel_id=1, source_target_pairs={{0,14},{2,0},{4,2},{6,4},{8,6},{10,8},{12,10},{14,12},{1,15},{3,1}... | collective-permute-start | bytes 442376 | tf_op jit(solution)/shard_map/ppermute | solution.py:453
  81.9 5.3 %collective-permute-start.16 = (bf16[144,512]{1,0:T(8,128)(2,1)S(1)}, bf16[144,512]{1,0:T(8,128)(2,1)S(1)}, u32[]{:S(2)}, u32[]{:S(2)}) collective-permute-start(bf16[144,512]{1,0:T(8,128)(2,1)S(1)} %pad_maximum_fusion.3), channel_id=1, source_target_pairs={{0,2},{2,4},{4,6},{6,8},{8,10},{10,12},{12,14},{14,0},{1,3},{3,5},... | collective-permute-start | bytes 442376 | tf_op jit(solution)/shard_map/ppermute | solution.py:450
  83.4 5.4 %collective-permute-start.7 = (bf16[144,512]{1,0:T(8,128)(2,1)S(1)}, bf16[144,512]{1,0:T(8,128)(2,1)S(1)}, u32[]{:S(2)}, u32[]{:S(2)}) collective-permute-start(bf16[144,512]{1,0:T(8,128)(2,1)S(1)} %get-tuple-element.31.refs_0_), channel_id=1, source_target_pairs={{0,1},{1,0},{2,3},{3,2},{4,5},{5,4},{6,7},{7,6},{8,9},{9,8},{10,11... | collective-permute-start | bytes 442376 | tf_op jit(solution)/shard_map/ppermute | solution.py:424
  86.3 6.6 %collective-permute-start.9 = (bf16[144,512]{1,0:T(8,128)(2,1)S(1)}, bf16[144,512]{1,0:T(8,128)(2,1)S(1)}, u32[]{:S(2)}, u32[]{:S(2)}) collective-permute-start(bf16[144,512]{1,0:T(8,128)(2,1)S(1)} %collective-permute-done.8.refs_2_), channel_id=1, source_target_pairs={{0,1},{1,0},{2,3},{3,2},{4,5},{5,4},{6,7},{7,6},{8,9},{9,8},{10,11... | collective-permute-start | bytes 442376 | tf_op jit(solution)/shard_map/ppermute | solution.py:424
  86.3 6.7 %collective-permute-start.21 = (bf16[144,512]{1,0:T(8,128)(2,1)S(1)}, bf16[144,512]{1,0:T(8,128)(2,1)S(1)}, u32[]{:S(2)}, u32[]{:S(2)}) collective-permute-start(bf16[144,512]{1,0:T(8,128)(2,1)S(1)} %collective-permute-done.14.refs_14_), channel_id=1, source_target_pairs={{0,1},{1,0},{2,3},{3,2},{4,5},{5,4},{6,7},{7,6},{8,9},{9,8},{10,11... | collective-permute-start | bytes 442376 | tf_op jit(solution)/shard_map/ppermute | solution.py:424
  87.2 6.2 %collective-permute-start.12 = (bf16[144,512]{1,0:T(8,128)(2,1)S(1)}, bf16[144,512]{1,0:T(8,128)(2,1)S(1)}, u32[]{:S(2)}, u32[]{:S(2)}) collective-permute-start(bf16[144,512]{1,0:T(8,128)(2,1)S(1)} %pad_maximum_fusion.1), channel_id=1, source_target_pairs={{0,14},{2,0},{4,2},{6,4},{8,6},{10,8},{12,10},{14,12},{1,15},{3,1}... | collective-permute-start | bytes 442376 | tf_op jit(solution)/shard_map/ppermute | solution.py:453
  87.9 8.0 %collective-permute-start.17 = (bf16[144,512]{1,0:T(8,128)(2,1)S(1)}, bf16[144,512]{1,0:T(8,128)(2,1)S(1)}, u32[]{:S(2)}, u32[]{:S(2)}) collective-permute-start(bf16[144,512]{1,0:T(8,128)(2,1)S(1)} %pad_maximum_fusion.4), channel_id=1, source_target_pairs={{0,2},{2,4},{4,6},{6,8},{8,10},{10,12},{12,14},{14,0},{1,3},{3,5},... | collective-permute-start | bytes 442376 | tf_op jit(solution)/shard_map/ppermute | solution.py:450
  88.8 8.4 %collective-permute-start.20 = (bf16[144,512]{1,0:T(8,128)(2,1)S(1)}, bf16[144,512]{1,0:T(8,128)(2,1)S(1)}, u32[]{:S(2)}, u32[]{:S(2)}) collective-permute-start(bf16[144,512]{1,0:T(8,128)(2,1)S(1)} %collective-permute-done.15.refs_12_), channel_id=1, source_target_pairs={{0,1},{1,0},{2,3},{3,2},{4,5},{5,4},{6,7},{7,6},{8,9},{9,8},{10,11... | collective-permute-start | bytes 442376 | tf_op jit(solution)/shard_map/ppermute | solution.py:424
  92.9 4.3 %collective-permute-start.19 = (bf16[144,512]{1,0:T(8,128)(2,1)S(1)}, bf16[144,512]{1,0:T(8,128)(2,1)S(1)}, u32[]{:S(2)}, u32[]{:S(2)}) collective-permute-start(bf16[144,512]{1,0:T(8,128)(2,1)S(1)} %collective-permute-done.16.refs_10_), channel_id=1, source_target_pairs={{0,1},{1,0},{2,3},{3,2},{4,5},{5,4},{6,7},{7,6},{8,9},{9,8},{10,11... | collective-permute-start | bytes 442376 | tf_op jit(solution)/shard_map/ppermute | solution.py:424
  93.0 4.3 %collective-permute-start.11 = (bf16[144,512]{1,0:T(8,128)(2,1)S(1)}, bf16[144,512]{1,0:T(8,128)(2,1)S(1)}, u32[]{:S(2)}, u32[]{:S(2)}) collective-permute-start(bf16[144,512]{1,0:T(8,128)(2,1)S(1)} %collective-permute-done.10.refs_4_), channel_id=1, source_target_pairs={{0,1},{1,0},{2,3},{3,2},{4,5},{5,4},{6,7},{7,6},{8,9},{9,8},{10,11... | collective-permute-start | bytes 442376 | tf_op jit(solution)/shard_map/ppermute | solution.py:424
  93.4 3.8 %collective-permute-start.13 = (bf16[144,512]{1,0:T(8,128)(2,1)S(1)}, bf16[144,512]{1,0:T(8,128)(2,1)S(1)}, u32[]{:S(2)}, u32[]{:S(2)}) collective-permute-start(bf16[144,512]{1,0:T(8,128)(2,1)S(1)} %collective-permute-done.12.refs_6_), channel_id=1, source_target_pairs={{0,1},{1,0},{2,3},{3,2},{4,5},{5,4},{6,7},{7,6},{8,9},{9,8},{10,11... | collective-permute-start | bytes 442376 | tf_op jit(solution)/shard_map/ppermute | solution.py:424
  95.9 2.3 %collective-permute-start.18 = (bf16[144,512]{1,0:T(8,128)(2,1)S(1)}, bf16[144,512]{1,0:T(8,128)(2,1)S(1)}, u32[]{:S(2)}, u32[]{:S(2)}) collective-permute-start(bf16[144,512]{1,0:T(8,128)(2,1)S(1)} %collective-permute-done.17.refs_8_), channel_id=1, source_target_pairs={{0,1},{1,0},{2,3},{3,2},{4,5},{5,4},{6,7},{7,6},{8,9},{9,8},{10,11... | collective-permute-start | bytes 442376 | tf_op jit(solution)/shard_map/ppermute | solution.py:424
  98.2 11.7 %copy-start.1 = (bf16[8192,128]{1,0:T(8,128)(2,1)S(1)}, bf16[8192,128]{1,0:T(8,128)(2,1)}, u32[]{:S(2)}) copy-start(bf16[8192,128]{1,0:T(8,128)(2,1)} %f_ref.3) | copy-start | bytes 6291460
  98.2 11.8 %copy-start.6 = (f32[128,128]{1,0:T(8,128)S(1)}, f32[128,128]{1,0:T(8,128)}, u32[]{:S(2)}) copy-start(f32[128,128]{1,0:T(8,128)} %a_ref.3) | copy-start | bytes 196612
  99.0 4.1 %collective-permute-start.24 = (bf16[128,128]{1,0:T(8,128)(2,1)S(1)}, bf16[128,128]{1,0:T(8,128)(2,1)S(1)}, u32[]{:S(2)}, u32[]{:S(2)}) collective-permute-start(bf16[128,128]{1,0:T(8,128)(2,1)S(1)} %get-tuple-element.39), channel_id=1, source_target_pairs={{0,48},{16,32},{32,16},{48,0},{1,49},{17,33},{33,17},{49,1},{2,50}... | collective-permute-start | bytes 98312 | tf_op jit(solution)/shard_map/ppermute | solution.py:428
  100.3 4.3 %collective-permute-start.23 = (bf16[128,128]{1,0:T(8,128)(2,1)S(1)}, bf16[128,128]{1,0:T(8,128)(2,1)S(1)}, u32[]{:S(2)}, u32[]{:S(2)}) collective-permute-start(bf16[128,128]{1,0:T(8,128)(2,1)S(1)} %get-tuple-element.39), channel_id=1, source_target_pairs={{0,32},{16,48},{32,0},{48,16},{1,33},{17,49},{33,1},{49,17},{2,34}... | collective-permute-start | bytes 98312 | tf_op jit(solution)/shard_map/ppermute | solution.py:428
  101.0 3.6 %collective-permute-start.22 = (bf16[128,128]{1,0:T(8,128)(2,1)S(1)}, bf16[128,128]{1,0:T(8,128)(2,1)S(1)}, u32[]{:S(2)}, u32[]{:S(2)}) collective-permute-start(bf16[128,128]{1,0:T(8,128)(2,1)S(1)} %get-tuple-element.39), channel_id=1, source_target_pairs={{0,16},{16,0},{32,48},{48,32},{1,17},{17,1},{33,49},{49,33},{2,18}... | collective-permute-start | bytes 98312 | tf_op jit(solution)/shard_map/ppermute | solution.py:428
  104.6 4.1 %collective-permute-start.27 = (bf16[128,128]{1,0:T(8,128)(2,1)S(1)}, bf16[128,128]{1,0:T(8,128)(2,1)S(1)}, u32[]{:S(2)}, u32[]{:S(2)}) collective-permute-start(bf16[128,128]{1,0:T(8,128)(2,1)S(1)} %add_convert_fusion.2.p0), channel_id=1, source_target_pairs={{0,192},{64,128},{128,64},{192,0},{1,193},{65,129},{129,65},{193,1... | collective-permute-start | bytes 98312 | tf_op jit(solution)/shard_map/ppermute | solution.py:428
  105.7 4.3 %collective-permute-start.26 = (bf16[128,128]{1,0:T(8,128)(2,1)S(1)}, bf16[128,128]{1,0:T(8,128)(2,1)S(1)}, u32[]{:S(2)}, u32[]{:S(2)}) collective-permute-start(bf16[128,128]{1,0:T(8,128)(2,1)S(1)} %add_convert_fusion.2.p0), channel_id=1, source_target_pairs={{0,128},{64,192},{128,0},{192,64},{1,129},{65,193},{129,1},{193,65... | collective-permute-start | bytes 98312 | tf_op jit(solution)/shard_map/ppermute | solution.py:428
  106.5 3.4 %collective-permute-start.25 = (bf16[128,128]{1,0:T(8,128)(2,1)S(1)}, bf16[128,128]{1,0:T(8,128)(2,1)S(1)}, u32[]{:S(2)}, u32[]{:S(2)}) collective-permute-start(bf16[128,128]{1,0:T(8,128)(2,1)S(1)} %add_convert_fusion.2.p0), channel_id=1, source_target_pairs={{0,64},{64,0},{128,192},{192,128},{1,65},{65,1},{129,193},{193,129... | collective-permute-start | bytes 98312 | tf_op jit(solution)/shard_map/ppermute | solution.py:428
  120.0 4.2 %collective-permute-start.30 = (bf16[176,128]{1,0:T(8,128)(2,1)S(1)}, bf16[176,128]{1,0:T(8,128)(2,1)S(1)}, u32[]{:S(2)}, u32[]{:S(2)}) collective-permute-start(bf16[176,128]{1,0:T(8,128)(2,1)S(1)} %constant_dynamic-update-slice_fusion), channel_id=1, source_target_pairs={{0,48},{16,32},{32,16},{48,0},{1,49},{17,33},{33,17},{49,1},{2,50}... | collective-permute-start | bytes 135176 | tf_op jit(solution)/shard_map/ppermute | solution.py:428
  121.6 4.4 %collective-permute-start.29 = (bf16[176,128]{1,0:T(8,128)(2,1)S(1)}, bf16[176,128]{1,0:T(8,128)(2,1)S(1)}, u32[]{:S(2)}, u32[]{:S(2)}) collective-permute-start(bf16[176,128]{1,0:T(8,128)(2,1)S(1)} %constant_dynamic-update-slice_fusion), channel_id=1, source_target_pairs={{0,32},{16,48},{32,0},{48,16},{1,33},{17,49},{33,1},{49,17},{2,34}... | collective-permute-start | bytes 135176 | tf_op jit(solution)/shard_map/ppermute | solution.py:428
  122.5 3.5 %collective-permute-start.28 = (bf16[176,128]{1,0:T(8,128)(2,1)S(1)}, bf16[176,128]{1,0:T(8,128)(2,1)S(1)}, u32[]{:S(2)}, u32[]{:S(2)}) collective-permute-start(bf16[176,128]{1,0:T(8,128)(2,1)S(1)} %constant_dynamic-update-slice_fusion), channel_id=1, source_target_pairs={{0,16},{16,0},{32,48},{48,32},{1,17},{17,1},{33,49},{49,33},{2,18}... | collective-permute-start | bytes 135176 | tf_op jit(solution)/shard_map/ppermute | solution.py:428
  126.1 4.2 %collective-permute-start.33 = (bf16[176,128]{1,0:T(8,128)(2,1)S(1)}, bf16[176,128]{1,0:T(8,128)(2,1)S(1)}, u32[]{:S(2)}, u32[]{:S(2)}) collective-permute-start(bf16[176,128]{1,0:T(8,128)(2,1)S(1)} %add_convert_fusion.p0), channel_id=1, source_target_pairs={{0,192},{64,128},{128,64},{192,0},{1,193},{65,129},{129,65},{193,1... | collective-permute-start | bytes 135176 | tf_op jit(solution)/shard_map/ppermute | solution.py:428
  127.7 4.4 %collective-permute-start.32 = (bf16[176,128]{1,0:T(8,128)(2,1)S(1)}, bf16[176,128]{1,0:T(8,128)(2,1)S(1)}, u32[]{:S(2)}, u32[]{:S(2)}) collective-permute-start(bf16[176,128]{1,0:T(8,128)(2,1)S(1)} %add_convert_fusion.p0), channel_id=1, source_target_pairs={{0,128},{64,192},{128,0},{192,64},{1,129},{65,193},{129,1},{193,65... | collective-permute-start | bytes 135176 | tf_op jit(solution)/shard_map/ppermute | solution.py:428
  128.6 3.6 %collective-permute-start.31 = (bf16[176,128]{1,0:T(8,128)(2,1)S(1)}, bf16[176,128]{1,0:T(8,128)(2,1)S(1)}, u32[]{:S(2)}, u32[]{:S(2)}) collective-permute-start(bf16[176,128]{1,0:T(8,128)(2,1)S(1)} %add_convert_fusion.p0), channel_id=1, source_target_pairs={{0,64},{64,0},{128,192},{192,128},{1,65},{65,1},{129,193},{193,129... | collective-permute-start | bytes 135176 | tf_op jit(solution)/shard_map/ppermute | solution.py:428
  132.8 6.9 %collective-permute-start.34 = (f32[40,128]{1,0:T(8,128)S(1)}, f32[40,128]{1,0:T(8,128)S(1)}, u32[]{:S(2)}, u32[]{:S(2)}) collective-permute-start(f32[40,128]{1,0:T(8,128)S(1)} %get-tuple-element.40), channel_id=1, source_target_pairs={{0,1},{1,0},{2,3},{3,2},{4,5},{5,4},{6,7},{7,6},{8,9},{9,8},{10,11... | collective-permute-start | bytes 61448 | tf_op jit(solution)/shard_map/ppermute | solution.py:424
Sparse Core Ops, SparseCore 0:
  9.8 43.1 all-gather.1

commit v3 on v2

--- a/solution.py
+++ b/solution.py
@@ -47,54 +47,56 @@
     return u, r, m
 
 
-def scaled_dirs(anchors, metric):
+def anchor_dirs(anchors, metric):
     rows = []
     for h in range(HEADS):
-        u, r, m = anchor_rows(anchors, metric, h)
-        rows.append((u * r * (m * (1.0 / HEADS))).astype(bf16))
-    return jnp.concatenate(rows, axis=0)
-
-
-def head_scores(am, ft, rinv):
-    prod = mm(am, ft, NN)
-    return [prod[h * APD : (h + 1) * APD, :] * rinv[h : h + 1, :] for h in range(HEADS)]
-
-
-def excess_of(parts):
-    score = (parts[0] + parts[1]) + (parts[2] + parts[3])
-    return jnp.maximum(score - threshold, 0.0)
+        u, r, _ = anchor_rows(anchors, metric, h)
+        rows.append((u * (r * (1.0 / HEADS))).astype(bf16))
+    return jnp.concatenate(rows, axis=1)
+
+
+def node_dirs(ft, m_cols):
+    dirs, norms = [], []
+    for h in range(HEADS):
+        u = ft * m_cols(h, ft.shape[1])
+        r = lax.rsqrt(jnp.sum(u * u, axis=0, keepdims=True) + 1e-06)
+        dirs.append((u * r).astype(bf16))
+        norms.append(r)
+    return jnp.concatenate(dirs, axis=0), jnp.concatenate(norms + norms, axis=0)
+
+
+def wide_column(x, width):
+    return jnp.concatenate([x] * (width // x.shape[1]), axis=1)
 
 
 LINK_BLOCK = 1024
 CHUNK = 256
 
 
-def link_kernel(f_ref, a_ref, m_ref, ft_ref, rinv_ref, lb_ref, am_ref, msg_ref, tot, raw, m2c):
+def link_kernel(f_ref, a_ref, m_ref, lab_ref, mask_ref, ft_ref, rinv_ref, e_ref, lb_ref, tag_ref, am_ref, msg_ref, tot, raw, mc, ad):
     i = pl.program_id(0)
 
     @pl.when(i == 0)
     def _():
-        am_ref[...] = scaled_dirs(a_ref[...], m_ref[...])
+        anchors, metric = a_ref[...], m_ref[...]
+        ad[...] = anchor_dirs(anchors, metric)
         for h in range(HEADS):
-            m = m_ref[h : h + 1, :]
-            m2c[h] = column(m * m)
+            u, r, m = anchor_rows(anchors, metric, h)
+            am_ref[h * APD : (h + 1) * APD, :] = (u * r * m).astype(bf16)
+            mc[h] = column(m)
         tot[...] = jnp.zeros_like(tot)
         raw[...] = jnp.zeros_like(raw)
 
+    tag_ref[...] = jnp.where(mask_ref[...] > 0, lab_ref[...], -1)
     for j in range(LINK_BLOCK // CHUNK):
         cols = slice(j * CHUNK, (j + 1) * CHUNK)
         ft = f_ref[cols, :].astype(f32).T
-        ft_b = ft.astype(bf16)
-        ft_ref[:, cols] = ft_b
-        sq = ft * ft
-        norms = []
-        for h in range(HEADS):
-            m2 = jnp.concatenate([m2c[h]] * (CHUNK // F), axis=1)
-            norms.append(jnp.sum(sq * m2, axis=0, keepdims=True))
-        rinv = lax.rsqrt(jnp.concatenate(norms + norms, axis=0) + 1e-06)
+        ft_ref[:, cols] = ft.astype(bf16)
+        dirs, rinv = node_dirs(ft, lambda h, width: wide_column(mc[h], width))
         rinv_ref[:, cols] = rinv
-        e = excess_of(head_scores(am_ref[...], ft_b, rinv))
+        e = jnp.maximum(mm(ad[...], dirs, NN) - threshold, 0.0)
         link = e * e
+        e_ref[:, cols] = e
         lb_ref[:, cols] = link.astype(bf16)
         raw[...] += sum(link[:, k * F : (k + 1) * F] for k in range(CHUNK // F))
     tot[...] += mm(lb_ref[...], f_ref[...], NN)
@@ -106,9 +108,10 @@
         msg_ref[APD : APD + 16, :] = sum(t[16 * k : 16 * k + 16, :] for k in range(8)).astype(bf16)
 
 
-def link_call(features, anchors, metric):
+def link_call(features, anchors, metric, labels, mask):
     n = features.shape[0]
     const = lambda i: (0, 0)
+    wide = lambda rows: pl.BlockSpec((rows, LINK_BLOCK), lambda i: (0, i))
     return pl.pallas_call(
         link_kernel,
         grid=(n // LINK_BLOCK,),
@@ -116,18 +119,24 @@
             pl.BlockSpec((LINK_BLOCK, F), lambda i: (i, 0)),
             pl.BlockSpec((APD, F), const),
             pl.BlockSpec((HEADS, F), const),
+            wide(1),
+            wide(1),
         ],
         out_specs=[
-            pl.BlockSpec((F, LINK_BLOCK), lambda i: (0, i)),
-            pl.BlockSpec((8, LINK_BLOCK), lambda i: (0, i)),
-            pl.BlockSpec((APD, LINK_BLOCK), lambda i: (0, i)),
+            wide(F),
+            wide(8),
+            wide(APD),
+            wide(APD),
+            wide(1),
             pl.BlockSpec((HEADS * APD, F), const),
             pl.BlockSpec((APD + 16, F), const),
         ],
         out_shape=[
             jax.ShapeDtypeStruct((F, n), bf16),
             jax.ShapeDtypeStruct((8, n), f32),
+            jax.ShapeDtypeStruct((APD, n), f32),
             jax.ShapeDtypeStruct((APD, n), bf16),
+            jax.ShapeDtypeStruct((1, n), jnp.int32),
             jax.ShapeDtypeStruct((HEADS * APD, F), bf16),
             jax.ShapeDtypeStruct((APD + 16, F), bf16),
         ],
@@ -135,59 +144,58 @@
             pltpu.VMEM((APD, F), f32),
             pltpu.VMEM((APD, F), f32),
             pltpu.VMEM((HEADS, F, F), f32),
-        ],
-        compiler_params=params(),
-    )(features, anchors, metric)
+            pltpu.VMEM((APD, HEADS * F), bf16),
+        ],
+        compiler_params=params(60),
+    )(features, anchors, metric, labels, mask)
 
 
 def four(a, b, c, d):
     return (a[...].astype(f32) + b[...].astype(f32)) + (c[...].astype(f32) + d[...].astype(f32))
 
 
-def mean_kernel(a, b, c, d, total_ref, degree_ref, means_ref):
+def mean_kernel(a, b, c, d, anchors_ref, total_ref, degree_ref, means_ref, msg_ref):
     s = four(a, b, c, d)
     total = s[0:APD, :]
     degree = column(jnp.sum(s[APD:, :], axis=0, keepdims=True) + degree_floor)
     total_ref[...] = total
     degree_ref[...] = degree
     means = (total / degree).astype(bf16)
+    means_ref[...] = means
+    anchors = anchors_ref[...].astype(bf16)
     for z in range(NZ):
-        means_ref[z] = means
-
-
-def mean_call(parts):
+        msg_ref[z, 0:APD, :] = means
+        msg_ref[z, APD:, :] = anchors
+
+
+def mean_call(parts, anchors):
     return pl.pallas_call(
         mean_kernel,
-        in_specs=[vspec()] * 4,
-        out_specs=[vspec()] * 3,
+        in_specs=[vspec()] * 5,
+        out_specs=[vspec()] * 4,
         out_shape=[
             jax.ShapeDtypeStruct((APD, F), f32),
             jax.ShapeDtypeStruct((APD, F), f32),
-            jax.ShapeDtypeStruct((NZ, APD, F), bf16),
-        ],
-        compiler_params=params(),
-    )(*parts)
-
-
-def head_kernel(s_ref, all_ref, m_ref, ft_ref, rinv_ref, ma_ref, mb_ref, cls_ref, lab_ref, mask_ref, emb_ref, up_ref, down_ref, part_ref, loss_ref):
-    core = lax.rem(s_ref[0], 2)
+            jax.ShapeDtypeStruct((APD, F), bf16),
+            jax.ShapeDtypeStruct((NZ, 2 * APD, F), bf16),
+        ],
+        compiler_params=params(),
+    )(*parts, anchors)
+
+
+def head_kernel(s_ref, m_ref, ft_ref, ma_ref, mb_ref, cls_ref, tag_ref, emb_ref, up_ref, down_ref, part_ref, loss_ref):
     metric = m_ref[...]
-    ft = ft_ref[...]
-    rinv = rinv_ref[...]
-
-    def links(z, which, means_ref, field, raw):
-        shard = 2 * z + which
-        rows = pl.ds(pl.multiple_of(shard * APD, APD), APD)
-        am = scaled_dirs(all_ref[rows, :], metric)
-        e = excess_of(head_scores(am, ft, rinv))
-        link = e * e
-        field = field + mm(means_ref[z], link.astype(bf16), TN)
-        raw = raw + sum(link[8 * k : 8 * k + 8, :] for k in range(APD // 8))
+    dirs, _ = node_dirs(ft_ref[...].astype(f32), lambda h, width: wide_column(column(metric[h : h + 1, :]), width))
+
+    def step(z, carry):
+        field, raw = carry
+        for ref in (ma_ref, mb_ref):
+            ad = anchor_dirs(ref[z, APD:, :].astype(f32), metric)
+            e = jnp.maximum(mm(ad, dirs, NN) - threshold, 0.0)
+            link = e * e
+            field = field + mm(ref[z, 0:APD, :], link.astype(bf16), TN)
+            raw = raw + sum(link[8 * k : 8 * k + 8, :] for k in range(APD // 8))
         return field, raw
-
-    def step(z, carry):
-        field, raw = links(z, core, ma_ref, *carry)
-        return links(z, 1 - core, mb_ref, field, raw)
 
     field, raw = lax.fori_loop(0, NZ, step, (jnp.zeros((F, OWN), f32), jnp.zeros((8, OWN), f32)))
     inv_degree = 1.0 / (jnp.sum(raw, axis=0, keepdims=True) + degree_floor)
@@ -197,8 +205,8 @@
     cls_t = cls_ref[...]
     logits = mm(cls_t, field, NN, highest)
     ids = lax.broadcasted_iota(jnp.int32, (CPAD, OWN), 0)
-    target = jnp.where(ids == lab_ref[...], 1.0, 0.0)
-    residual = mask_ref[...].astype(f32) * (logits - target)
+    tag = tag_ref[...]
+    residual = jnp.where(tag >= 0, logits - jnp.where(ids == tag, 1.0, 0.0), 0.0)
     loss_row = jnp.sum(residual * residual, axis=0, keepdims=True)
     loss_row = sum(loss_row[:, k * F : (k + 1) * F] for k in range(OWN // F))
     loss_ref[...] = jnp.concatenate([loss_row, jnp.zeros((7, F), f32)], axis=0)
@@ -214,7 +222,7 @@
         ref[F : F + 16, :] = jnp.concatenate([degree_grads, jnp.zeros((7, OWN), f32), part_ref[k]], axis=0).astype(bf16)
 
 
-def head_call(shard, anchors_all, metric, ft, rinv, means_a, means_b, cls_t, labels, mask):
+def head_call(shard, metric, ft, means_a, means_b, cls_t, tags):
     zero2 = lambda i, s: (0, 0)
     zero3 = lambda i, s: (0, 0, 0)
     own = lambda i, s: (0, s[0])
@@ -224,14 +232,11 @@
             num_scalar_prefetch=1,
             grid=(1,),
             in_specs=[
-                pl.BlockSpec(anchors_all.shape, zero2),
                 pl.BlockSpec((HEADS, F), zero2),
                 pl.BlockSpec((F, OWN), own),
-                pl.BlockSpec((8, OWN), own),
-                pl.BlockSpec((NZ, APD, F), zero3),
-                pl.BlockSpec((NZ, APD, F), zero3),
+                pl.BlockSpec((NZ, 2 * APD, F), zero3),
+                pl.BlockSpec((NZ, 2 * APD, F), zero3),
                 pl.BlockSpec((CPAD, F), zero2),
-                pl.BlockSpec((1, OWN), own),
                 pl.BlockSpec((1, OWN), own),
             ],
             out_specs=[
@@ -250,7 +255,7 @@
             jax.ShapeDtypeStruct((8, F), f32),
         ],
         compiler_params=params(),
-    )(shard, anchors_all, metric, ft, rinv, means_a, means_b, cls_t, labels, mask)
+    )(shard, metric, ft, means_a, means_b, cls_t, tags)
 
 
 def mean_grad_kernel(s_ref, lb_ref, *refs):
@@ -280,8 +285,8 @@
 
 
 def score_kernel(
-    f_ref, ft_ref, r_ref, g_ref, am_ref, a_ref, m_ref, means_ref, total_ref, degree_ref, loss_ref,
-    p0, p1, p2, p3, msg_ref, acc, vacc, tg, adg, sgr
+    f_ref, ft_ref, r_ref, e_ref, g_ref, am_ref, a_ref, m_ref, means_ref, total_ref, degree_ref, loss_ref,
+    p0, p1, p2, p3, msg_ref, acc, vacc, lhs, adg, sgr
 ):
     i = pl.program_id(0)
 
@@ -289,29 +294,27 @@
     def _():
         grads = four(p0, p1, p2, p3)
         inv = 1.0 / degree_ref[...]
-        tg[...] = (grads * inv).astype(bf16)
+        lhs[:, 0:F] = means_ref[...] * 0.5
+        lhs[:, F:] = (grads * inv).astype(bf16) * 0.5
         dots = jnp.sum(grads * total_ref[...], axis=1, keepdims=True)
-        adg[...] = -dots * (inv * inv)
+        adg[...] = (-2.0 / HEADS) * dots * (inv * inv)
         acc[...] = jnp.zeros_like(acc)
         vacc[...] = jnp.zeros_like(vacc)
 
-    am = am_ref[...]
     rows = []
     for j in range(SCORE_BLOCK // CHUNK):
         cols = slice(j * CHUNK, (j + 1) * CHUNK)
         ft = ft_ref[:, cols]
         rinv = r_ref[:, cols]
-        dg = g_ref[F : F + 16, cols].astype(f32)[0:1, :]
-        parts = head_scores(am, ft, rinv)
-        e = excess_of(parts)
-        link_grads = mm(means_ref[...], g_ref[0:F, cols], NN) + mm(tg[...], ft, NN)
-        link_grads = link_grads + dg + jnp.concatenate([adg[...]] * (CHUNK // F), axis=1)
-        sg = link_grads * (2.0 / HEADS) * e
+        dg = g_ref[F : F + 16, cols].astype(f32)[0:1, :] * (2.0 / HEADS)
+        link_grads = mm(lhs[...], jnp.concatenate([g_ref[0:F, cols], ft], axis=0), NN)
+        sg = (link_grads + dg + wide_column(adg[...], CHUNK)) * e_ref[:, cols]
         ws = []
         for h in range(HEADS):
             r = rinv[h : h + 1, :]
             sgr[h * APD : (h + 1) * APD, cols] = (sg * r).astype(bf16)
-            ws.append(jnp.sum(sg * parts[h], axis=0, keepdims=True) * (r * r))
+            prod = mm(am_ref[h * APD : (h + 1) * APD, :], ft, NN)
+            ws.append(jnp.sum(sg * prod, axis=0, keepdims=True) * (r * r * r))
         w = jnp.concatenate(ws, axis=0)
         hi = w.astype(bf16).astype(f32)
         rows.append(jnp.concatenate([hi, w - hi], axis=0))
@@ -340,8 +343,8 @@
             dirs = am_ref[h * APD : (h + 1) * APD, :].astype(f32)
             along = vacc[h : h + 1, :] + vacc[HEADS + h : HEADS + h + 1, :]
             row = jnp.sum(g * anchors, axis=0, keepdims=True)
-            row = row + jnp.sum(dirs * raw, axis=0, keepdims=True) * (HEADS / m)
-            rows.append(row - (m * HEADS) * along)
+            row = row + jnp.sum(dirs * raw, axis=0, keepdims=True) / m
+            rows.append(row - m * along)
         msg_ref[0:APD, :] = out.astype(bf16)
         rows.append(loss_ref[0:1, :])
         rows.append(jnp.zeros((11, F), f32))
@@ -351,7 +354,7 @@
 SCORE_BLOCK = 1024
 
 
-def score_call(features, ft, rinv, grads, am, anchors, metric, means, total, degree, loss, parts):
+def score_call(features, ft, rinv, excess, grads, am, anchors, metric, means, total, degree, loss, parts):
     n = features.shape[0]
     c2 = lambda i: (0, 0)
     whole = lambda x: pl.BlockSpec(x.shape, c2)
@@ -359,19 +362,19 @@
     return pl.pallas_call(
         score_kernel,
         grid=(n // SCORE_BLOCK,),
-        in_specs=[pl.BlockSpec((SCORE_BLOCK, F), lambda i: (i, 0)), wide(ft), wide(rinv), wide(grads)]
+        in_specs=[pl.BlockSpec((SCORE_BLOCK, F), lambda i: (i, 0)), wide(ft), wide(rinv), wide(excess), wide(grads)]
         + [whole(x) for x in (am, anchors, metric, means, total, degree, loss, *parts)],
         out_specs=pl.BlockSpec((APD + 16, F), c2),
         out_shape=jax.ShapeDtypeStruct((APD + 16, F), bf16),
         scratch_shapes=[
             pltpu.VMEM((HEADS * APD, F), f32),
             pltpu.VMEM((8, F), f32),
-            pltpu.VMEM((APD, F), bf16),
+            pltpu.VMEM((APD, 2 * F), bf16),
             pltpu.VMEM((APD, F), f32),
             pltpu.VMEM((HEADS * APD, SCORE_BLOCK), bf16),
         ],
         compiler_params=params(),
-    )(features, ft, rinv, grads, am, anchors, metric, means, total, degree, loss, *parts)
+    )(features, ft, rinv, excess, grads, am, anchors, metric, means, total, degree, loss, *parts)
 
 
 def last_kernel(p0, p1, p2, p3, out_ref, small_ref):
@@ -462,19 +465,16 @@
 def body(features, anchors, metric, classifier, labels, train_mask):
     n = features.shape[0]
     shard = (lax.axis_index("z") * 2 + lax.axis_index("c")).astype(jnp.int32).reshape(1)
-    anchors_all = lax.all_gather(anchors, ("z", "c"), tiled=True)
     cls_t = jnp.pad(classifier.T, ((0, CPAD - CLASSES), (0, 0)))
-    ft, rinv, lb, am, msg = link_call(features, anchors, metric)
-    total, degree, means8 = mean_call(over_dp(msg))
-    means_a = lax.all_to_all(means8, "z", 0, 0, tiled=True)
+    ft, rinv, excess, lb, tags, am, msg = link_call(features, anchors, metric, labels.reshape(1, n), train_mask.reshape(1, n))
+    total, degree, means, msg = mean_call(over_dp(msg), anchors)
+    means_a = lax.all_to_all(msg, "z", 0, 0, tiled=True)
     means_b = swap(means_a)
-    embedding, up, down, part, loss = head_call(
-        shard, anchors_all, metric, ft, rinv, means_a, means_b, cls_t, labels.reshape(1, n), train_mask.reshape(1, n)
-    )
+    embedding, up, down, part, loss = head_call(shard, metric, ft, means_a, means_b, cls_t, tags)
     blocks, cls = ring(up, down, part)
     blocks = [b for block in blocks for b in (block, swap(block))]
     msg, grads = mean_grad_call(shard, lb, blocks)
-    msg = score_call(features, ft, rinv, grads, am, anchors, metric, means8[0], total, degree, loss, over_dp(msg))
+    msg = score_call(features, ft, rinv, excess, grads, am, anchors, metric, means, total, degree, loss, over_dp(msg))
     msg = jnp.concatenate([msg, cls.astype(bf16)], axis=0)
     grad_anchors, small = last_call(over_dp(msg))
     small = small + swap(small)

time: 159 us -> 146 us (0.918)
  between operations: 14.3 us -> 0.91 us
  local copies, waits for them, and re-layouts: 8.21 us -> 2.5 us
  blocking collectives: 28.8 us -> 32.5 us
    unnamed x26, local copies, waits for them, and re-layouts: 7.24 us -> 2.42 us
    all_to_all x1, blocking collectives: 17.3 us -> 21 us  [body(): means_a = lax.all_to_all(msg, 'z', 0, 0, tiled=True)]
    pallas_call x1, Pallas kernels: 7.07 us -> 10.7 us  [link_call(): pl.pallas_call(link_kernel, grid=(n // LINK_BLOCK,), in_specs=[pl.BlockSp...]
    pallas_call x1, Pallas kernels: 9.9 us -> 8.13 us  [score_call(): pl.pallas_call(score_kernel, grid=(n // SCORE_BLOCK,), in_specs=[pl.Block...]
  transfers between devices with their start and end apart: 36 -> 35, of which waited for: 18 -> 18; matrix products, arithmetic and copies ran while one was open for 1% -> 0% of each run, Pallas kernels for 5% -> 0%
where the time goes in v3:
time: 146 us
  starting transfers between devices  50.2 us (34%)
  blocking collectives  32.5 us (22%)
  waiting for transfers between devices  29.7 us (20%)
  Pallas kernels  29.2 us (20%)
  local copies, waits for them, and re-layouts  2.5 us (2%)
    ppermute x10, starting transfers between devices, swap(): return lax.ppermute(x, 'c', [(0, 1), (1, 0)])  23.3 us
    all_to_all x1, blocking collectives, body(): means_a = lax.all_to_all(msg, 'z', 0, 0, tiled=True)  21 us
    ppermute x18, starting transfers between devices, shared(): lax.ppermute(x, axis, [(i, i ^ k) for i in range(4)])  20.9 us
    ppermute x18, waiting for transfers between devices, shared(): lax.ppermute(x, axis, [(i, i ^ k) for i in range(4)])  17.2 us
    all_to_all x1, blocking collectives, body(): lax.all_to_all(jnp.broadcast_to(small[None], (NZ,) + small.shape), 'z', 0...  11.6 us
    pallas_call x1, Pallas kernels, link_call(): pl.pallas_call(link_kernel, grid=(n // LINK_BLOCK,), in_specs=[pl.BlockSp...  10.7 us
    ppermute x4, waiting for transfers between devices, ring(): up = lax.ppermute(up, 'z', ups)  9.08 us
    pallas_call x1, Pallas kernels, score_call(): pl.pallas_call(score_kernel, grid=(n // SCORE_BLOCK,), in_specs=[pl.Block...  8.13 us
  transfers between devices with their start and end apart: 35, of which 18 were waited for; matrix products, arithmetic and copies ran while one was open for 0% of the time, Pallas kernels for 0%

profile of v3, /device:TPU:1, one launch (start us, length us, event | category | flops | bytes accessed | tf_op | source)
XLA Modules:
  0.0 146.0 jit_solution(8337360924765775868)
XLA Ops:
  0.7 10.7 %shard_map.101 = (bf16[128,8192]{1,0:T(8,128)(2,1)}, f32[8,8192]{1,0:T(8,128)}, f32[128,8192]{1,0:T(8,128)}, bf16[128,8192]{1,0:T(8,128)(2,1)}, s32[1,8192]{1,0:...) custom-call(bf16[8192,128]{1,0:T(8,128)(2,1)} %f_ref.3, f32[128,128]{1,0:T(8,128)} %a_ref.3, ...), custom_call_target="tpu_custom_call" | custom-call | tf_op jit(solution)/shard_map/pallas_call | solution.py:115
  11.4 3.4 %collective-permute-start.2 = (bf16[144,128]{1,0:T(8,128)(2,1)}, bf16[144,128]{1,0:T(8,128)(2,1)S(1)}, u32[]{:S(2)}, u32[]{:S(2)}) collective-permute-start(bf16[144,128]{1,0:T(8,128)(2,1)} %get-tuple-element.29), channel_id=1, source_target_pairs={{0,48},{16,32},{32,16},{48,0},{1,49},{17,33},{33,17},{49,1},{2,50}... | collective-permute-start | bytes 110600 | tf_op jit(solution)/shard_map/ppermute | solution.py:431
  15.4 0.9 collective-permute-done.2
  16.3 3.0 %collective-permute-done.1 = bf16[144,128]{1,0:T(8,128)(2,1)S(1)} collective-permute-done((bf16[144,128]{1,0:T(8,128)(2,1)}, bf16[144,128]{1,0:T(8,128)(2,1)S(1)}, u32[]{:S(2)}, u32[]{:S(2)}) %collective-permute-start.1) | collective-permute-done | bytes 36896 | tf_op jit(solution)/shard_map/ppermute | solution.py:431
  19.3 0.8 add_convert_fusion.1.a
  20.1 2.8 %collective-permute-start.5 = (bf16[144,128]{1,0:T(8,128)(2,1)S(1)}, bf16[144,128]{1,0:T(8,128)(2,1)S(1)}, u32[]{:S(2)}, u32[]{:S(2)}) collective-permute-start(bf16[144,128]{1,0:T(8,128)(2,1)S(1)} %add_convert_fusion.1.a), channel_id=1, source_target_pairs={{0,192},{64,128},{128,64},{192,0},{1,193},{65,129},{129,65},{193,1... | collective-permute-start | bytes 110600 | tf_op jit(solution)/shard_map/ppermute | solution.py:431
  24.3 3.0 %collective-permute-done.4.c = bf16[144,128]{1,0:T(8,128)(2,1)S(1)} collective-permute-done((bf16[144,128]{1,0:T(8,128)(2,1)S(1)}, bf16[144,128]{1,0:T(8,128)(2,1)S(1)}, u32[]{:S(2)}, u32[]{:S(2)}) %collective-permute-start.4) | collective-permute-done | bytes 36896 | tf_op jit(solution)/shard_map/ppermute | solution.py:431
  27.4 21.0 %all_to_all.10.ma_ref = bf16[8,256,128]{2,1,0:T(8,128)(2,1)S(1)} all-to-all(bf16[8,256,128]{2,1,0:T(8,128)(2,1)S(1)} %get-tuple-element.30), channel_id=1, replica_groups=mesh['y'=4,'x'=4,'z'=8,'c'=2] {'z'}, dimensions={0} | all-to-all | bytes 1048576 | tf_op jit(solution)/shard_map/all_to_all | solution.py:471
  48.3 5.5 %collective-permute-start.6 = (bf16[8,256,128]{2,1,0:T(8,128)(2,1)S(1)}, bf16[8,256,128]{2,1,0:T(8,128)(2,1)S(1)}, u32[]{:S(2)}, u32[]{:S(2)}) collective-permute-start(bf16[8,256,128]{2,1,0:T(8,128)(2,1)S(1)} %all_to_all.10.ma_ref), channel_id=1, source_target_pairs={{0,1},{1,0},{2,3},{3,2},{4,5},{5,4},{6,7},{7,6},{8,9},{9,8},{10,11... | collective-permute-start | bytes 1572872 | tf_op jit(solution)/shard_map/ppermute | solution.py:427
  53.8 1.5 %collective-permute-done.6.mb_ref = bf16[8,256,128]{2,1,0:T(8,128)(2,1)S(1)} collective-permute-done((bf16[8,256,128]{2,1,0:T(8,128)(2,1)S(1)}, bf16[8,256,128]{2,1,0:T(8,128)(2,1)S(1)}, u32[]{:S(2)}, u32[]{:S(2)}) %collective-permute-start.6) | collective-permute-done | bytes 524320 | tf_op jit(solution)/shard_map/ppermute | solution.py:427
  55.3 1.6 %copy-done.1 = bf16[128,8192]{1,0:T(8,128)(2,1)S(1)} copy-done((bf16[128,8192]{1,0:T(8,128)(2,1)S(1)}, bf16[128,8192]{1,0:T(8,128)(2,1)}, u32[]{:S(2)}) %copy-start.1) | copy-done | bytes 2097176
  56.9 0.8 copy-done.8
  57.7 8.1 %shard_map.103 = (bf16[512,128]{1,0:T(8,128)(2,1)}, bf16[144,512]{1,0:T(8,128)(2,1)S(1)}, bf16[144,512]{1,0:T(8,128)(2,1)S(1)}, f32[8,8,512]{2,1,0:T(8,128)S(1)}, f32[8,128]{1,0:T(8,128)S(1)}) custom-call(s32[1]{0:T(128)} %bitcast.s_ref, f32[4,128]{1,0:T(4,128)S(1)} %copy-done.9, bf16[128,8192]{1,0:T(8,128)(2,1)S(1)} %copy-done.1, ...), custom_call_target="tpu_custom_call" | custom-call | tf_op jit(solution)/shard_map/pallas_call | solution.py:229
  66.1 2.4 %collective-permute-start.8 = (bf16[144,512]{1,0:T(8,128)(2,1)S(1)}, bf16[144,512]{1,0:T(8,128)(2,1)S(1)}, u32[]{:S(2)}, u32[]{:S(2)}) collective-permute-start(bf16[144,512]{1,0:T(8,128)(2,1)S(1)} %get-tuple-element.37), channel_id=1, source_target_pairs={{0,14},{2,0},{4,2},{6,4},{8,6},{10,8},{12,10},{14,12},{1,15},{3,1}... | collective-permute-start | bytes 442376 | tf_op jit(solution)/shard_map/ppermute | solution.py:456
  68.5 3.6 %collective-permute-done.14.refs_14_ = bf16[144,512]{1,0:T(8,128)(2,1)S(1)} collective-permute-done((bf16[144,512]{1,0:T(8,128)(2,1)S(1)}, bf16[144,512]{1,0:T(8,128)(2,1)S(1)}, u32[]{:S(2)}, u32[]{:S(2)}) %collective-permute-start.14) | collective-permute-done | bytes 147488 | tf_op jit(solution)/shard_map/ppermute | solution.py:453
  72.2 5.2 %collective-permute-done.15.refs_12_ = bf16[144,512]{1,0:T(8,128)(2,1)S(1)} collective-permute-done((bf16[144,512]{1,0:T(8,128)(2,1)S(1)}, bf16[144,512]{1,0:T(8,128)(2,1)S(1)}, u32[]{:S(2)}, u32[]{:S(2)}) %collective-permute-start.15) | collective-permute-done | bytes 147488 | tf_op jit(solution)/shard_map/ppermute | solution.py:453
  77.5 1.5 %collective-permute-start.16 = (bf16[144,512]{1,0:T(8,128)(2,1)S(1)}, bf16[144,512]{1,0:T(8,128)(2,1)S(1)}, u32[]{:S(2)}, u32[]{:S(2)}) collective-permute-start(bf16[144,512]{1,0:T(8,128)(2,1)S(1)} %pad_maximum_fusion.3), channel_id=1, source_target_pairs={{0,2},{2,4},{4,6},{6,8},{8,10},{10,12},{12,14},{14,0},{1,3},{3,5},... | collective-permute-start | bytes 442376 | tf_op jit(solution)/shard_map/ppermute | solution.py:453
  79.1 2.9 %collective-permute-start.7 = (bf16[144,512]{1,0:T(8,128)(2,1)S(1)}, bf16[144,512]{1,0:T(8,128)(2,1)S(1)}, u32[]{:S(2)}, u32[]{:S(2)}) collective-permute-start(bf16[144,512]{1,0:T(8,128)(2,1)S(1)} %get-tuple-element.36.refs_0_), channel_id=1, source_target_pairs={{0,1},{1,0},{2,3},{3,2},{4,5},{5,4},{6,7},{7,6},{8,9},{9,8},{10,11... | collective-permute-start | bytes 442376 | tf_op jit(solution)/shard_map/ppermute | solution.py:427
  82.8 0.7 collective-permute-start.12
  83.6 0.9 collective-permute-start.17
  84.5 4.1 %collective-permute-start.20 = (bf16[144,512]{1,0:T(8,128)(2,1)S(1)}, bf16[144,512]{1,0:T(8,128)(2,1)S(1)}, u32[]{:S(2)}, u32[]{:S(2)}) collective-permute-start(bf16[144,512]{1,0:T(8,128)(2,1)S(1)} %collective-permute-done.15.refs_12_), channel_id=1, source_target_pairs={{0,1},{1,0},{2,3},{3,2},{4,5},{5,4},{6,7},{7,6},{8,9},{9,8},{10,11... | collective-permute-start | bytes 442376 | tf_op jit(solution)/shard_map/ppermute | solution.py:427
  89.1 2.5 %collective-permute-start.13 = (bf16[144,512]{1,0:T(8,128)(2,1)S(1)}, bf16[144,512]{1,0:T(8,128)(2,1)S(1)}, u32[]{:S(2)}, u32[]{:S(2)}) collective-permute-start(bf16[144,512]{1,0:T(8,128)(2,1)S(1)} %collective-permute-done.12.refs_6_), channel_id=1, source_target_pairs={{0,1},{1,0},{2,3},{3,2},{4,5},{5,4},{6,7},{7,6},{8,9},{9,8},{10,11... | collective-permute-start | bytes 442376 | tf_op jit(solution)/shard_map/ppermute | solution.py:427
  91.6 1.3 collective-permute-start.18
  92.9 1.0 collective-permute-done.18.refs_9_
  93.9 0.8 shard_map.104
  94.8 1.2 collective-permute-start.24
  96.6 1.5 %collective-permute-start.22 = (bf16[128,128]{1,0:T(8,128)(2,1)S(1)}, bf16[128,128]{1,0:T(8,128)(2,1)S(1)}, u32[]{:S(2)}, u32[]{:S(2)}) collective-permute-start(bf16[128,128]{1,0:T(8,128)(2,1)S(1)} %get-tuple-element.45), channel_id=1, source_target_pairs={{0,16},{16,0},{32,48},{48,32},{1,17},{17,1},{33,49},{49,33},{2,18}... | collective-permute-start | bytes 98312 | tf_op jit(solution)/shard_map/ppermute | solution.py:431
  98.1 0.7 collective-permute-done.24
  98.8 1.4 collective-permute-done.23
  100.3 0.8 collective-permute-start.27
  101.1 1.0 collective-permute-start.26
  102.1 1.5 %collective-permute-start.25 = (bf16[128,128]{1,0:T(8,128)(2,1)S(1)}, bf16[128,128]{1,0:T(8,128)(2,1)S(1)}, u32[]{:S(2)}, u32[]{:S(2)}) collective-permute-start(bf16[128,128]{1,0:T(8,128)(2,1)S(1)} %add_convert_fusion.2.p0), channel_id=1, source_target_pairs={{0,64},{64,0},{128,192},{192,128},{1,65},{65,1},{129,193},{193,129... | collective-permute-start | bytes 98312 | tf_op jit(solution)/shard_map/ppermute | solution.py:431
  103.6 0.7 collective-permute-done.27.p3
  104.3 1.0 collective-permute-done.26.p2
  105.4 8.1 %shard_map.105 = bf16[144,128]{1,0:T(8,128)(2,1)S(1)} custom-call(bf16[8192,128]{1,0:T(8,128)(2,1)S(1)} %copy-done, bf16[128,8192]{1,0:T(8,128)(2,1)S(1)} %copy-done.2, f32[8,8192]{1,0:T(8,128)S(1)} %copy-done.6, f32[128,8192]{1,0:T(8,128)S(1)} %copy-done.3, bf16[144,8192]{1,0:T(8,128)(2,1)S(1)} %get-tuple-element.39.g_ref, bf16[512,128]{1,0:T(8,128)(2,1)S(1)} %copy-done.7, ...), custom_call_target="tpu_custom_call" | custom-call | tf_op jit(solution)/shard_map/pallas_call | solution.py:362
  113.6 1.6 %collective-permute-start.30 = (bf16[176,128]{1,0:T(8,128)(2,1)S(1)}, bf16[176,128]{1,0:T(8,128)(2,1)S(1)}, u32[]{:S(2)}, u32[]{:S(2)}) collective-permute-start(bf16[176,128]{1,0:T(8,128)(2,1)S(1)} %constant_dynamic-update-slice_fusion), channel_id=1, source_target_pairs={{0,48},{16,32},{32,16},{48,0},{1,49},{17,33},{33,17},{49,1},{2,50}... | collective-permute-start | bytes 135176 | tf_op jit(solution)/shard_map/ppermute | solution.py:431
  115.2 0.9 collective-permute-start.29
  116.1 0.8 collective-permute-start.28
  116.9 0.9 collective-permute-done.30
  117.8 1.8 %collective-permute-done.29 = bf16[176,128]{1,0:T(8,128)(2,1)S(1)} collective-permute-done((bf16[176,128]{1,0:T(8,128)(2,1)S(1)}, bf16[176,128]{1,0:T(8,128)(2,1)S(1)}, u32[]{:S(2)}, u32[]{:S(2)}) %collective-permute-start.29) | collective-permute-done | bytes 45088 | tf_op jit(solution)/shard_map/ppermute | solution.py:431
  119.7 2.1 %collective-permute-start.33 = (bf16[176,128]{1,0:T(8,128)(2,1)S(1)}, bf16[176,128]{1,0:T(8,128)(2,1)S(1)}, u32[]{:S(2)}, u32[]{:S(2)}) collective-permute-start(bf16[176,128]{1,0:T(8,128)(2,1)S(1)} %add_convert_fusion.p0), channel_id=1, source_target_pairs={{0,192},{64,128},{128,64},{192,0},{1,193},{65,129},{129,65},{193,1... | collective-permute-start | bytes 135176 | tf_op jit(solution)/shard_map/ppermute | solution.py:431
  121.7 0.8 collective-permute-start.32
  123.0 0.9 collective-permute-done.33.p3
  123.9 2.2 %collective-permute-done.32.p2 = bf16[176,128]{1,0:T(8,128)(2,1)S(1)} collective-permute-done((bf16[176,128]{1,0:T(8,128)(2,1)S(1)}, bf16[176,128]{1,0:T(8,128)(2,1)S(1)}, u32[]{:S(2)}, u32[]{:S(2)}) %collective-permute-start.32) | collective-permute-done | bytes 45088 | tf_op jit(solution)/shard_map/ppermute | solution.py:431
  126.8 6.0 %collective-permute-start.34 = (f32[40,128]{1,0:T(8,128)S(1)}, f32[40,128]{1,0:T(8,128)S(1)}, u32[]{:S(2)}, u32[]{:S(2)}) collective-permute-start(f32[40,128]{1,0:T(8,128)S(1)} %get-tuple-element.46), channel_id=1, source_target_pairs={{0,1},{1,0},{2,3},{3,2},{4,5},{5,4},{6,7},{7,6},{8,9},{9,8},{10,11... | collective-permute-start | bytes 61448 | tf_op jit(solution)/shard_map/ppermute | solution.py:427
  132.8 0.8 collective-permute-done.34
  133.7 11.6 %all_to_all.11.refs_0_ = f32[8,40,128]{2,1,0:T(8,128)S(1)} all-to-all(f32[8,40,128]{2,1,0:T(8,128)S(1)} %broadcast_in_dim.2), channel_id=1, replica_groups=mesh['y'=4,'x'=4,'z'=8,'c'=2] {'z'}, dimensions={0} | all-to-all | bytes 327680 | tf_op jit(solution)/shard_map/all_to_all | solution.py:481
  145.3 0.7 shard_map.107
  (78 shorter events, 6.0 us)
Async XLA Ops:
  0.6 54.7 %copy-start.9 = (f32[4,128]{1,0:T(4,128)S(1)}, f32[4,128]{1,0:T(4,128)}, u32[]{:S(2)}) copy-start(f32[4,128]{1,0:T(4,128)} %m_ref.5) | copy-start | bytes 6148
  0.6 26.6 %copy-start.5 = (f32[128,128]{1,0:T(8,128)S(1)}, f32[128,128]{1,0:T(8,128)}, u32[]{:S(2)}) copy-start(f32[128,128]{1,0:T(8,128)} %a_ref.3) | copy-start | bytes 196612
  0.7 53.1 %copy-start.10 = (f32[128,172]{0,1:T(8,128)S(1)}, f32[128,172]{0,1:T(8,128)}, u32[]{:S(2)}) copy-start(f32[128,172]{0,1:T(8,128)} %param.9) | copy-start | bytes 264196
  11.4 5.0 %collective-permute-start.2 = (bf16[144,128]{1,0:T(8,128)(2,1)}, bf16[144,128]{1,0:T(8,128)(2,1)S(1)}, u32[]{:S(2)}, u32[]{:S(2)}) collective-permute-start(bf16[144,128]{1,0:T(8,128)(2,1)} %get-tuple-element.29), channel_id=1, source_target_pairs={{0,48},{16,32},{32,16},{48,0},{1,49},{17,33},{33,17},{49,1},{2,50}... | collective-permute-start | bytes 110600 | tf_op jit(solution)/shard_map/ppermute | solution.py:431
  14.8 4.6 %collective-permute-start.1 = (bf16[144,128]{1,0:T(8,128)(2,1)}, bf16[144,128]{1,0:T(8,128)(2,1)S(1)}, u32[]{:S(2)}, u32[]{:S(2)}) collective-permute-start(bf16[144,128]{1,0:T(8,128)(2,1)} %get-tuple-element.29), channel_id=1, source_target_pairs={{0,32},{16,48},{32,0},{48,16},{1,33},{17,49},{33,1},{49,17},{2,34}... | collective-permute-start | bytes 110600 | tf_op jit(solution)/shard_map/ppermute | solution.py:431
  15.3 4.0 %collective-permute-start = (bf16[144,128]{1,0:T(8,128)(2,1)}, bf16[144,128]{1,0:T(8,128)(2,1)S(1)}, u32[]{:S(2)}, u32[]{:S(2)}) collective-permute-start(bf16[144,128]{1,0:T(8,128)(2,1)} %get-tuple-element.29), channel_id=1, source_target_pairs={{0,16},{16,0},{32,48},{48,32},{1,17},{17,1},{33,49},{49,33},{2,18}... | collective-permute-start | bytes 110600 | tf_op jit(solution)/shard_map/ppermute | solution.py:431
  20.1 4.1 %collective-permute-start.5 = (bf16[144,128]{1,0:T(8,128)(2,1)S(1)}, bf16[144,128]{1,0:T(8,128)(2,1)S(1)}, u32[]{:S(2)}, u32[]{:S(2)}) collective-permute-start(bf16[144,128]{1,0:T(8,128)(2,1)S(1)} %add_convert_fusion.1.a), channel_id=1, source_target_pairs={{0,192},{64,128},{128,64},{192,0},{1,193},{65,129},{129,65},{193,1... | collective-permute-start | bytes 110600 | tf_op jit(solution)/shard_map/ppermute | solution.py:431
  22.9 4.3 %collective-permute-start.4 = (bf16[144,128]{1,0:T(8,128)(2,1)S(1)}, bf16[144,128]{1,0:T(8,128)(2,1)S(1)}, u32[]{:S(2)}, u32[]{:S(2)}) collective-permute-start(bf16[144,128]{1,0:T(8,128)(2,1)S(1)} %add_convert_fusion.1.a), channel_id=1, source_target_pairs={{0,128},{64,192},{128,0},{192,64},{1,129},{65,193},{129,1},{193,65... | collective-permute-start | bytes 110600 | tf_op jit(solution)/shard_map/ppermute | solution.py:431
  23.3 4.0 %collective-permute-start.3 = (bf16[144,128]{1,0:T(8,128)(2,1)S(1)}, bf16[144,128]{1,0:T(8,128)(2,1)S(1)}, u32[]{:S(2)}, u32[]{:S(2)}) collective-permute-start(bf16[144,128]{1,0:T(8,128)(2,1)S(1)} %add_convert_fusion.1.a), channel_id=1, source_target_pairs={{0,64},{64,0},{128,192},{192,128},{1,65},{65,1},{129,193},{193,129... | collective-permute-start | bytes 110600 | tf_op jit(solution)/shard_map/ppermute | solution.py:431
  48.3 7.0 %collective-permute-start.6 = (bf16[8,256,128]{2,1,0:T(8,128)(2,1)S(1)}, bf16[8,256,128]{2,1,0:T(8,128)(2,1)S(1)}, u32[]{:S(2)}, u32[]{:S(2)}) collective-permute-start(bf16[8,256,128]{2,1,0:T(8,128)(2,1)S(1)} %all_to_all.10.ma_ref), channel_id=1, source_target_pairs={{0,1},{1,0},{2,3},{3,2},{4,5},{5,4},{6,7},{7,6},{8,9},{9,8},{10,11... | collective-permute-start | bytes 1572872 | tf_op jit(solution)/shard_map/ppermute | solution.py:427
  55.3 1.6 %copy-start.1 = (bf16[128,8192]{1,0:T(8,128)(2,1)S(1)}, bf16[128,8192]{1,0:T(8,128)(2,1)}, u32[]{:S(2)}) copy-start(bf16[128,8192]{1,0:T(8,128)(2,1)} %get-tuple-element.28.ft_ref) | copy-start | bytes 6291460
  56.9 0.8 copy-start.8
  57.7 47.7 %copy-start.3 = (f32[128,8192]{1,0:T(8,128)S(1)}, f32[128,8192]{1,0:T(8,128)}, u32[]{:S(2)}) copy-start(f32[128,8192]{1,0:T(8,128)} %get-tuple-element.34.e_ref) | copy-start | bytes 12582916
  65.8 28.1 %copy-start.4 = (bf16[128,8192]{1,0:T(8,128)(2,1)S(1)}, bf16[128,8192]{1,0:T(8,128)(2,1)}, u32[]{:S(2)}) copy-start(bf16[128,8192]{1,0:T(8,128)(2,1)} %get-tuple-element.35.lb_ref) | copy-start | bytes 6291460
  65.8 6.3 %collective-permute-start.14 = (bf16[144,512]{1,0:T(8,128)(2,1)S(1)}, bf16[144,512]{1,0:T(8,128)(2,1)S(1)}, u32[]{:S(2)}, u32[]{:S(2)}) collective-permute-start(bf16[144,512]{1,0:T(8,128)(2,1)S(1)} %get-tuple-element.36.refs_0_), channel_id=1, source_target_pairs={{0,2},{2,4},{4,6},{6,8},{8,10},{10,12},{12,14},{14,0},{1,3},{3,5},... | collective-permute-start | bytes 442376 | tf_op jit(solution)/shard_map/ppermute | solution.py:453
  66.1 6.1 %collective-permute-start.8 = (bf16[144,512]{1,0:T(8,128)(2,1)S(1)}, bf16[144,512]{1,0:T(8,128)(2,1)S(1)}, u32[]{:S(2)}, u32[]{:S(2)}) collective-permute-start(bf16[144,512]{1,0:T(8,128)(2,1)S(1)} %get-tuple-element.37), channel_id=1, source_target_pairs={{0,14},{2,0},{4,2},{6,4},{8,6},{10,8},{12,10},{14,12},{1,15},{3,1}... | collective-permute-start | bytes 442376 | tf_op jit(solution)/shard_map/ppermute | solution.py:456
  72.1 5.3 %collective-permute-start.15 = (bf16[144,512]{1,0:T(8,128)(2,1)S(1)}, bf16[144,512]{1,0:T(8,128)(2,1)S(1)}, u32[]{:S(2)}, u32[]{:S(2)}) collective-permute-start(bf16[144,512]{1,0:T(8,128)(2,1)S(1)} %pad_maximum_fusion.2), channel_id=1, source_target_pairs={{0,2},{2,4},{4,6},{6,8},{8,10},{10,12},{12,14},{14,0},{1,3},{3,5},... | collective-permute-start | bytes 442376 | tf_op jit(solution)/shard_map/ppermute | solution.py:453
  77.4 5.1 %collective-permute-start.10 = (bf16[144,512]{1,0:T(8,128)(2,1)S(1)}, bf16[144,512]{1,0:T(8,128)(2,1)S(1)}, u32[]{:S(2)}, u32[]{:S(2)}) collective-permute-start(bf16[144,512]{1,0:T(8,128)(2,1)S(1)} %pad_maximum_fusion), channel_id=1, source_target_pairs={{0,14},{2,0},{4,2},{6,4},{8,6},{10,8},{12,10},{14,12},{1,15},{3,1}... | collective-permute-start | bytes 442376 | tf_op jit(solution)/shard_map/ppermute | solution.py:456
  77.5 5.3 %collective-permute-start.16 = (bf16[144,512]{1,0:T(8,128)(2,1)S(1)}, bf16[144,512]{1,0:T(8,128)(2,1)S(1)}, u32[]{:S(2)}, u32[]{:S(2)}) collective-permute-start(bf16[144,512]{1,0:T(8,128)(2,1)S(1)} %pad_maximum_fusion.3), channel_id=1, source_target_pairs={{0,2},{2,4},{4,6},{6,8},{8,10},{10,12},{12,14},{14,0},{1,3},{3,5},... | collective-permute-start | bytes 442376 | tf_op jit(solution)/shard_map/ppermute | solution.py:453
  79.1 5.4 %collective-permute-start.7 = (bf16[144,512]{1,0:T(8,128)(2,1)S(1)}, bf16[144,512]{1,0:T(8,128)(2,1)S(1)}, u32[]{:S(2)}, u32[]{:S(2)}) collective-permute-start(bf16[144,512]{1,0:T(8,128)(2,1)S(1)} %get-tuple-element.36.refs_0_), channel_id=1, source_target_pairs={{0,1},{1,0},{2,3},{3,2},{4,5},{5,4},{6,7},{7,6},{8,9},{9,8},{10,11... | collective-permute-start | bytes 442376 | tf_op jit(solution)/shard_map/ppermute | solution.py:427
  82.0 6.6 %collective-permute-start.9 = (bf16[144,512]{1,0:T(8,128)(2,1)S(1)}, bf16[144,512]{1,0:T(8,128)(2,1)S(1)}, u32[]{:S(2)}, u32[]{:S(2)}) collective-permute-start(bf16[144,512]{1,0:T(8,128)(2,1)S(1)} %collective-permute-done.8.refs_2_), channel_id=1, source_target_pairs={{0,1},{1,0},{2,3},{3,2},{4,5},{5,4},{6,7},{7,6},{8,9},{9,8},{10,11... | collective-permute-start | bytes 442376 | tf_op jit(solution)/shard_map/ppermute | solution.py:427
  82.0 6.7 %collective-permute-start.21 = (bf16[144,512]{1,0:T(8,128)(2,1)S(1)}, bf16[144,512]{1,0:T(8,128)(2,1)S(1)}, u32[]{:S(2)}, u32[]{:S(2)}) collective-permute-start(bf16[144,512]{1,0:T(8,128)(2,1)S(1)} %collective-permute-done.14.refs_14_), channel_id=1, source_target_pairs={{0,1},{1,0},{2,3},{3,2},{4,5},{5,4},{6,7},{7,6},{8,9},{9,8},{10,11... | collective-permute-start | bytes 442376 | tf_op jit(solution)/shard_map/ppermute | solution.py:427
  82.8 6.2 %collective-permute-start.12 = (bf16[144,512]{1,0:T(8,128)(2,1)S(1)}, bf16[144,512]{1,0:T(8,128)(2,1)S(1)}, u32[]{:S(2)}, u32[]{:S(2)}) collective-permute-start(bf16[144,512]{1,0:T(8,128)(2,1)S(1)} %pad_maximum_fusion.1), channel_id=1, source_target_pairs={{0,14},{2,0},{4,2},{6,4},{8,6},{10,8},{12,10},{14,12},{1,15},{3,1}... | collective-permute-start | bytes 442376 | tf_op jit(solution)/shard_map/ppermute | solution.py:456
  83.6 8.0 %collective-permute-start.17 = (bf16[144,512]{1,0:T(8,128)(2,1)S(1)}, bf16[144,512]{1,0:T(8,128)(2,1)S(1)}, u32[]{:S(2)}, u32[]{:S(2)}) collective-permute-start(bf16[144,512]{1,0:T(8,128)(2,1)S(1)} %pad_maximum_fusion.4), channel_id=1, source_target_pairs={{0,2},{2,4},{4,6},{6,8},{8,10},{10,12},{12,14},{14,0},{1,3},{3,5},... | collective-permute-start | bytes 442376 | tf_op jit(solution)/shard_map/ppermute | solution.py:453
  84.5 8.4 %collective-permute-start.20 = (bf16[144,512]{1,0:T(8,128)(2,1)S(1)}, bf16[144,512]{1,0:T(8,128)(2,1)S(1)}, u32[]{:S(2)}, u32[]{:S(2)}) collective-permute-start(bf16[144,512]{1,0:T(8,128)(2,1)S(1)} %collective-permute-done.15.refs_12_), channel_id=1, source_target_pairs={{0,1},{1,0},{2,3},{3,2},{4,5},{5,4},{6,7},{7,6},{8,9},{9,8},{10,11... | collective-permute-start | bytes 442376 | tf_op jit(solution)/shard_map/ppermute | solution.py:427
  88.6 4.3 %collective-permute-start.19 = (bf16[144,512]{1,0:T(8,128)(2,1)S(1)}, bf16[144,512]{1,0:T(8,128)(2,1)S(1)}, u32[]{:S(2)}, u32[]{:S(2)}) collective-permute-start(bf16[144,512]{1,0:T(8,128)(2,1)S(1)} %collective-permute-done.16.refs_10_), channel_id=1, source_target_pairs={{0,1},{1,0},{2,3},{3,2},{4,5},{5,4},{6,7},{7,6},{8,9},{9,8},{10,11... | collective-permute-start | bytes 442376 | tf_op jit(solution)/shard_map/ppermute | solution.py:427
  88.7 4.3 %collective-permute-start.11 = (bf16[144,512]{1,0:T(8,128)(2,1)S(1)}, bf16[144,512]{1,0:T(8,128)(2,1)S(1)}, u32[]{:S(2)}, u32[]{:S(2)}) collective-permute-start(bf16[144,512]{1,0:T(8,128)(2,1)S(1)} %collective-permute-done.10.refs_4_), channel_id=1, source_target_pairs={{0,1},{1,0},{2,3},{3,2},{4,5},{5,4},{6,7},{7,6},{8,9},{9,8},{10,11... | collective-permute-start | bytes 442376 | tf_op jit(solution)/shard_map/ppermute | solution.py:427
  89.1 3.8 %collective-permute-start.13 = (bf16[144,512]{1,0:T(8,128)(2,1)S(1)}, bf16[144,512]{1,0:T(8,128)(2,1)S(1)}, u32[]{:S(2)}, u32[]{:S(2)}) collective-permute-start(bf16[144,512]{1,0:T(8,128)(2,1)S(1)} %collective-permute-done.12.refs_6_), channel_id=1, source_target_pairs={{0,1},{1,0},{2,3},{3,2},{4,5},{5,4},{6,7},{7,6},{8,9},{9,8},{10,11... | collective-permute-start | bytes 442376 | tf_op jit(solution)/shard_map/ppermute | solution.py:427
  91.6 2.3 %collective-permute-start.18 = (bf16[144,512]{1,0:T(8,128)(2,1)S(1)}, bf16[144,512]{1,0:T(8,128)(2,1)S(1)}, u32[]{:S(2)}, u32[]{:S(2)}) collective-permute-start(bf16[144,512]{1,0:T(8,128)(2,1)S(1)} %collective-permute-done.17.refs_8_), channel_id=1, source_target_pairs={{0,1},{1,0},{2,3},{3,2},{4,5},{5,4},{6,7},{7,6},{8,9},{9,8},{10,11... | collective-permute-start | bytes 442376 | tf_op jit(solution)/shard_map/ppermute | solution.py:427
  93.9 11.5 %copy-start = (bf16[8192,128]{1,0:T(8,128)(2,1)S(1)}, bf16[8192,128]{1,0:T(8,128)(2,1)}, u32[]{:S(2)}) copy-start(bf16[8192,128]{1,0:T(8,128)(2,1)} %f_ref.3) | copy-start | bytes 6291460
  93.9 11.5 %copy-start.2 = (bf16[128,8192]{1,0:T(8,128)(2,1)S(1)}, bf16[128,8192]{1,0:T(8,128)(2,1)}, u32[]{:S(2)}) copy-start(bf16[128,8192]{1,0:T(8,128)(2,1)} %get-tuple-element.28.ft_ref) | copy-start | bytes 6291460
  93.9 11.5 %copy-start.6 = (f32[8,8192]{1,0:T(8,128)S(1)}, f32[8,8192]{1,0:T(8,128)}, u32[]{:S(2)}) copy-start(f32[8,8192]{1,0:T(8,128)} %get-tuple-element.33.r_ref) | copy-start | bytes 786436
  93.9 11.5 %copy-start.7 = (bf16[512,128]{1,0:T(8,128)(2,1)S(1)}, bf16[512,128]{1,0:T(8,128)(2,1)}, u32[]{:S(2)}) copy-start(bf16[512,128]{1,0:T(8,128)(2,1)} %get-tuple-element.40.am_ref) | copy-start | bytes 393220
  94.8 4.1 %collective-permute-start.24 = (bf16[128,128]{1,0:T(8,128)(2,1)S(1)}, bf16[128,128]{1,0:T(8,128)(2,1)S(1)}, u32[]{:S(2)}, u32[]{:S(2)}) collective-permute-start(bf16[128,128]{1,0:T(8,128)(2,1)S(1)} %get-tuple-element.45), channel_id=1, source_target_pairs={{0,48},{16,32},{32,16},{48,0},{1,49},{17,33},{33,17},{49,1},{2,50}... | collective-permute-start | bytes 98312 | tf_op jit(solution)/shard_map/ppermute | solution.py:431
  96.0 4.3 %collective-permute-start.23 = (bf16[128,128]{1,0:T(8,128)(2,1)S(1)}, bf16[128,128]{1,0:T(8,128)(2,1)S(1)}, u32[]{:S(2)}, u32[]{:S(2)}) collective-permute-start(bf16[128,128]{1,0:T(8,128)(2,1)S(1)} %get-tuple-element.45), channel_id=1, source_target_pairs={{0,32},{16,48},{32,0},{48,16},{1,33},{17,49},{33,1},{49,17},{2,34}... | collective-permute-start | bytes 98312 | tf_op jit(solution)/shard_map/ppermute | solution.py:431
  96.6 3.7 %collective-permute-start.22 = (bf16[128,128]{1,0:T(8,128)(2,1)S(1)}, bf16[128,128]{1,0:T(8,128)(2,1)S(1)}, u32[]{:S(2)}, u32[]{:S(2)}) collective-permute-start(bf16[128,128]{1,0:T(8,128)(2,1)S(1)} %get-tuple-element.45), channel_id=1, source_target_pairs={{0,16},{16,0},{32,48},{48,32},{1,17},{17,1},{33,49},{49,33},{2,18}... | collective-permute-start | bytes 98312 | tf_op jit(solution)/shard_map/ppermute | solution.py:431
  100.3 4.1 %collective-permute-start.27 = (bf16[128,128]{1,0:T(8,128)(2,1)S(1)}, bf16[128,128]{1,0:T(8,128)(2,1)S(1)}, u32[]{:S(2)}, u32[]{:S(2)}) collective-permute-start(bf16[128,128]{1,0:T(8,128)(2,1)S(1)} %add_convert_fusion.2.p0), channel_id=1, source_target_pairs={{0,192},{64,128},{128,64},{192,0},{1,193},{65,129},{129,65},{193,1... | collective-permute-start | bytes 98312 | tf_op jit(solution)/shard_map/ppermute | solution.py:431
  101.1 4.3 %collective-permute-start.26 = (bf16[128,128]{1,0:T(8,128)(2,1)S(1)}, bf16[128,128]{1,0:T(8,128)(2,1)S(1)}, u32[]{:S(2)}, u32[]{:S(2)}) collective-permute-start(bf16[128,128]{1,0:T(8,128)(2,1)S(1)} %add_convert_fusion.2.p0), channel_id=1, source_target_pairs={{0,128},{64,192},{128,0},{192,64},{1,129},{65,193},{129,1},{193,65... | collective-permute-start | bytes 98312 | tf_op jit(solution)/shard_map/ppermute | solution.py:431
  102.1 3.3 %collective-permute-start.25 = (bf16[128,128]{1,0:T(8,128)(2,1)S(1)}, bf16[128,128]{1,0:T(8,128)(2,1)S(1)}, u32[]{:S(2)}, u32[]{:S(2)}) collective-permute-start(bf16[128,128]{1,0:T(8,128)(2,1)S(1)} %add_convert_fusion.2.p0), channel_id=1, source_target_pairs={{0,64},{64,0},{128,192},{192,128},{1,65},{65,1},{129,193},{193,129... | collective-permute-start | bytes 98312 | tf_op jit(solution)/shard_map/ppermute | solution.py:431
  113.6 4.2 %collective-permute-start.30 = (bf16[176,128]{1,0:T(8,128)(2,1)S(1)}, bf16[176,128]{1,0:T(8,128)(2,1)S(1)}, u32[]{:S(2)}, u32[]{:S(2)}) collective-permute-start(bf16[176,128]{1,0:T(8,128)(2,1)S(1)} %constant_dynamic-update-slice_fusion), channel_id=1, source_target_pairs={{0,48},{16,32},{32,16},{48,0},{1,49},{17,33},{33,17},{49,1},{2,50}... | collective-permute-start | bytes 135176 | tf_op jit(solution)/shard_map/ppermute | solution.py:431
  115.2 4.4 %collective-permute-start.29 = (bf16[176,128]{1,0:T(8,128)(2,1)S(1)}, bf16[176,128]{1,0:T(8,128)(2,1)S(1)}, u32[]{:S(2)}, u32[]{:S(2)}) collective-permute-start(bf16[176,128]{1,0:T(8,128)(2,1)S(1)} %constant_dynamic-update-slice_fusion), channel_id=1, source_target_pairs={{0,32},{16,48},{32,0},{48,16},{1,33},{17,49},{33,1},{49,17},{2,34}... | collective-permute-start | bytes 135176 | tf_op jit(solution)/shard_map/ppermute | solution.py:431
  116.1 3.5 %collective-permute-start.28 = (bf16[176,128]{1,0:T(8,128)(2,1)S(1)}, bf16[176,128]{1,0:T(8,128)(2,1)S(1)}, u32[]{:S(2)}, u32[]{:S(2)}) collective-permute-start(bf16[176,128]{1,0:T(8,128)(2,1)S(1)} %constant_dynamic-update-slice_fusion), channel_id=1, source_target_pairs={{0,16},{16,0},{32,48},{48,32},{1,17},{17,1},{33,49},{49,33},{2,18}... | collective-permute-start | bytes 135176 | tf_op jit(solution)/shard_map/ppermute | solution.py:431
  119.7 4.2 %collective-permute-start.33 = (bf16[176,128]{1,0:T(8,128)(2,1)S(1)}, bf16[176,128]{1,0:T(8,128)(2,1)S(1)}, u32[]{:S(2)}, u32[]{:S(2)}) collective-permute-start(bf16[176,128]{1,0:T(8,128)(2,1)S(1)} %add_convert_fusion.p0), channel_id=1, source_target_pairs={{0,192},{64,128},{128,64},{192,0},{1,193},{65,129},{129,65},{193,1... | collective-permute-start | bytes 135176 | tf_op jit(solution)/shard_map/ppermute | solution.py:431
  121.7 4.4 %collective-permute-start.32 = (bf16[176,128]{1,0:T(8,128)(2,1)S(1)}, bf16[176,128]{1,0:T(8,128)(2,1)S(1)}, u32[]{:S(2)}, u32[]{:S(2)}) collective-permute-start(bf16[176,128]{1,0:T(8,128)(2,1)S(1)} %add_convert_fusion.p0), channel_id=1, source_target_pairs={{0,128},{64,192},{128,0},{192,64},{1,129},{65,193},{129,1},{193,65... | collective-permute-start | bytes 135176 | tf_op jit(solution)/shard_map/ppermute | solution.py:431
  122.6 3.6 %collective-permute-start.31 = (bf16[176,128]{1,0:T(8,128)(2,1)S(1)}, bf16[176,128]{1,0:T(8,128)(2,1)S(1)}, u32[]{:S(2)}, u32[]{:S(2)}) collective-permute-start(bf16[176,128]{1,0:T(8,128)(2,1)S(1)} %add_convert_fusion.p0), channel_id=1, source_target_pairs={{0,64},{64,0},{128,192},{192,128},{1,65},{65,1},{129,193},{193,129... | collective-permute-start | bytes 135176 | tf_op jit(solution)/shard_map/ppermute | solution.py:431
  126.8 6.9 %collective-permute-start.34 = (f32[40,128]{1,0:T(8,128)S(1)}, f32[40,128]{1,0:T(8,128)S(1)}, u32[]{:S(2)}, u32[]{:S(2)}) collective-permute-start(f32[40,128]{1,0:T(8,128)S(1)} %get-tuple-element.46), channel_id=1, source_target_pairs={{0,1},{1,0},{2,3},{3,2},{4,5},{5,4},{6,7},{7,6},{8,9},{9,8},{10,11... | collective-permute-start | bytes 61448 | tf_op jit(solution)/shard_map/ppermute | solution.py:427

commit v4 on v3

--- a/solution.py
+++ b/solution.py
@@ -69,7 +69,7 @@
     return jnp.concatenate([x] * (width // x.shape[1]), axis=1)
 
 
-LINK_BLOCK = 1024
+LINK_BLOCK = 2048
 CHUNK = 256
 
 
@@ -87,7 +87,6 @@
         tot[...] = jnp.zeros_like(tot)
         raw[...] = jnp.zeros_like(raw)
 
-    tag_ref[...] = jnp.where(mask_ref[...] > 0, lab_ref[...], -1)
     for j in range(LINK_BLOCK // CHUNK):
         cols = slice(j * CHUNK, (j + 1) * CHUNK)
         ft = f_ref[cols, :].astype(f32).T
@@ -96,10 +95,11 @@
         rinv_ref[:, cols] = rinv
         e = jnp.maximum(mm(ad[...], dirs, NN) - threshold, 0.0)
         link = e * e
-        e_ref[:, cols] = e
+        e_ref[:, cols] = e.astype(bf16)
         lb_ref[:, cols] = link.astype(bf16)
         raw[...] += sum(link[:, k * F : (k + 1) * F] for k in range(CHUNK // F))
     tot[...] += mm(lb_ref[...], f_ref[...], NN)
+    tag_ref[...] = jnp.where(mask_ref[...] > 0, lab_ref[...], -1)
 
     @pl.when(i == pl.num_programs(0) - 1)
     def _():
@@ -134,7 +134,7 @@
         out_shape=[
             jax.ShapeDtypeStruct((F, n), bf16),
             jax.ShapeDtypeStruct((8, n), f32),
-            jax.ShapeDtypeStruct((APD, n), f32),
+            jax.ShapeDtypeStruct((APD, n), bf16),
             jax.ShapeDtypeStruct((APD, n), bf16),
             jax.ShapeDtypeStruct((1, n), jnp.int32),
             jax.ShapeDtypeStruct((HEADS * APD, F), bf16),
@@ -183,21 +183,25 @@
     )(*parts, anchors)
 
 
+HEAD_STEP = 2
+
+
 def head_kernel(s_ref, m_ref, ft_ref, ma_ref, mb_ref, cls_ref, tag_ref, emb_ref, up_ref, down_ref, part_ref, loss_ref):
     metric = m_ref[...]
     dirs, _ = node_dirs(ft_ref[...].astype(f32), lambda h, width: wide_column(column(metric[h : h + 1, :]), width))
 
-    def step(z, carry):
+    def step(i, carry):
         field, raw = carry
-        for ref in (ma_ref, mb_ref):
-            ad = anchor_dirs(ref[z, APD:, :].astype(f32), metric)
-            e = jnp.maximum(mm(ad, dirs, NN) - threshold, 0.0)
-            link = e * e
-            field = field + mm(ref[z, 0:APD, :], link.astype(bf16), TN)
-            raw = raw + sum(link[8 * k : 8 * k + 8, :] for k in range(APD // 8))
+        blocks = [ref[HEAD_STEP * i + k] for k in range(HEAD_STEP) for ref in (ma_ref, mb_ref)]
+        ad = jnp.concatenate([anchor_dirs(b[APD:, :].astype(f32), metric) for b in blocks], axis=0)
+        means = jnp.concatenate([b[0:APD, :] for b in blocks], axis=0)
+        e = jnp.maximum(mm(ad, dirs, NN) - threshold, 0.0)
+        link = e * e
+        field = field + mm(means, link.astype(bf16), TN)
+        raw = raw + sum(link[8 * k : 8 * k + 8, :] for k in range(link.shape[0] // 8))
         return field, raw
 
-    field, raw = lax.fori_loop(0, NZ, step, (jnp.zeros((F, OWN), f32), jnp.zeros((8, OWN), f32)))
+    field, raw = lax.fori_loop(0, NZ // HEAD_STEP, step, (jnp.zeros((F, OWN), f32), jnp.zeros((8, OWN), f32)))
     inv_degree = 1.0 / (jnp.sum(raw, axis=0, keepdims=True) + degree_floor)
     field = field * inv_degree
     emb_ref[...] = field.T.astype(bf16)
@@ -222,31 +226,11 @@
         ref[F : F + 16, :] = jnp.concatenate([degree_grads, jnp.zeros((7, OWN), f32), part_ref[k]], axis=0).astype(bf16)
 
 
-def head_call(shard, metric, ft, means_a, means_b, cls_t, tags):
-    zero2 = lambda i, s: (0, 0)
-    zero3 = lambda i, s: (0, 0, 0)
-    own = lambda i, s: (0, s[0])
+def head_call(shard, *operands):
     return pl.pallas_call(
         head_kernel,
-        grid_spec=pltpu.PrefetchScalarGridSpec(
-            num_scalar_prefetch=1,
-            grid=(1,),
-            in_specs=[
-                pl.BlockSpec((HEADS, F), zero2),
-                pl.BlockSpec((F, OWN), own),
-                pl.BlockSpec((NZ, 2 * APD, F), zero3),
-                pl.BlockSpec((NZ, 2 * APD, F), zero3),
-                pl.BlockSpec((CPAD, F), zero2),
-                pl.BlockSpec((1, OWN), own),
-            ],
-            out_specs=[
-                pl.BlockSpec((OWN, F), zero2),
-                pl.BlockSpec((F + 16, OWN), zero2),
-                pl.BlockSpec((F + 16, OWN), zero2),
-                pl.BlockSpec((NZ, 8, OWN), zero3),
-                pl.BlockSpec((8, F), zero2),
-            ],
-        ),
+        in_specs=[pl.BlockSpec(memory_space=pltpu.SMEM)] + [vspec()] * len(operands),
+        out_specs=[vspec()] * 5,
         out_shape=[
             jax.ShapeDtypeStruct((OWN, F), bf16),
             jax.ShapeDtypeStruct((F + 16, OWN), bf16),
@@ -255,7 +239,7 @@
             jax.ShapeDtypeStruct((8, F), f32),
         ],
         compiler_params=params(),
-    )(shard, metric, ft, means_a, means_b, cls_t, tags)
+    )(shard, *operands)
 
 
 def mean_grad_kernel(s_ref, lb_ref, *refs):
@@ -302,13 +286,13 @@
         vacc[...] = jnp.zeros_like(vacc)
 
     rows = []
-    for j in range(SCORE_BLOCK // CHUNK):
-        cols = slice(j * CHUNK, (j + 1) * CHUNK)
+    for j in range(SCORE_BLOCK // SCORE_CHUNK):
+        cols = slice(j * SCORE_CHUNK, (j + 1) * SCORE_CHUNK)
         ft = ft_ref[:, cols]
         rinv = r_ref[:, cols]
         dg = g_ref[F : F + 16, cols].astype(f32)[0:1, :] * (2.0 / HEADS)
         link_grads = mm(lhs[...], jnp.concatenate([g_ref[0:F, cols], ft], axis=0), NN)
-        sg = (link_grads + dg + wide_column(adg[...], CHUNK)) * e_ref[:, cols]
+        sg = (link_grads + dg + wide_column(adg[...], SCORE_CHUNK)) * e_ref[:, cols].astype(f32)
         ws = []
         for h in range(HEADS):
             r = rinv[h : h + 1, :]
@@ -351,7 +335,8 @@
         msg_ref[APD : APD + 16, :] = jnp.concatenate(rows, axis=0).astype(bf16)
 
 
-SCORE_BLOCK = 1024
+SCORE_BLOCK = 2048
+SCORE_CHUNK = 256
 
 
 def score_call(features, ft, rinv, excess, grads, am, anchors, metric, means, total, degree, loss, parts):
@@ -373,7 +358,7 @@
             pltpu.VMEM((APD, F), f32),
             pltpu.VMEM((HEADS * APD, SCORE_BLOCK), bf16),
         ],
-        compiler_params=params(),
+        compiler_params=params(24),
     )(features, ft, rinv, excess, grads, am, anchors, metric, means, total, degree, loss, *parts)
 
 
@@ -470,7 +455,9 @@
     total, degree, means, msg = mean_call(over_dp(msg), anchors)
     means_a = lax.all_to_all(msg, "z", 0, 0, tiled=True)
     means_b = swap(means_a)
-    embedding, up, down, part, loss = head_call(shard, metric, ft, means_a, means_b, cls_t, tags)
+    own_ft = lax.dynamic_slice_in_dim(ft, shard[0] * OWN, OWN, 1)
+    own_tags = lax.dynamic_slice_in_dim(tags, shard[0] * OWN, OWN, 1)
+    embedding, up, down, part, loss = head_call(shard, metric, own_ft, means_a, means_b, cls_t, own_tags)
     blocks, cls = ring(up, down, part)
     blocks = [b for block in blocks for b in (block, swap(block))]
     msg, grads = mean_grad_call(shard, lb, blocks)

time: 146 us -> 139 us (0.952)
  Pallas kernels: 29.2 us -> 23.9 us
    pallas_call x1, Pallas kernels: 8.09 us -> 5.12 us  [head_call(): pl.pallas_call(head_kernel, in_specs=[pl.BlockSpec(memory_space=pltpu.SME...]
    unnamed x26 -> x22, local copies, waits for them, and re-layouts: 2.42 us -> 0.07 us
    pallas_call x1, Pallas kernels: 10.7 us -> 9.08 us  [link_call(): pl.pallas_call(link_kernel, grid=(n // LINK_BLOCK,), in_specs=[pl.BlockSp...]
    dynamic_slice x0 -> x2, local copies, waits for them, and re-layouts: none -> 1.6 us  [the longest x1 0.91 us: body(): own_ft = lax.dynamic_slice_in_dim(ft, shard[0] * OWN, OWN, 1)]
    ppermute x10, waiting for transfers between devices: 3.37 us -> 1.85 us  [swap(): return lax.ppermute(x, 'c', [(0, 1), (1, 0)])]
  transfers between devices with their start and end apart: 35 -> 35, of which waited for: 18 -> 17; matrix products, arithmetic and copies ran while one was open for 0% -> 1% of each run, Pallas kernels for 0% -> 0%
where the time goes in v4:
time: 139 us
  starting transfers between devices  50.3 us (36%)
  blocking collectives  32.4 us (23%)
  waiting for transfers between devices  28.4 us (20%)
  Pallas kernels  23.9 us (17%)
  local copies, waits for them, and re-layouts  1.76 us (1%)
    ppermute x10, starting transfers between devices, swap(): return lax.ppermute(x, 'c', [(0, 1), (1, 0)])  23.2 us
    ppermute x18, starting transfers between devices, shared(): lax.ppermute(x, axis, [(i, i ^ k) for i in range(4)])  21.1 us
    all_to_all x1, blocking collectives, body(): means_a = lax.all_to_all(msg, 'z', 0, 0, tiled=True)  21 us
    ppermute x18, waiting for transfers between devices, shared(): lax.ppermute(x, axis, [(i, i ^ k) for i in range(4)])  17.2 us
    all_to_all x1, blocking collectives, body(): lax.all_to_all(jnp.broadcast_to(small[None], (NZ,) + small.shape), 'z', 0...  11.4 us
    ppermute x4, waiting for transfers between devices, ring(): up = lax.ppermute(up, 'z', ups)  9.3 us
    pallas_call x1, Pallas kernels, link_call(): pl.pallas_call(link_kernel, grid=(n // LINK_BLOCK,), in_specs=[pl.BlockSp...  9.08 us
    pallas_call x1, Pallas kernels, score_call(): pl.pallas_call(score_kernel, grid=(n // SCORE_BLOCK,), in_specs=[pl.Block...  7.39 us
  transfers between devices with their start and end apart: 35, of which 17 were waited for; matrix products, arithmetic and copies ran while one was open for 1% of the time, Pallas kernels for 0%

profile of v4, /device:TPU:1, one launch (start us, length us, event | category | flops | bytes accessed | tf_op | source)
XLA Modules:
  0.0 138.5 jit_solution(12703541323701327373)
XLA Ops:
  0.7 9.1 %shard_map.101 = (bf16[128,8192]{1,0:T(8,128)(2,1)}, f32[8,8192]{1,0:T(8,128)}, bf16[128,8192]{1,0:T(8,128)(2,1)}, bf16[128,8192]{1,0:T(8,128)(2,1)}, s32[1,8192...) custom-call(bf16[8192,128]{1,0:T(8,128)(2,1)} %f_ref.3, f32[128,128]{1,0:T(8,128)} %a_ref.3, ...), custom_call_target="tpu_custom_call" | custom-call | tf_op jit(solution)/shard_map/pallas_call | solution.py:115
  9.7 3.4 %collective-permute-start.2 = (bf16[144,128]{1,0:T(8,128)(2,1)}, bf16[144,128]{1,0:T(8,128)(2,1)S(1)}, u32[]{:S(2)}, u32[]{:S(2)}) collective-permute-start(bf16[144,128]{1,0:T(8,128)(2,1)} %get-tuple-element.29), channel_id=1, source_target_pairs={{0,48},{16,32},{32,16},{48,0},{1,49},{17,33},{33,17},{49,1},{2,50}... | collective-permute-start | bytes 110600 | tf_op jit(solution)/shard_map/ppermute | solution.py:416
  13.8 0.9 collective-permute-done.2
  14.7 3.0 %collective-permute-done.1 = bf16[144,128]{1,0:T(8,128)(2,1)S(1)} collective-permute-done((bf16[144,128]{1,0:T(8,128)(2,1)}, bf16[144,128]{1,0:T(8,128)(2,1)S(1)}, u32[]{:S(2)}, u32[]{:S(2)}) %collective-permute-start.1) | collective-permute-done | bytes 36896 | tf_op jit(solution)/shard_map/ppermute | solution.py:416
  17.7 0.8 add_convert_fusion.1.a
  18.5 2.8 %collective-permute-start.5 = (bf16[144,128]{1,0:T(8,128)(2,1)S(1)}, bf16[144,128]{1,0:T(8,128)(2,1)S(1)}, u32[]{:S(2)}, u32[]{:S(2)}) collective-permute-start(bf16[144,128]{1,0:T(8,128)(2,1)S(1)} %add_convert_fusion.1.a), channel_id=1, source_target_pairs={{0,192},{64,128},{128,64},{192,0},{1,193},{65,129},{129,65},{193,1... | collective-permute-start | bytes 110600 | tf_op jit(solution)/shard_map/ppermute | solution.py:416
  22.0 0.7 collective-permute-done.5.d
  22.6 3.0 %collective-permute-done.4.c = bf16[144,128]{1,0:T(8,128)(2,1)S(1)} collective-permute-done((bf16[144,128]{1,0:T(8,128)(2,1)S(1)}, bf16[144,128]{1,0:T(8,128)(2,1)S(1)}, u32[]{:S(2)}, u32[]{:S(2)}) %collective-permute-start.4) | collective-permute-done | bytes 36896 | tf_op jit(solution)/shard_map/ppermute | solution.py:416
  25.7 21.0 %all_to_all.10.ma_ref = bf16[8,256,128]{2,1,0:T(8,128)(2,1)S(1)} all-to-all(bf16[8,256,128]{2,1,0:T(8,128)(2,1)S(1)} %get-tuple-element.30), channel_id=1, replica_groups=mesh['y'=4,'x'=4,'z'=8,'c'=2] {'z'}, dimensions={0} | all-to-all | bytes 1048576 | tf_op jit(solution)/shard_map/all_to_all | solution.py:456
  46.7 5.5 %collective-permute-start.6 = (bf16[8,256,128]{2,1,0:T(8,128)(2,1)S(1)}, bf16[8,256,128]{2,1,0:T(8,128)(2,1)S(1)}, u32[]{:S(2)}, u32[]{:S(2)}) collective-permute-start(bf16[8,256,128]{2,1,0:T(8,128)(2,1)S(1)} %all_to_all.10.ma_ref), channel_id=1, source_target_pairs={{0,1},{1,0},{2,3},{3,2},{4,5},{5,4},{6,7},{7,6},{8,9},{9,8},{10,11... | collective-permute-start | bytes 1572872 | tf_op jit(solution)/shard_map/ppermute | solution.py:412
  52.2 0.7 constant_dynamic-slice_fusion.tag_ref
  52.9 0.9 constant_dynamic-slice_fusion.1.ft_ref
  53.8 5.1 %shard_map.103 = (bf16[512,128]{1,0:T(8,128)(2,1)}, bf16[144,512]{1,0:T(8,128)(2,1)S(1)}, bf16[144,512]{1,0:T(8,128)(2,1)S(1)}, f32[8,8,512]{2,1,0:T(8,128)S(1)}, f32[8,128]{1,0:T(8,128)S(1)}) custom-call(s32[1]{0:T(128)} %bitcast.s_ref, f32[4,128]{1,0:T(4,128)S(1)} %copy-done.7, bf16[128,512]{1,0:T(8,128)(2,1)S(1)} %constant_dynamic-slice_fusion.1.ft_ref, ...), custom_call_target="tpu_custom_call" | custom-call | tf_op jit(solution)/shard_map/pallas_call | solution.py:230
  59.2 2.4 %collective-permute-start.8 = (bf16[144,512]{1,0:T(8,128)(2,1)S(1)}, bf16[144,512]{1,0:T(8,128)(2,1)S(1)}, u32[]{:S(2)}, u32[]{:S(2)}) collective-permute-start(bf16[144,512]{1,0:T(8,128)(2,1)S(1)} %get-tuple-element.37), channel_id=1, source_target_pairs={{0,14},{2,0},{4,2},{6,4},{8,6},{10,8},{12,10},{14,12},{1,15},{3,1}... | collective-permute-start | bytes 442376 | tf_op jit(solution)/shard_map/ppermute | solution.py:441
  61.6 3.7 %collective-permute-done.14.refs_14_ = bf16[144,512]{1,0:T(8,128)(2,1)S(1)} collective-permute-done((bf16[144,512]{1,0:T(8,128)(2,1)S(1)}, bf16[144,512]{1,0:T(8,128)(2,1)S(1)}, u32[]{:S(2)}, u32[]{:S(2)}) %collective-permute-start.14) | collective-permute-done | bytes 147488 | tf_op jit(solution)/shard_map/ppermute | solution.py:438
  65.5 5.2 %collective-permute-done.15.refs_12_ = bf16[144,512]{1,0:T(8,128)(2,1)S(1)} collective-permute-done((bf16[144,512]{1,0:T(8,128)(2,1)S(1)}, bf16[144,512]{1,0:T(8,128)(2,1)S(1)}, u32[]{:S(2)}, u32[]{:S(2)}) %collective-permute-start.15) | collective-permute-done | bytes 147488 | tf_op jit(solution)/shard_map/ppermute | solution.py:438
  70.9 1.5 %collective-permute-start.16 = (bf16[144,512]{1,0:T(8,128)(2,1)S(1)}, bf16[144,512]{1,0:T(8,128)(2,1)S(1)}, u32[]{:S(2)}, u32[]{:S(2)}) collective-permute-start(bf16[144,512]{1,0:T(8,128)(2,1)S(1)} %pad_maximum_fusion.3), channel_id=1, source_target_pairs={{0,2},{2,4},{4,6},{6,8},{8,10},{10,12},{12,14},{14,0},{1,3},{3,5},... | collective-permute-start | bytes 442376 | tf_op jit(solution)/shard_map/ppermute | solution.py:438
  72.4 2.8 %collective-permute-start.7 = (bf16[144,512]{1,0:T(8,128)(2,1)S(1)}, bf16[144,512]{1,0:T(8,128)(2,1)S(1)}, u32[]{:S(2)}, u32[]{:S(2)}) collective-permute-start(bf16[144,512]{1,0:T(8,128)(2,1)S(1)} %get-tuple-element.36.refs_0_), channel_id=1, source_target_pairs={{0,1},{1,0},{2,3},{3,2},{4,5},{5,4},{6,7},{7,6},{8,9},{9,8},{10,11... | collective-permute-start | bytes 442376 | tf_op jit(solution)/shard_map/ppermute | solution.py:412
  76.2 0.7 collective-permute-start.12
  76.8 1.0 collective-permute-start.17
  77.8 4.0 %collective-permute-start.20 = (bf16[144,512]{1,0:T(8,128)(2,1)S(1)}, bf16[144,512]{1,0:T(8,128)(2,1)S(1)}, u32[]{:S(2)}, u32[]{:S(2)}) collective-permute-start(bf16[144,512]{1,0:T(8,128)(2,1)S(1)} %collective-permute-done.15.refs_12_), channel_id=1, source_target_pairs={{0,1},{1,0},{2,3},{3,2},{4,5},{5,4},{6,7},{7,6},{8,9},{9,8},{10,11... | collective-permute-start | bytes 442376 | tf_op jit(solution)/shard_map/ppermute | solution.py:412
  82.3 2.5 %collective-permute-start.13 = (bf16[144,512]{1,0:T(8,128)(2,1)S(1)}, bf16[144,512]{1,0:T(8,128)(2,1)S(1)}, u32[]{:S(2)}, u32[]{:S(2)}) collective-permute-start(bf16[144,512]{1,0:T(8,128)(2,1)S(1)} %collective-permute-done.12.refs_6_), channel_id=1, source_target_pairs={{0,1},{1,0},{2,3},{3,2},{4,5},{5,4},{6,7},{7,6},{8,9},{9,8},{10,11... | collective-permute-start | bytes 442376 | tf_op jit(solution)/shard_map/ppermute | solution.py:412
  84.8 1.3 collective-permute-start.18
  86.2 1.0 collective-permute-done.18.refs_9_
  87.2 0.8 shard_map.104
  88.0 1.2 collective-permute-start.24
  89.8 1.5 %collective-permute-start.22 = (bf16[128,128]{1,0:T(8,128)(2,1)S(1)}, bf16[128,128]{1,0:T(8,128)(2,1)S(1)}, u32[]{:S(2)}, u32[]{:S(2)}) collective-permute-start(bf16[128,128]{1,0:T(8,128)(2,1)S(1)} %get-tuple-element.45), channel_id=1, source_target_pairs={{0,16},{16,0},{32,48},{48,32},{1,17},{17,1},{33,49},{49,33},{2,18}... | collective-permute-start | bytes 98312 | tf_op jit(solution)/shard_map/ppermute | solution.py:416
  91.3 0.7 collective-permute-done.24
  92.0 1.4 %collective-permute-done.23 = bf16[128,128]{1,0:T(8,128)(2,1)S(1)} collective-permute-done((bf16[128,128]{1,0:T(8,128)(2,1)S(1)}, bf16[128,128]{1,0:T(8,128)(2,1)S(1)}, u32[]{:S(2)}, u32[]{:S(2)}) %collective-permute-start.23) | collective-permute-done | bytes 32800 | tf_op jit(solution)/shard_map/ppermute | solution.py:416
  93.5 0.8 collective-permute-start.27
  94.3 1.0 collective-permute-start.26
  95.3 1.5 %collective-permute-start.25 = (bf16[128,128]{1,0:T(8,128)(2,1)S(1)}, bf16[128,128]{1,0:T(8,128)(2,1)S(1)}, u32[]{:S(2)}, u32[]{:S(2)}) collective-permute-start(bf16[128,128]{1,0:T(8,128)(2,1)S(1)} %add_convert_fusion.2.p0), channel_id=1, source_target_pairs={{0,64},{64,0},{128,192},{192,128},{1,65},{65,1},{129,193},{193,129... | collective-permute-start | bytes 98312 | tf_op jit(solution)/shard_map/ppermute | solution.py:416
  96.8 0.7 collective-permute-done.27.p3
  97.5 1.0 collective-permute-done.26.p2
  98.6 7.4 %shard_map.105 = bf16[144,128]{1,0:T(8,128)(2,1)S(1)} custom-call(bf16[8192,128]{1,0:T(8,128)(2,1)S(1)} %copy-done, bf16[128,8192]{1,0:T(8,128)(2,1)S(1)} %copy-done.1, f32[8,8192]{1,0:T(8,128)S(1)} %copy-done.5, bf16[128,8192]{1,0:T(8,128)(2,1)S(1)} %copy-done.3, bf16[144,8192]{1,0:T(8,128)(2,1)S(1)} %get-tuple-element.39.g_ref, ...), custom_call_target="tpu_custom_call" | custom-call | tf_op jit(solution)/shard_map/pallas_call | solution.py:347
  106.1 1.9 %collective-permute-start.30 = (bf16[176,128]{1,0:T(8,128)(2,1)S(1)}, bf16[176,128]{1,0:T(8,128)(2,1)S(1)}, u32[]{:S(2)}, u32[]{:S(2)}) collective-permute-start(bf16[176,128]{1,0:T(8,128)(2,1)S(1)} %constant_dynamic-update-slice_fusion), channel_id=1, source_target_pairs={{0,48},{16,32},{32,16},{48,0},{1,49},{17,33},{33,17},{49,1},{2,50}... | collective-permute-start | bytes 135176 | tf_op jit(solution)/shard_map/ppermute | solution.py:416
  107.9 0.9 collective-permute-start.29
  108.8 0.8 collective-permute-start.28
  109.6 0.9 collective-permute-done.30
  110.5 1.9 %collective-permute-done.29 = bf16[176,128]{1,0:T(8,128)(2,1)S(1)} collective-permute-done((bf16[176,128]{1,0:T(8,128)(2,1)S(1)}, bf16[176,128]{1,0:T(8,128)(2,1)S(1)}, u32[]{:S(2)}, u32[]{:S(2)}) %collective-permute-start.29) | collective-permute-done | bytes 45088 | tf_op jit(solution)/shard_map/ppermute | solution.py:416
  112.4 2.0 %collective-permute-start.33 = (bf16[176,128]{1,0:T(8,128)(2,1)S(1)}, bf16[176,128]{1,0:T(8,128)(2,1)S(1)}, u32[]{:S(2)}, u32[]{:S(2)}) collective-permute-start(bf16[176,128]{1,0:T(8,128)(2,1)S(1)} %add_convert_fusion.p0), channel_id=1, source_target_pairs={{0,192},{64,128},{128,64},{192,0},{1,193},{65,129},{129,65},{193,1... | collective-permute-start | bytes 135176 | tf_op jit(solution)/shard_map/ppermute | solution.py:416
  114.4 0.8 collective-permute-start.32
  115.7 0.9 collective-permute-done.33.p3
  116.6 2.2 %collective-permute-done.32.p2 = bf16[176,128]{1,0:T(8,128)(2,1)S(1)} collective-permute-done((bf16[176,128]{1,0:T(8,128)(2,1)S(1)}, bf16[176,128]{1,0:T(8,128)(2,1)S(1)}, u32[]{:S(2)}, u32[]{:S(2)}) %collective-permute-start.32) | collective-permute-done | bytes 45088 | tf_op jit(solution)/shard_map/ppermute | solution.py:416
  119.5 6.0 %collective-permute-start.34 = (f32[40,128]{1,0:T(8,128)S(1)}, f32[40,128]{1,0:T(8,128)S(1)}, u32[]{:S(2)}, u32[]{:S(2)}) collective-permute-start(f32[40,128]{1,0:T(8,128)S(1)} %get-tuple-element.46), channel_id=1, source_target_pairs={{0,1},{1,0},{2,3},{3,2},{4,5},{5,4},{6,7},{7,6},{8,9},{9,8},{10,11... | collective-permute-start | bytes 61448 | tf_op jit(solution)/shard_map/ppermute | solution.py:412
  125.5 0.8 collective-permute-done.34
  126.4 11.4 %all_to_all.11.refs_0_ = f32[8,40,128]{2,1,0:T(8,128)S(1)} all-to-all(f32[8,40,128]{2,1,0:T(8,128)S(1)} %broadcast_in_dim.2), channel_id=1, replica_groups=mesh['y'=4,'x'=4,'z'=8,'c'=2] {'z'}, dimensions={0} | all-to-all | bytes 327680 | tf_op jit(solution)/shard_map/all_to_all | solution.py:468
  137.8 0.7 shard_map.107
  (76 shorter events, 5.4 us)
Async XLA Ops:
  0.6 25.0 %copy-start.4 = (f32[128,128]{1,0:T(8,128)S(1)}, f32[128,128]{1,0:T(8,128)}, u32[]{:S(2)}) copy-start(f32[128,128]{1,0:T(8,128)} %a_ref.3) | copy-start | bytes 196612
  0.6 51.5 %copy-start.8 = (f32[128,172]{0,1:T(8,128)S(1)}, f32[128,172]{0,1:T(8,128)}, u32[]{:S(2)}) copy-start(f32[128,172]{0,1:T(8,128)} %param.9) | copy-start | bytes 264196
  0.7 53.2 %copy-start.7 = (f32[4,128]{1,0:T(4,128)S(1)}, f32[4,128]{1,0:T(4,128)}, u32[]{:S(2)}) copy-start(f32[4,128]{1,0:T(4,128)} %m_ref.5) | copy-start | bytes 6148
  9.7 5.0 %collective-permute-start.2 = (bf16[144,128]{1,0:T(8,128)(2,1)}, bf16[144,128]{1,0:T(8,128)(2,1)S(1)}, u32[]{:S(2)}, u32[]{:S(2)}) collective-permute-start(bf16[144,128]{1,0:T(8,128)(2,1)} %get-tuple-element.29), channel_id=1, source_target_pairs={{0,48},{16,32},{32,16},{48,0},{1,49},{17,33},{33,17},{49,1},{2,50}... | collective-permute-start | bytes 110600 | tf_op jit(solution)/shard_map/ppermute | solution.py:416
  13.1 4.6 %collective-permute-start.1 = (bf16[144,128]{1,0:T(8,128)(2,1)}, bf16[144,128]{1,0:T(8,128)(2,1)S(1)}, u32[]{:S(2)}, u32[]{:S(2)}) collective-permute-start(bf16[144,128]{1,0:T(8,128)(2,1)} %get-tuple-element.29), channel_id=1, source_target_pairs={{0,32},{16,48},{32,0},{48,16},{1,33},{17,49},{33,1},{49,17},{2,34}... | collective-permute-start | bytes 110600 | tf_op jit(solution)/shard_map/ppermute | solution.py:416
  13.7 4.0 %collective-permute-start = (bf16[144,128]{1,0:T(8,128)(2,1)}, bf16[144,128]{1,0:T(8,128)(2,1)S(1)}, u32[]{:S(2)}, u32[]{:S(2)}) collective-permute-start(bf16[144,128]{1,0:T(8,128)(2,1)} %get-tuple-element.29), channel_id=1, source_target_pairs={{0,16},{16,0},{32,48},{48,32},{1,17},{17,1},{33,49},{49,33},{2,18}... | collective-permute-start | bytes 110600 | tf_op jit(solution)/shard_map/ppermute | solution.py:416
  18.5 4.1 %collective-permute-start.5 = (bf16[144,128]{1,0:T(8,128)(2,1)S(1)}, bf16[144,128]{1,0:T(8,128)(2,1)S(1)}, u32[]{:S(2)}, u32[]{:S(2)}) collective-permute-start(bf16[144,128]{1,0:T(8,128)(2,1)S(1)} %add_convert_fusion.1.a), channel_id=1, source_target_pairs={{0,192},{64,128},{128,64},{192,0},{1,193},{65,129},{129,65},{193,1... | collective-permute-start | bytes 110600 | tf_op jit(solution)/shard_map/ppermute | solution.py:416
  21.3 4.3 %collective-permute-start.4 = (bf16[144,128]{1,0:T(8,128)(2,1)S(1)}, bf16[144,128]{1,0:T(8,128)(2,1)S(1)}, u32[]{:S(2)}, u32[]{:S(2)}) collective-permute-start(bf16[144,128]{1,0:T(8,128)(2,1)S(1)} %add_convert_fusion.1.a), channel_id=1, source_target_pairs={{0,128},{64,192},{128,0},{192,64},{1,129},{65,193},{129,1},{193,65... | collective-permute-start | bytes 110600 | tf_op jit(solution)/shard_map/ppermute | solution.py:416
  21.6 4.0 %collective-permute-start.3 = (bf16[144,128]{1,0:T(8,128)(2,1)S(1)}, bf16[144,128]{1,0:T(8,128)(2,1)S(1)}, u32[]{:S(2)}, u32[]{:S(2)}) collective-permute-start(bf16[144,128]{1,0:T(8,128)(2,1)S(1)} %add_convert_fusion.1.a), channel_id=1, source_target_pairs={{0,64},{64,0},{128,192},{192,128},{1,65},{65,1},{129,193},{193,129... | collective-permute-start | bytes 110600 | tf_op jit(solution)/shard_map/ppermute | solution.py:416
  46.7 7.1 %collective-permute-start.6 = (bf16[8,256,128]{2,1,0:T(8,128)(2,1)S(1)}, bf16[8,256,128]{2,1,0:T(8,128)(2,1)S(1)}, u32[]{:S(2)}, u32[]{:S(2)}) collective-permute-start(bf16[8,256,128]{2,1,0:T(8,128)(2,1)S(1)} %all_to_all.10.ma_ref), channel_id=1, source_target_pairs={{0,1},{1,0},{2,3},{3,2},{4,5},{5,4},{6,7},{7,6},{8,9},{9,8},{10,11... | collective-permute-start | bytes 1572872 | tf_op jit(solution)/shard_map/ppermute | solution.py:412
  53.8 33.3 %copy-start.2 = (bf16[128,8192]{1,0:T(8,128)(2,1)S(1)}, bf16[128,8192]{1,0:T(8,128)(2,1)}, u32[]{:S(2)}) copy-start(bf16[128,8192]{1,0:T(8,128)(2,1)} %get-tuple-element.35.lb_ref) | copy-start | bytes 6291460
  58.9 6.4 %collective-permute-start.14 = (bf16[144,512]{1,0:T(8,128)(2,1)S(1)}, bf16[144,512]{1,0:T(8,128)(2,1)S(1)}, u32[]{:S(2)}, u32[]{:S(2)}) collective-permute-start(bf16[144,512]{1,0:T(8,128)(2,1)S(1)} %get-tuple-element.36.refs_0_), channel_id=1, source_target_pairs={{0,2},{2,4},{4,6},{6,8},{8,10},{10,12},{12,14},{14,0},{1,3},{3,5},... | collective-permute-start | bytes 442376 | tf_op jit(solution)/shard_map/ppermute | solution.py:438
  59.2 6.3 %collective-permute-start.8 = (bf16[144,512]{1,0:T(8,128)(2,1)S(1)}, bf16[144,512]{1,0:T(8,128)(2,1)S(1)}, u32[]{:S(2)}, u32[]{:S(2)}) collective-permute-start(bf16[144,512]{1,0:T(8,128)(2,1)S(1)} %get-tuple-element.37), channel_id=1, source_target_pairs={{0,14},{2,0},{4,2},{6,4},{8,6},{10,8},{12,10},{14,12},{1,15},{3,1}... | collective-permute-start | bytes 442376 | tf_op jit(solution)/shard_map/ppermute | solution.py:441
  65.4 5.3 %collective-permute-start.15 = (bf16[144,512]{1,0:T(8,128)(2,1)S(1)}, bf16[144,512]{1,0:T(8,128)(2,1)S(1)}, u32[]{:S(2)}, u32[]{:S(2)}) collective-permute-start(bf16[144,512]{1,0:T(8,128)(2,1)S(1)} %pad_maximum_fusion.2), channel_id=1, source_target_pairs={{0,2},{2,4},{4,6},{6,8},{8,10},{10,12},{12,14},{14,0},{1,3},{3,5},... | collective-permute-start | bytes 442376 | tf_op jit(solution)/shard_map/ppermute | solution.py:438
  70.7 27.9 %copy-start.5 = (f32[8,8192]{1,0:T(8,128)S(1)}, f32[8,8192]{1,0:T(8,128)}, u32[]{:S(2)}) copy-start(f32[8,8192]{1,0:T(8,128)} %get-tuple-element.33.r_ref) | copy-start | bytes 786436
  70.7 5.0 %collective-permute-start.10 = (bf16[144,512]{1,0:T(8,128)(2,1)S(1)}, bf16[144,512]{1,0:T(8,128)(2,1)S(1)}, u32[]{:S(2)}, u32[]{:S(2)}) collective-permute-start(bf16[144,512]{1,0:T(8,128)(2,1)S(1)} %pad_maximum_fusion), channel_id=1, source_target_pairs={{0,14},{2,0},{4,2},{6,4},{8,6},{10,8},{12,10},{14,12},{1,15},{3,1}... | collective-permute-start | bytes 442376 | tf_op jit(solution)/shard_map/ppermute | solution.py:441
  70.8 27.8 %copy-start.3 = (bf16[128,8192]{1,0:T(8,128)(2,1)S(1)}, bf16[128,8192]{1,0:T(8,128)(2,1)}, u32[]{:S(2)}) copy-start(bf16[128,8192]{1,0:T(8,128)(2,1)} %get-tuple-element.34.e_ref) | copy-start | bytes 6291460
  70.9 5.3 %collective-permute-start.16 = (bf16[144,512]{1,0:T(8,128)(2,1)S(1)}, bf16[144,512]{1,0:T(8,128)(2,1)S(1)}, u32[]{:S(2)}, u32[]{:S(2)}) collective-permute-start(bf16[144,512]{1,0:T(8,128)(2,1)S(1)} %pad_maximum_fusion.3), channel_id=1, source_target_pairs={{0,2},{2,4},{4,6},{6,8},{8,10},{10,12},{12,14},{14,0},{1,3},{3,5},... | collective-permute-start | bytes 442376 | tf_op jit(solution)/shard_map/ppermute | solution.py:438
  72.4 5.4 %collective-permute-start.7 = (bf16[144,512]{1,0:T(8,128)(2,1)S(1)}, bf16[144,512]{1,0:T(8,128)(2,1)S(1)}, u32[]{:S(2)}, u32[]{:S(2)}) collective-permute-start(bf16[144,512]{1,0:T(8,128)(2,1)S(1)} %get-tuple-element.36.refs_0_), channel_id=1, source_target_pairs={{0,1},{1,0},{2,3},{3,2},{4,5},{5,4},{6,7},{7,6},{8,9},{9,8},{10,11... | collective-permute-start | bytes 442376 | tf_op jit(solution)/shard_map/ppermute | solution.py:412
  75.2 6.6 %collective-permute-start.9 = (bf16[144,512]{1,0:T(8,128)(2,1)S(1)}, bf16[144,512]{1,0:T(8,128)(2,1)S(1)}, u32[]{:S(2)}, u32[]{:S(2)}) collective-permute-start(bf16[144,512]{1,0:T(8,128)(2,1)S(1)} %collective-permute-done.8.refs_2_), channel_id=1, source_target_pairs={{0,1},{1,0},{2,3},{3,2},{4,5},{5,4},{6,7},{7,6},{8,9},{9,8},{10,11... | collective-permute-start | bytes 442376 | tf_op jit(solution)/shard_map/ppermute | solution.py:412
  75.2 6.7 %collective-permute-start.21 = (bf16[144,512]{1,0:T(8,128)(2,1)S(1)}, bf16[144,512]{1,0:T(8,128)(2,1)S(1)}, u32[]{:S(2)}, u32[]{:S(2)}) collective-permute-start(bf16[144,512]{1,0:T(8,128)(2,1)S(1)} %collective-permute-done.14.refs_14_), channel_id=1, source_target_pairs={{0,1},{1,0},{2,3},{3,2},{4,5},{5,4},{6,7},{7,6},{8,9},{9,8},{10,11... | collective-permute-start | bytes 442376 | tf_op jit(solution)/shard_map/ppermute | solution.py:412
  76.2 6.2 %collective-permute-start.12 = (bf16[144,512]{1,0:T(8,128)(2,1)S(1)}, bf16[144,512]{1,0:T(8,128)(2,1)S(1)}, u32[]{:S(2)}, u32[]{:S(2)}) collective-permute-start(bf16[144,512]{1,0:T(8,128)(2,1)S(1)} %pad_maximum_fusion.1), channel_id=1, source_target_pairs={{0,14},{2,0},{4,2},{6,4},{8,6},{10,8},{12,10},{14,12},{1,15},{3,1}... | collective-permute-start | bytes 442376 | tf_op jit(solution)/shard_map/ppermute | solution.py:441
  76.8 8.0 %collective-permute-start.17 = (bf16[144,512]{1,0:T(8,128)(2,1)S(1)}, bf16[144,512]{1,0:T(8,128)(2,1)S(1)}, u32[]{:S(2)}, u32[]{:S(2)}) collective-permute-start(bf16[144,512]{1,0:T(8,128)(2,1)S(1)} %pad_maximum_fusion.4), channel_id=1, source_target_pairs={{0,2},{2,4},{4,6},{6,8},{8,10},{10,12},{12,14},{14,0},{1,3},{3,5},... | collective-permute-start | bytes 442376 | tf_op jit(solution)/shard_map/ppermute | solution.py:438
  77.8 8.3 %collective-permute-start.20 = (bf16[144,512]{1,0:T(8,128)(2,1)S(1)}, bf16[144,512]{1,0:T(8,128)(2,1)S(1)}, u32[]{:S(2)}, u32[]{:S(2)}) collective-permute-start(bf16[144,512]{1,0:T(8,128)(2,1)S(1)} %collective-permute-done.15.refs_12_), channel_id=1, source_target_pairs={{0,1},{1,0},{2,3},{3,2},{4,5},{5,4},{6,7},{7,6},{8,9},{9,8},{10,11... | collective-permute-start | bytes 442376 | tf_op jit(solution)/shard_map/ppermute | solution.py:412
  81.8 4.3 %collective-permute-start.19 = (bf16[144,512]{1,0:T(8,128)(2,1)S(1)}, bf16[144,512]{1,0:T(8,128)(2,1)S(1)}, u32[]{:S(2)}, u32[]{:S(2)}) collective-permute-start(bf16[144,512]{1,0:T(8,128)(2,1)S(1)} %collective-permute-done.16.refs_10_), channel_id=1, source_target_pairs={{0,1},{1,0},{2,3},{3,2},{4,5},{5,4},{6,7},{7,6},{8,9},{9,8},{10,11... | collective-permute-start | bytes 442376 | tf_op jit(solution)/shard_map/ppermute | solution.py:412
  81.9 4.3 %collective-permute-start.11 = (bf16[144,512]{1,0:T(8,128)(2,1)S(1)}, bf16[144,512]{1,0:T(8,128)(2,1)S(1)}, u32[]{:S(2)}, u32[]{:S(2)}) collective-permute-start(bf16[144,512]{1,0:T(8,128)(2,1)S(1)} %collective-permute-done.10.refs_4_), channel_id=1, source_target_pairs={{0,1},{1,0},{2,3},{3,2},{4,5},{5,4},{6,7},{7,6},{8,9},{9,8},{10,11... | collective-permute-start | bytes 442376 | tf_op jit(solution)/shard_map/ppermute | solution.py:412
  82.3 3.8 %collective-permute-start.13 = (bf16[144,512]{1,0:T(8,128)(2,1)S(1)}, bf16[144,512]{1,0:T(8,128)(2,1)S(1)}, u32[]{:S(2)}, u32[]{:S(2)}) collective-permute-start(bf16[144,512]{1,0:T(8,128)(2,1)S(1)} %collective-permute-done.12.refs_6_), channel_id=1, source_target_pairs={{0,1},{1,0},{2,3},{3,2},{4,5},{5,4},{6,7},{7,6},{8,9},{9,8},{10,11... | collective-permute-start | bytes 442376 | tf_op jit(solution)/shard_map/ppermute | solution.py:412
  84.8 2.3 %collective-permute-start.18 = (bf16[144,512]{1,0:T(8,128)(2,1)S(1)}, bf16[144,512]{1,0:T(8,128)(2,1)S(1)}, u32[]{:S(2)}, u32[]{:S(2)}) collective-permute-start(bf16[144,512]{1,0:T(8,128)(2,1)S(1)} %collective-permute-done.17.refs_8_), channel_id=1, source_target_pairs={{0,1},{1,0},{2,3},{3,2},{4,5},{5,4},{6,7},{7,6},{8,9},{9,8},{10,11... | collective-permute-start | bytes 442376 | tf_op jit(solution)/shard_map/ppermute | solution.py:412
  87.2 11.4 %copy-start = (bf16[8192,128]{1,0:T(8,128)(2,1)S(1)}, bf16[8192,128]{1,0:T(8,128)(2,1)}, u32[]{:S(2)}) copy-start(bf16[8192,128]{1,0:T(8,128)(2,1)} %f_ref.3) | copy-start | bytes 6291460
  87.2 11.4 %copy-start.1 = (bf16[128,8192]{1,0:T(8,128)(2,1)S(1)}, bf16[128,8192]{1,0:T(8,128)(2,1)}, u32[]{:S(2)}) copy-start(bf16[128,8192]{1,0:T(8,128)(2,1)} %get-tuple-element.28.ft_ref) | copy-start | bytes 6291460
  87.2 11.4 %copy-start.6 = (bf16[512,128]{1,0:T(8,128)(2,1)S(1)}, bf16[512,128]{1,0:T(8,128)(2,1)}, u32[]{:S(2)}) copy-start(bf16[512,128]{1,0:T(8,128)(2,1)} %get-tuple-element.40.am_ref) | copy-start | bytes 393220
  88.0 4.1 %collective-permute-start.24 = (bf16[128,128]{1,0:T(8,128)(2,1)S(1)}, bf16[128,128]{1,0:T(8,128)(2,1)S(1)}, u32[]{:S(2)}, u32[]{:S(2)}) collective-permute-start(bf16[128,128]{1,0:T(8,128)(2,1)S(1)} %get-tuple-element.45), channel_id=1, source_target_pairs={{0,48},{16,32},{32,16},{48,0},{1,49},{17,33},{33,17},{49,1},{2,50}... | collective-permute-start | bytes 98312 | tf_op jit(solution)/shard_map/ppermute | solution.py:416
  89.2 4.3 %collective-permute-start.23 = (bf16[128,128]{1,0:T(8,128)(2,1)S(1)}, bf16[128,128]{1,0:T(8,128)(2,1)S(1)}, u32[]{:S(2)}, u32[]{:S(2)}) collective-permute-start(bf16[128,128]{1,0:T(8,128)(2,1)S(1)} %get-tuple-element.45), channel_id=1, source_target_pairs={{0,32},{16,48},{32,0},{48,16},{1,33},{17,49},{33,1},{49,17},{2,34}... | collective-permute-start | bytes 98312 | tf_op jit(solution)/shard_map/ppermute | solution.py:416
  89.8 3.7 %collective-permute-start.22 = (bf16[128,128]{1,0:T(8,128)(2,1)S(1)}, bf16[128,128]{1,0:T(8,128)(2,1)S(1)}, u32[]{:S(2)}, u32[]{:S(2)}) collective-permute-start(bf16[128,128]{1,0:T(8,128)(2,1)S(1)} %get-tuple-element.45), channel_id=1, source_target_pairs={{0,16},{16,0},{32,48},{48,32},{1,17},{17,1},{33,49},{49,33},{2,18}... | collective-permute-start | bytes 98312 | tf_op jit(solution)/shard_map/ppermute | solution.py:416
  93.5 4.1 %collective-permute-start.27 = (bf16[128,128]{1,0:T(8,128)(2,1)S(1)}, bf16[128,128]{1,0:T(8,128)(2,1)S(1)}, u32[]{:S(2)}, u32[]{:S(2)}) collective-permute-start(bf16[128,128]{1,0:T(8,128)(2,1)S(1)} %add_convert_fusion.2.p0), channel_id=1, source_target_pairs={{0,192},{64,128},{128,64},{192,0},{1,193},{65,129},{129,65},{193,1... | collective-permute-start | bytes 98312 | tf_op jit(solution)/shard_map/ppermute | solution.py:416
  94.3 4.3 %collective-permute-start.26 = (bf16[128,128]{1,0:T(8,128)(2,1)S(1)}, bf16[128,128]{1,0:T(8,128)(2,1)S(1)}, u32[]{:S(2)}, u32[]{:S(2)}) collective-permute-start(bf16[128,128]{1,0:T(8,128)(2,1)S(1)} %add_convert_fusion.2.p0), channel_id=1, source_target_pairs={{0,128},{64,192},{128,0},{192,64},{1,129},{65,193},{129,1},{193,65... | collective-permute-start | bytes 98312 | tf_op jit(solution)/shard_map/ppermute | solution.py:416
  95.3 3.2 %collective-permute-start.25 = (bf16[128,128]{1,0:T(8,128)(2,1)S(1)}, bf16[128,128]{1,0:T(8,128)(2,1)S(1)}, u32[]{:S(2)}, u32[]{:S(2)}) collective-permute-start(bf16[128,128]{1,0:T(8,128)(2,1)S(1)} %add_convert_fusion.2.p0), channel_id=1, source_target_pairs={{0,64},{64,0},{128,192},{192,128},{1,65},{65,1},{129,193},{193,129... | collective-permute-start | bytes 98312 | tf_op jit(solution)/shard_map/ppermute | solution.py:416
  106.1 4.4 %collective-permute-start.30 = (bf16[176,128]{1,0:T(8,128)(2,1)S(1)}, bf16[176,128]{1,0:T(8,128)(2,1)S(1)}, u32[]{:S(2)}, u32[]{:S(2)}) collective-permute-start(bf16[176,128]{1,0:T(8,128)(2,1)S(1)} %constant_dynamic-update-slice_fusion), channel_id=1, source_target_pairs={{0,48},{16,32},{32,16},{48,0},{1,49},{17,33},{33,17},{49,1},{2,50}... | collective-permute-start | bytes 135176 | tf_op jit(solution)/shard_map/ppermute | solution.py:416
  107.9 4.4 %collective-permute-start.29 = (bf16[176,128]{1,0:T(8,128)(2,1)S(1)}, bf16[176,128]{1,0:T(8,128)(2,1)S(1)}, u32[]{:S(2)}, u32[]{:S(2)}) collective-permute-start(bf16[176,128]{1,0:T(8,128)(2,1)S(1)} %constant_dynamic-update-slice_fusion), channel_id=1, source_target_pairs={{0,32},{16,48},{32,0},{48,16},{1,33},{17,49},{33,1},{49,17},{2,34}... | collective-permute-start | bytes 135176 | tf_op jit(solution)/shard_map/ppermute | solution.py:416
  108.8 3.5 %collective-permute-start.28 = (bf16[176,128]{1,0:T(8,128)(2,1)S(1)}, bf16[176,128]{1,0:T(8,128)(2,1)S(1)}, u32[]{:S(2)}, u32[]{:S(2)}) collective-permute-start(bf16[176,128]{1,0:T(8,128)(2,1)S(1)} %constant_dynamic-update-slice_fusion), channel_id=1, source_target_pairs={{0,16},{16,0},{32,48},{48,32},{1,17},{17,1},{33,49},{49,33},{2,18}... | collective-permute-start | bytes 135176 | tf_op jit(solution)/shard_map/ppermute | solution.py:416
  112.4 4.2 %collective-permute-start.33 = (bf16[176,128]{1,0:T(8,128)(2,1)S(1)}, bf16[176,128]{1,0:T(8,128)(2,1)S(1)}, u32[]{:S(2)}, u32[]{:S(2)}) collective-permute-start(bf16[176,128]{1,0:T(8,128)(2,1)S(1)} %add_convert_fusion.p0), channel_id=1, source_target_pairs={{0,192},{64,128},{128,64},{192,0},{1,193},{65,129},{129,65},{193,1... | collective-permute-start | bytes 135176 | tf_op jit(solution)/shard_map/ppermute | solution.py:416
  114.4 4.4 %collective-permute-start.32 = (bf16[176,128]{1,0:T(8,128)(2,1)S(1)}, bf16[176,128]{1,0:T(8,128)(2,1)S(1)}, u32[]{:S(2)}, u32[]{:S(2)}) collective-permute-start(bf16[176,128]{1,0:T(8,128)(2,1)S(1)} %add_convert_fusion.p0), channel_id=1, source_target_pairs={{0,128},{64,192},{128,0},{192,64},{1,129},{65,193},{129,1},{193,65... | collective-permute-start | bytes 135176 | tf_op jit(solution)/shard_map/ppermute | solution.py:416
  115.2 3.6 %collective-permute-start.31 = (bf16[176,128]{1,0:T(8,128)(2,1)S(1)}, bf16[176,128]{1,0:T(8,128)(2,1)S(1)}, u32[]{:S(2)}, u32[]{:S(2)}) collective-permute-start(bf16[176,128]{1,0:T(8,128)(2,1)S(1)} %add_convert_fusion.p0), channel_id=1, source_target_pairs={{0,64},{64,0},{128,192},{192,128},{1,65},{65,1},{129,193},{193,129... | collective-permute-start | bytes 135176 | tf_op jit(solution)/shard_map/ppermute | solution.py:416
  119.5 6.9 %collective-permute-start.34 = (f32[40,128]{1,0:T(8,128)S(1)}, f32[40,128]{1,0:T(8,128)S(1)}, u32[]{:S(2)}, u32[]{:S(2)}) collective-permute-start(f32[40,128]{1,0:T(8,128)S(1)} %get-tuple-element.46), channel_id=1, source_target_pairs={{0,1},{1,0},{2,3},{3,2},{4,5},{5,4},{6,7},{7,6},{8,9},{9,8},{10,11... | collective-permute-start | bytes 61448 | tf_op jit(solution)/shard_map/ppermute | solution.py:412

commit v5 on v4

--- a/solution.py
+++ b/solution.py
@@ -183,7 +183,7 @@
     )(*parts, anchors)
 
 
-HEAD_STEP = 2
+HEAD_STEP = 4
 
 
 def head_kernel(s_ref, m_ref, ft_ref, ma_ref, mb_ref, cls_ref, tag_ref, emb_ref, up_ref, down_ref, part_ref, loss_ref):
@@ -335,7 +335,7 @@
         msg_ref[APD : APD + 16, :] = jnp.concatenate(rows, axis=0).astype(bf16)
 
 
-SCORE_BLOCK = 2048
+SCORE_BLOCK = 4096
 SCORE_CHUNK = 256
 
 
@@ -358,7 +358,7 @@
             pltpu.VMEM((APD, F), f32),
             pltpu.VMEM((HEADS * APD, SCORE_BLOCK), bf16),
         ],
-        compiler_params=params(24),
+        compiler_params=params(32),
     )(features, ft, rinv, excess, grads, am, anchors, metric, means, total, degree, loss, *parts)
 
 

time: 139 us -> 138 us (level)
  no operation moved by 1% of the time
where the time goes in v5:
time: 138 us; the launch traced here: 137 us
  starting transfers between devices  50.2 us (36%)
  blocking collectives  32.4 us (23%)
  waiting for transfers between devices  28.4 us (21%)
  Pallas kernels  22.8 us (17%)
  local copies, waits for them, and re-layouts  1.76 us (1%)
    ppermute x10, starting transfers between devices, swap(): return lax.ppermute(x, 'c', [(0, 1), (1, 0)])  23.2 us
    all_to_all x1, blocking collectives, body(): means_a = lax.all_to_all(msg, 'z', 0, 0, tiled=True)  21 us
    ppermute x18, starting transfers between devices, shared(): lax.ppermute(x, axis, [(i, i ^ k) for i in range(4)])  20.9 us
    ppermute x18, waiting for transfers between devices, shared(): lax.ppermute(x, axis, [(i, i ^ k) for i in range(4)])  17.2 us
    all_to_all x1, blocking collectives, body(): lax.all_to_all(jnp.broadcast_to(small[None], (NZ,) + small.shape), 'z', 0...  11.4 us
    ppermute x4, waiting for transfers between devices, ring(): up = lax.ppermute(up, 'z', ups)  9.3 us
    pallas_call x1, Pallas kernels, link_call(): pl.pallas_call(link_kernel, grid=(n // LINK_BLOCK,), in_specs=[pl.BlockSp...  9.08 us
    pallas_call x1, Pallas kernels, score_call(): pl.pallas_call(score_kernel, grid=(n // SCORE_BLOCK,), in_specs=[pl.Block...  7.01 us
  transfers between devices with their start and end apart: 35, of which 17 were waited for; matrix products, arithmetic and copies ran while one was open for 1% of the time, Pallas kernels for 0%

profile of v5, /device:TPU:1, one launch (start us, length us, event | category | flops | bytes accessed | tf_op | source)
XLA Modules:
  0.0 137.4 jit_solution(11145939303984600427)
XLA Ops:
  0.7 9.1 %shard_map.101 = (bf16[128,8192]{1,0:T(8,128)(2,1)}, f32[8,8192]{1,0:T(8,128)}, bf16[128,8192]{1,0:T(8,128)(2,1)}, bf16[128,8192]{1,0:T(8,128)(2,1)}, s32[1,8192...) custom-call(bf16[8192,128]{1,0:T(8,128)(2,1)} %f_ref.3, f32[128,128]{1,0:T(8,128)} %a_ref.3, ...), custom_call_target="tpu_custom_call" | custom-call | tf_op jit(solution)/shard_map/pallas_call | solution.py:115
  9.7 3.4 %collective-permute-start.2 = (bf16[144,128]{1,0:T(8,128)(2,1)}, bf16[144,128]{1,0:T(8,128)(2,1)S(1)}, u32[]{:S(2)}, u32[]{:S(2)}) collective-permute-start(bf16[144,128]{1,0:T(8,128)(2,1)} %get-tuple-element.29), channel_id=1, source_target_pairs={{0,48},{16,32},{32,16},{48,0},{1,49},{17,33},{33,17},{49,1},{2,50}... | collective-permute-start | bytes 110600 | tf_op jit(solution)/shard_map/ppermute | solution.py:416
  13.8 0.9 collective-permute-done.2
  14.7 3.0 %collective-permute-done.1 = bf16[144,128]{1,0:T(8,128)(2,1)S(1)} collective-permute-done((bf16[144,128]{1,0:T(8,128)(2,1)}, bf16[144,128]{1,0:T(8,128)(2,1)S(1)}, u32[]{:S(2)}, u32[]{:S(2)}) %collective-permute-start.1) | collective-permute-done | bytes 36896 | tf_op jit(solution)/shard_map/ppermute | solution.py:416
  17.7 0.8 add_convert_fusion.1.a
  18.5 2.8 %collective-permute-start.5 = (bf16[144,128]{1,0:T(8,128)(2,1)S(1)}, bf16[144,128]{1,0:T(8,128)(2,1)S(1)}, u32[]{:S(2)}, u32[]{:S(2)}) collective-permute-start(bf16[144,128]{1,0:T(8,128)(2,1)S(1)} %add_convert_fusion.1.a), channel_id=1, source_target_pairs={{0,192},{64,128},{128,64},{192,0},{1,193},{65,129},{129,65},{193,1... | collective-permute-start | bytes 110600 | tf_op jit(solution)/shard_map/ppermute | solution.py:416
  22.0 0.7 collective-permute-done.5.d
  22.6 3.0 %collective-permute-done.4.c = bf16[144,128]{1,0:T(8,128)(2,1)S(1)} collective-permute-done((bf16[144,128]{1,0:T(8,128)(2,1)S(1)}, bf16[144,128]{1,0:T(8,128)(2,1)S(1)}, u32[]{:S(2)}, u32[]{:S(2)}) %collective-permute-start.4) | collective-permute-done | bytes 36896 | tf_op jit(solution)/shard_map/ppermute | solution.py:416
  25.7 21.0 %all_to_all.10.ma_ref = bf16[8,256,128]{2,1,0:T(8,128)(2,1)S(1)} all-to-all(bf16[8,256,128]{2,1,0:T(8,128)(2,1)S(1)} %get-tuple-element.30), channel_id=1, replica_groups=mesh['y'=4,'x'=4,'z'=8,'c'=2] {'z'}, dimensions={0} | all-to-all | bytes 1048576 | tf_op jit(solution)/shard_map/all_to_all | solution.py:456
  46.7 5.5 %collective-permute-start.6 = (bf16[8,256,128]{2,1,0:T(8,128)(2,1)S(1)}, bf16[8,256,128]{2,1,0:T(8,128)(2,1)S(1)}, u32[]{:S(2)}, u32[]{:S(2)}) collective-permute-start(bf16[8,256,128]{2,1,0:T(8,128)(2,1)S(1)} %all_to_all.10.ma_ref), channel_id=1, source_target_pairs={{0,1},{1,0},{2,3},{3,2},{4,5},{5,4},{6,7},{7,6},{8,9},{9,8},{10,11... | collective-permute-start | bytes 1572872 | tf_op jit(solution)/shard_map/ppermute | solution.py:412
  52.2 0.7 constant_dynamic-slice_fusion.tag_ref
  52.9 0.9 constant_dynamic-slice_fusion.1.ft_ref
  53.8 4.4 %shard_map.103 = (bf16[512,128]{1,0:T(8,128)(2,1)}, bf16[144,512]{1,0:T(8,128)(2,1)S(1)}, bf16[144,512]{1,0:T(8,128)(2,1)S(1)}, f32[8,8,512]{2,1,0:T(8,128)S(1)}, f32[8,128]{1,0:T(8,128)S(1)}) custom-call(s32[1]{0:T(128)} %bitcast.s_ref, f32[4,128]{1,0:T(4,128)S(1)} %copy-done.7, bf16[128,512]{1,0:T(8,128)(2,1)S(1)} %constant_dynamic-slice_fusion.1.ft_ref, ...), custom_call_target="tpu_custom_call" | custom-call | tf_op jit(solution)/shard_map/pallas_call | solution.py:230
  58.5 2.4 %collective-permute-start.8 = (bf16[144,512]{1,0:T(8,128)(2,1)S(1)}, bf16[144,512]{1,0:T(8,128)(2,1)S(1)}, u32[]{:S(2)}, u32[]{:S(2)}) collective-permute-start(bf16[144,512]{1,0:T(8,128)(2,1)S(1)} %get-tuple-element.37), channel_id=1, source_target_pairs={{0,14},{2,0},{4,2},{6,4},{8,6},{10,8},{12,10},{14,12},{1,15},{3,1}... | collective-permute-start | bytes 442376 | tf_op jit(solution)/shard_map/ppermute | solution.py:441
  60.9 3.7 %collective-permute-done.14.refs_14_ = bf16[144,512]{1,0:T(8,128)(2,1)S(1)} collective-permute-done((bf16[144,512]{1,0:T(8,128)(2,1)S(1)}, bf16[144,512]{1,0:T(8,128)(2,1)S(1)}, u32[]{:S(2)}, u32[]{:S(2)}) %collective-permute-start.14) | collective-permute-done | bytes 147488 | tf_op jit(solution)/shard_map/ppermute | solution.py:438
  64.8 5.2 %collective-permute-done.15.refs_12_ = bf16[144,512]{1,0:T(8,128)(2,1)S(1)} collective-permute-done((bf16[144,512]{1,0:T(8,128)(2,1)S(1)}, bf16[144,512]{1,0:T(8,128)(2,1)S(1)}, u32[]{:S(2)}, u32[]{:S(2)}) %collective-permute-start.15) | collective-permute-done | bytes 147488 | tf_op jit(solution)/shard_map/ppermute | solution.py:438
  70.1 1.7 %collective-permute-start.16 = (bf16[144,512]{1,0:T(8,128)(2,1)S(1)}, bf16[144,512]{1,0:T(8,128)(2,1)S(1)}, u32[]{:S(2)}, u32[]{:S(2)}) collective-permute-start(bf16[144,512]{1,0:T(8,128)(2,1)S(1)} %pad_maximum_fusion.3), channel_id=1, source_target_pairs={{0,2},{2,4},{4,6},{6,8},{8,10},{10,12},{12,14},{14,0},{1,3},{3,5},... | collective-permute-start | bytes 442376 | tf_op jit(solution)/shard_map/ppermute | solution.py:438
  71.8 2.8 %collective-permute-start.7 = (bf16[144,512]{1,0:T(8,128)(2,1)S(1)}, bf16[144,512]{1,0:T(8,128)(2,1)S(1)}, u32[]{:S(2)}, u32[]{:S(2)}) collective-permute-start(bf16[144,512]{1,0:T(8,128)(2,1)S(1)} %get-tuple-element.36.refs_0_), channel_id=1, source_target_pairs={{0,1},{1,0},{2,3},{3,2},{4,5},{5,4},{6,7},{7,6},{8,9},{9,8},{10,11... | collective-permute-start | bytes 442376 | tf_op jit(solution)/shard_map/ppermute | solution.py:412
  75.6 0.7 collective-permute-start.12
  76.3 1.0 collective-permute-start.17
  77.3 4.0 %collective-permute-start.20 = (bf16[144,512]{1,0:T(8,128)(2,1)S(1)}, bf16[144,512]{1,0:T(8,128)(2,1)S(1)}, u32[]{:S(2)}, u32[]{:S(2)}) collective-permute-start(bf16[144,512]{1,0:T(8,128)(2,1)S(1)} %collective-permute-done.15.refs_12_), channel_id=1, source_target_pairs={{0,1},{1,0},{2,3},{3,2},{4,5},{5,4},{6,7},{7,6},{8,9},{9,8},{10,11... | collective-permute-start | bytes 442376 | tf_op jit(solution)/shard_map/ppermute | solution.py:412
  81.8 2.5 %collective-permute-start.13 = (bf16[144,512]{1,0:T(8,128)(2,1)S(1)}, bf16[144,512]{1,0:T(8,128)(2,1)S(1)}, u32[]{:S(2)}, u32[]{:S(2)}) collective-permute-start(bf16[144,512]{1,0:T(8,128)(2,1)S(1)} %collective-permute-done.12.refs_6_), channel_id=1, source_target_pairs={{0,1},{1,0},{2,3},{3,2},{4,5},{5,4},{6,7},{7,6},{8,9},{9,8},{10,11... | collective-permute-start | bytes 442376 | tf_op jit(solution)/shard_map/ppermute | solution.py:412
  84.3 1.3 collective-permute-start.18
  85.6 1.0 collective-permute-done.18.refs_9_
  86.6 0.8 shard_map.104
  87.4 1.2 collective-permute-start.24
  89.2 1.5 %collective-permute-start.22 = (bf16[128,128]{1,0:T(8,128)(2,1)S(1)}, bf16[128,128]{1,0:T(8,128)(2,1)S(1)}, u32[]{:S(2)}, u32[]{:S(2)}) collective-permute-start(bf16[128,128]{1,0:T(8,128)(2,1)S(1)} %get-tuple-element.45), channel_id=1, source_target_pairs={{0,16},{16,0},{32,48},{48,32},{1,17},{17,1},{33,49},{49,33},{2,18}... | collective-permute-start | bytes 98312 | tf_op jit(solution)/shard_map/ppermute | solution.py:416
  90.8 0.7 collective-permute-done.24
  91.5 1.4 %collective-permute-done.23 = bf16[128,128]{1,0:T(8,128)(2,1)S(1)} collective-permute-done((bf16[128,128]{1,0:T(8,128)(2,1)S(1)}, bf16[128,128]{1,0:T(8,128)(2,1)S(1)}, u32[]{:S(2)}, u32[]{:S(2)}) %collective-permute-start.23) | collective-permute-done | bytes 32800 | tf_op jit(solution)/shard_map/ppermute | solution.py:416
  92.9 0.8 collective-permute-start.27
  93.8 1.0 collective-permute-start.26
  94.8 1.5 %collective-permute-start.25 = (bf16[128,128]{1,0:T(8,128)(2,1)S(1)}, bf16[128,128]{1,0:T(8,128)(2,1)S(1)}, u32[]{:S(2)}, u32[]{:S(2)}) collective-permute-start(bf16[128,128]{1,0:T(8,128)(2,1)S(1)} %add_convert_fusion.2.p0), channel_id=1, source_target_pairs={{0,64},{64,0},{128,192},{192,128},{1,65},{65,1},{129,193},{193,129... | collective-permute-start | bytes 98312 | tf_op jit(solution)/shard_map/ppermute | solution.py:416
  96.3 0.7 collective-permute-done.27.p3
  97.0 1.0 collective-permute-done.26.p2
  98.1 7.0 %shard_map.105 = bf16[144,128]{1,0:T(8,128)(2,1)S(1)} custom-call(bf16[8192,128]{1,0:T(8,128)(2,1)S(1)} %copy-done, bf16[128,8192]{1,0:T(8,128)(2,1)S(1)} %copy-done.1, f32[8,8192]{1,0:T(8,128)S(1)} %copy-done.5, bf16[128,8192]{1,0:T(8,128)(2,1)S(1)} %copy-done.3, bf16[144,8192]{1,0:T(8,128)(2,1)S(1)} %get-tuple-element.39.g_ref, ...), custom_call_target="tpu_custom_call" | custom-call | tf_op jit(solution)/shard_map/pallas_call | solution.py:347
  105.1 1.6 %collective-permute-start.30 = (bf16[176,128]{1,0:T(8,128)(2,1)S(1)}, bf16[176,128]{1,0:T(8,128)(2,1)S(1)}, u32[]{:S(2)}, u32[]{:S(2)}) collective-permute-start(bf16[176,128]{1,0:T(8,128)(2,1)S(1)} %constant_dynamic-update-slice_fusion), channel_id=1, source_target_pairs={{0,48},{16,32},{32,16},{48,0},{1,49},{17,33},{33,17},{49,1},{2,50}... | collective-permute-start | bytes 135176 | tf_op jit(solution)/shard_map/ppermute | solution.py:416
  106.8 0.9 collective-permute-start.29
  107.6 0.8 collective-permute-start.28
  108.5 0.9 collective-permute-done.30
  109.3 1.8 %collective-permute-done.29 = bf16[176,128]{1,0:T(8,128)(2,1)S(1)} collective-permute-done((bf16[176,128]{1,0:T(8,128)(2,1)S(1)}, bf16[176,128]{1,0:T(8,128)(2,1)S(1)}, u32[]{:S(2)}, u32[]{:S(2)}) %collective-permute-start.29) | collective-permute-done | bytes 45088 | tf_op jit(solution)/shard_map/ppermute | solution.py:416
  111.2 2.1 %collective-permute-start.33 = (bf16[176,128]{1,0:T(8,128)(2,1)S(1)}, bf16[176,128]{1,0:T(8,128)(2,1)S(1)}, u32[]{:S(2)}, u32[]{:S(2)}) collective-permute-start(bf16[176,128]{1,0:T(8,128)(2,1)S(1)} %add_convert_fusion.p0), channel_id=1, source_target_pairs={{0,192},{64,128},{128,64},{192,0},{1,193},{65,129},{129,65},{193,1... | collective-permute-start | bytes 135176 | tf_op jit(solution)/shard_map/ppermute | solution.py:416
  113.3 0.8 collective-permute-start.32
  114.6 0.9 collective-permute-done.33.p3
  115.4 2.2 %collective-permute-done.32.p2 = bf16[176,128]{1,0:T(8,128)(2,1)S(1)} collective-permute-done((bf16[176,128]{1,0:T(8,128)(2,1)S(1)}, bf16[176,128]{1,0:T(8,128)(2,1)S(1)}, u32[]{:S(2)}, u32[]{:S(2)}) %collective-permute-start.32) | collective-permute-done | bytes 45088 | tf_op jit(solution)/shard_map/ppermute | solution.py:416
  118.3 6.0 %collective-permute-start.34 = (f32[40,128]{1,0:T(8,128)S(1)}, f32[40,128]{1,0:T(8,128)S(1)}, u32[]{:S(2)}, u32[]{:S(2)}) collective-permute-start(f32[40,128]{1,0:T(8,128)S(1)} %get-tuple-element.46), channel_id=1, source_target_pairs={{0,1},{1,0},{2,3},{3,2},{4,5},{5,4},{6,7},{7,6},{8,9},{9,8},{10,11... | collective-permute-start | bytes 61448 | tf_op jit(solution)/shard_map/ppermute | solution.py:412
  124.4 0.8 collective-permute-done.34
  125.2 11.4 %all_to_all.11.refs_0_ = f32[8,40,128]{2,1,0:T(8,128)S(1)} all-to-all(f32[8,40,128]{2,1,0:T(8,128)S(1)} %broadcast_in_dim.2), channel_id=1, replica_groups=mesh['y'=4,'x'=4,'z'=8,'c'=2] {'z'}, dimensions={0} | all-to-all | bytes 327680 | tf_op jit(solution)/shard_map/all_to_all | solution.py:468
  136.7 0.7 shard_map.107
  (76 shorter events, 5.4 us)
Async XLA Ops:
  0.6 25.0 %copy-start.4 = (f32[128,128]{1,0:T(8,128)S(1)}, f32[128,128]{1,0:T(8,128)}, u32[]{:S(2)}) copy-start(f32[128,128]{1,0:T(8,128)} %a_ref.3) | copy-start | bytes 196612
  0.6 51.5 %copy-start.8 = (f32[128,172]{0,1:T(8,128)S(1)}, f32[128,172]{0,1:T(8,128)}, u32[]{:S(2)}) copy-start(f32[128,172]{0,1:T(8,128)} %param.9) | copy-start | bytes 264196
  0.7 53.2 %copy-start.7 = (f32[4,128]{1,0:T(4,128)S(1)}, f32[4,128]{1,0:T(4,128)}, u32[]{:S(2)}) copy-start(f32[4,128]{1,0:T(4,128)} %m_ref.5) | copy-start | bytes 6148
  9.7 5.0 %collective-permute-start.2 = (bf16[144,128]{1,0:T(8,128)(2,1)}, bf16[144,128]{1,0:T(8,128)(2,1)S(1)}, u32[]{:S(2)}, u32[]{:S(2)}) collective-permute-start(bf16[144,128]{1,0:T(8,128)(2,1)} %get-tuple-element.29), channel_id=1, source_target_pairs={{0,48},{16,32},{32,16},{48,0},{1,49},{17,33},{33,17},{49,1},{2,50}... | collective-permute-start | bytes 110600 | tf_op jit(solution)/shard_map/ppermute | solution.py:416
  13.1 4.6 %collective-permute-start.1 = (bf16[144,128]{1,0:T(8,128)(2,1)}, bf16[144,128]{1,0:T(8,128)(2,1)S(1)}, u32[]{:S(2)}, u32[]{:S(2)}) collective-permute-start(bf16[144,128]{1,0:T(8,128)(2,1)} %get-tuple-element.29), channel_id=1, source_target_pairs={{0,32},{16,48},{32,0},{48,16},{1,33},{17,49},{33,1},{49,17},{2,34}... | collective-permute-start | bytes 110600 | tf_op jit(solution)/shard_map/ppermute | solution.py:416
  13.7 4.0 %collective-permute-start = (bf16[144,128]{1,0:T(8,128)(2,1)}, bf16[144,128]{1,0:T(8,128)(2,1)S(1)}, u32[]{:S(2)}, u32[]{:S(2)}) collective-permute-start(bf16[144,128]{1,0:T(8,128)(2,1)} %get-tuple-element.29), channel_id=1, source_target_pairs={{0,16},{16,0},{32,48},{48,32},{1,17},{17,1},{33,49},{49,33},{2,18}... | collective-permute-start | bytes 110600 | tf_op jit(solution)/shard_map/ppermute | solution.py:416
  18.5 4.1 %collective-permute-start.5 = (bf16[144,128]{1,0:T(8,128)(2,1)S(1)}, bf16[144,128]{1,0:T(8,128)(2,1)S(1)}, u32[]{:S(2)}, u32[]{:S(2)}) collective-permute-start(bf16[144,128]{1,0:T(8,128)(2,1)S(1)} %add_convert_fusion.1.a), channel_id=1, source_target_pairs={{0,192},{64,128},{128,64},{192,0},{1,193},{65,129},{129,65},{193,1... | collective-permute-start | bytes 110600 | tf_op jit(solution)/shard_map/ppermute | solution.py:416
  21.3 4.3 %collective-permute-start.4 = (bf16[144,128]{1,0:T(8,128)(2,1)S(1)}, bf16[144,128]{1,0:T(8,128)(2,1)S(1)}, u32[]{:S(2)}, u32[]{:S(2)}) collective-permute-start(bf16[144,128]{1,0:T(8,128)(2,1)S(1)} %add_convert_fusion.1.a), channel_id=1, source_target_pairs={{0,128},{64,192},{128,0},{192,64},{1,129},{65,193},{129,1},{193,65... | collective-permute-start | bytes 110600 | tf_op jit(solution)/shard_map/ppermute | solution.py:416
  21.6 4.0 %collective-permute-start.3 = (bf16[144,128]{1,0:T(8,128)(2,1)S(1)}, bf16[144,128]{1,0:T(8,128)(2,1)S(1)}, u32[]{:S(2)}, u32[]{:S(2)}) collective-permute-start(bf16[144,128]{1,0:T(8,128)(2,1)S(1)} %add_convert_fusion.1.a), channel_id=1, source_target_pairs={{0,64},{64,0},{128,192},{192,128},{1,65},{65,1},{129,193},{193,129... | collective-permute-start | bytes 110600 | tf_op jit(solution)/shard_map/ppermute | solution.py:416
  46.7 7.1 %collective-permute-start.6 = (bf16[8,256,128]{2,1,0:T(8,128)(2,1)S(1)}, bf16[8,256,128]{2,1,0:T(8,128)(2,1)S(1)}, u32[]{:S(2)}, u32[]{:S(2)}) collective-permute-start(bf16[8,256,128]{2,1,0:T(8,128)(2,1)S(1)} %all_to_all.10.ma_ref), channel_id=1, source_target_pairs={{0,1},{1,0},{2,3},{3,2},{4,5},{5,4},{6,7},{7,6},{8,9},{9,8},{10,11... | collective-permute-start | bytes 1572872 | tf_op jit(solution)/shard_map/ppermute | solution.py:412
  53.8 32.8 %copy-start.2 = (bf16[128,8192]{1,0:T(8,128)(2,1)S(1)}, bf16[128,8192]{1,0:T(8,128)(2,1)}, u32[]{:S(2)}) copy-start(bf16[128,8192]{1,0:T(8,128)(2,1)} %get-tuple-element.35.lb_ref) | copy-start | bytes 6291460
  58.2 6.4 %collective-permute-start.14 = (bf16[144,512]{1,0:T(8,128)(2,1)S(1)}, bf16[144,512]{1,0:T(8,128)(2,1)S(1)}, u32[]{:S(2)}, u32[]{:S(2)}) collective-permute-start(bf16[144,512]{1,0:T(8,128)(2,1)S(1)} %get-tuple-element.36.refs_0_), channel_id=1, source_target_pairs={{0,2},{2,4},{4,6},{6,8},{8,10},{10,12},{12,14},{14,0},{1,3},{3,5},... | collective-permute-start | bytes 442376 | tf_op jit(solution)/shard_map/ppermute | solution.py:438
  58.5 6.3 %collective-permute-start.8 = (bf16[144,512]{1,0:T(8,128)(2,1)S(1)}, bf16[144,512]{1,0:T(8,128)(2,1)S(1)}, u32[]{:S(2)}, u32[]{:S(2)}) collective-permute-start(bf16[144,512]{1,0:T(8,128)(2,1)S(1)} %get-tuple-element.37), channel_id=1, source_target_pairs={{0,14},{2,0},{4,2},{6,4},{8,6},{10,8},{12,10},{14,12},{1,15},{3,1}... | collective-permute-start | bytes 442376 | tf_op jit(solution)/shard_map/ppermute | solution.py:441
  64.7 5.3 %collective-permute-start.15 = (bf16[144,512]{1,0:T(8,128)(2,1)S(1)}, bf16[144,512]{1,0:T(8,128)(2,1)S(1)}, u32[]{:S(2)}, u32[]{:S(2)}) collective-permute-start(bf16[144,512]{1,0:T(8,128)(2,1)S(1)} %pad_maximum_fusion.2), channel_id=1, source_target_pairs={{0,2},{2,4},{4,6},{6,8},{8,10},{10,12},{12,14},{14,0},{1,3},{3,5},... | collective-permute-start | bytes 442376 | tf_op jit(solution)/shard_map/ppermute | solution.py:438
  70.0 28.1 %copy-start.5 = (f32[8,8192]{1,0:T(8,128)S(1)}, f32[8,8192]{1,0:T(8,128)}, u32[]{:S(2)}) copy-start(f32[8,8192]{1,0:T(8,128)} %get-tuple-element.33.r_ref) | copy-start | bytes 786436
  70.0 5.2 %collective-permute-start.10 = (bf16[144,512]{1,0:T(8,128)(2,1)S(1)}, bf16[144,512]{1,0:T(8,128)(2,1)S(1)}, u32[]{:S(2)}, u32[]{:S(2)}) collective-permute-start(bf16[144,512]{1,0:T(8,128)(2,1)S(1)} %pad_maximum_fusion), channel_id=1, source_target_pairs={{0,14},{2,0},{4,2},{6,4},{8,6},{10,8},{12,10},{14,12},{1,15},{3,1}... | collective-permute-start | bytes 442376 | tf_op jit(solution)/shard_map/ppermute | solution.py:441
  70.1 27.9 %copy-start.3 = (bf16[128,8192]{1,0:T(8,128)(2,1)S(1)}, bf16[128,8192]{1,0:T(8,128)(2,1)}, u32[]{:S(2)}) copy-start(bf16[128,8192]{1,0:T(8,128)(2,1)} %get-tuple-element.34.e_ref) | copy-start | bytes 6291460
  70.1 5.5 %collective-permute-start.16 = (bf16[144,512]{1,0:T(8,128)(2,1)S(1)}, bf16[144,512]{1,0:T(8,128)(2,1)S(1)}, u32[]{:S(2)}, u32[]{:S(2)}) collective-permute-start(bf16[144,512]{1,0:T(8,128)(2,1)S(1)} %pad_maximum_fusion.3), channel_id=1, source_target_pairs={{0,2},{2,4},{4,6},{6,8},{8,10},{10,12},{12,14},{14,0},{1,3},{3,5},... | collective-permute-start | bytes 442376 | tf_op jit(solution)/shard_map/ppermute | solution.py:438
  71.8 5.4 %collective-permute-start.7 = (bf16[144,512]{1,0:T(8,128)(2,1)S(1)}, bf16[144,512]{1,0:T(8,128)(2,1)S(1)}, u32[]{:S(2)}, u32[]{:S(2)}) collective-permute-start(bf16[144,512]{1,0:T(8,128)(2,1)S(1)} %get-tuple-element.36.refs_0_), channel_id=1, source_target_pairs={{0,1},{1,0},{2,3},{3,2},{4,5},{5,4},{6,7},{7,6},{8,9},{9,8},{10,11... | collective-permute-start | bytes 442376 | tf_op jit(solution)/shard_map/ppermute | solution.py:412
  74.7 6.6 %collective-permute-start.9 = (bf16[144,512]{1,0:T(8,128)(2,1)S(1)}, bf16[144,512]{1,0:T(8,128)(2,1)S(1)}, u32[]{:S(2)}, u32[]{:S(2)}) collective-permute-start(bf16[144,512]{1,0:T(8,128)(2,1)S(1)} %collective-permute-done.8.refs_2_), channel_id=1, source_target_pairs={{0,1},{1,0},{2,3},{3,2},{4,5},{5,4},{6,7},{7,6},{8,9},{9,8},{10,11... | collective-permute-start | bytes 442376 | tf_op jit(solution)/shard_map/ppermute | solution.py:412
  74.7 6.7 %collective-permute-start.21 = (bf16[144,512]{1,0:T(8,128)(2,1)S(1)}, bf16[144,512]{1,0:T(8,128)(2,1)S(1)}, u32[]{:S(2)}, u32[]{:S(2)}) collective-permute-start(bf16[144,512]{1,0:T(8,128)(2,1)S(1)} %collective-permute-done.14.refs_14_), channel_id=1, source_target_pairs={{0,1},{1,0},{2,3},{3,2},{4,5},{5,4},{6,7},{7,6},{8,9},{9,8},{10,11... | collective-permute-start | bytes 442376 | tf_op jit(solution)/shard_map/ppermute | solution.py:412
  75.6 6.2 %collective-permute-start.12 = (bf16[144,512]{1,0:T(8,128)(2,1)S(1)}, bf16[144,512]{1,0:T(8,128)(2,1)S(1)}, u32[]{:S(2)}, u32[]{:S(2)}) collective-permute-start(bf16[144,512]{1,0:T(8,128)(2,1)S(1)} %pad_maximum_fusion.1), channel_id=1, source_target_pairs={{0,14},{2,0},{4,2},{6,4},{8,6},{10,8},{12,10},{14,12},{1,15},{3,1}... | collective-permute-start | bytes 442376 | tf_op jit(solution)/shard_map/ppermute | solution.py:441
  76.3 8.0 %collective-permute-start.17 = (bf16[144,512]{1,0:T(8,128)(2,1)S(1)}, bf16[144,512]{1,0:T(8,128)(2,1)S(1)}, u32[]{:S(2)}, u32[]{:S(2)}) collective-permute-start(bf16[144,512]{1,0:T(8,128)(2,1)S(1)} %pad_maximum_fusion.4), channel_id=1, source_target_pairs={{0,2},{2,4},{4,6},{6,8},{8,10},{10,12},{12,14},{14,0},{1,3},{3,5},... | collective-permute-start | bytes 442376 | tf_op jit(solution)/shard_map/ppermute | solution.py:438
  77.3 8.3 %collective-permute-start.20 = (bf16[144,512]{1,0:T(8,128)(2,1)S(1)}, bf16[144,512]{1,0:T(8,128)(2,1)S(1)}, u32[]{:S(2)}, u32[]{:S(2)}) collective-permute-start(bf16[144,512]{1,0:T(8,128)(2,1)S(1)} %collective-permute-done.15.refs_12_), channel_id=1, source_target_pairs={{0,1},{1,0},{2,3},{3,2},{4,5},{5,4},{6,7},{7,6},{8,9},{9,8},{10,11... | collective-permute-start | bytes 442376 | tf_op jit(solution)/shard_map/ppermute | solution.py:412
  81.3 4.3 %collective-permute-start.19 = (bf16[144,512]{1,0:T(8,128)(2,1)S(1)}, bf16[144,512]{1,0:T(8,128)(2,1)S(1)}, u32[]{:S(2)}, u32[]{:S(2)}) collective-permute-start(bf16[144,512]{1,0:T(8,128)(2,1)S(1)} %collective-permute-done.16.refs_10_), channel_id=1, source_target_pairs={{0,1},{1,0},{2,3},{3,2},{4,5},{5,4},{6,7},{7,6},{8,9},{9,8},{10,11... | collective-permute-start | bytes 442376 | tf_op jit(solution)/shard_map/ppermute | solution.py:412
  81.4 4.3 %collective-permute-start.11 = (bf16[144,512]{1,0:T(8,128)(2,1)S(1)}, bf16[144,512]{1,0:T(8,128)(2,1)S(1)}, u32[]{:S(2)}, u32[]{:S(2)}) collective-permute-start(bf16[144,512]{1,0:T(8,128)(2,1)S(1)} %collective-permute-done.10.refs_4_), channel_id=1, source_target_pairs={{0,1},{1,0},{2,3},{3,2},{4,5},{5,4},{6,7},{7,6},{8,9},{9,8},{10,11... | collective-permute-start | bytes 442376 | tf_op jit(solution)/shard_map/ppermute | solution.py:412
  81.8 3.8 %collective-permute-start.13 = (bf16[144,512]{1,0:T(8,128)(2,1)S(1)}, bf16[144,512]{1,0:T(8,128)(2,1)S(1)}, u32[]{:S(2)}, u32[]{:S(2)}) collective-permute-start(bf16[144,512]{1,0:T(8,128)(2,1)S(1)} %collective-permute-done.12.refs_6_), channel_id=1, source_target_pairs={{0,1},{1,0},{2,3},{3,2},{4,5},{5,4},{6,7},{7,6},{8,9},{9,8},{10,11... | collective-permute-start | bytes 442376 | tf_op jit(solution)/shard_map/ppermute | solution.py:412
  84.3 2.3 %collective-permute-start.18 = (bf16[144,512]{1,0:T(8,128)(2,1)S(1)}, bf16[144,512]{1,0:T(8,128)(2,1)S(1)}, u32[]{:S(2)}, u32[]{:S(2)}) collective-permute-start(bf16[144,512]{1,0:T(8,128)(2,1)S(1)} %collective-permute-done.17.refs_8_), channel_id=1, source_target_pairs={{0,1},{1,0},{2,3},{3,2},{4,5},{5,4},{6,7},{7,6},{8,9},{9,8},{10,11... | collective-permute-start | bytes 442376 | tf_op jit(solution)/shard_map/ppermute | solution.py:412
  86.6 11.4 %copy-start = (bf16[8192,128]{1,0:T(8,128)(2,1)S(1)}, bf16[8192,128]{1,0:T(8,128)(2,1)}, u32[]{:S(2)}) copy-start(bf16[8192,128]{1,0:T(8,128)(2,1)} %f_ref.3) | copy-start | bytes 6291460
  86.6 11.4 %copy-start.1 = (bf16[128,8192]{1,0:T(8,128)(2,1)S(1)}, bf16[128,8192]{1,0:T(8,128)(2,1)}, u32[]{:S(2)}) copy-start(bf16[128,8192]{1,0:T(8,128)(2,1)} %get-tuple-element.28.ft_ref) | copy-start | bytes 6291460
  86.6 11.4 %copy-start.6 = (bf16[512,128]{1,0:T(8,128)(2,1)S(1)}, bf16[512,128]{1,0:T(8,128)(2,1)}, u32[]{:S(2)}) copy-start(bf16[512,128]{1,0:T(8,128)(2,1)} %get-tuple-element.40.am_ref) | copy-start | bytes 393220
  87.4 4.1 %collective-permute-start.24 = (bf16[128,128]{1,0:T(8,128)(2,1)S(1)}, bf16[128,128]{1,0:T(8,128)(2,1)S(1)}, u32[]{:S(2)}, u32[]{:S(2)}) collective-permute-start(bf16[128,128]{1,0:T(8,128)(2,1)S(1)} %get-tuple-element.45), channel_id=1, source_target_pairs={{0,48},{16,32},{32,16},{48,0},{1,49},{17,33},{33,17},{49,1},{2,50}... | collective-permute-start | bytes 98312 | tf_op jit(solution)/shard_map/ppermute | solution.py:416
  88.6 4.3 %collective-permute-start.23 = (bf16[128,128]{1,0:T(8,128)(2,1)S(1)}, bf16[128,128]{1,0:T(8,128)(2,1)S(1)}, u32[]{:S(2)}, u32[]{:S(2)}) collective-permute-start(bf16[128,128]{1,0:T(8,128)(2,1)S(1)} %get-tuple-element.45), channel_id=1, source_target_pairs={{0,32},{16,48},{32,0},{48,16},{1,33},{17,49},{33,1},{49,17},{2,34}... | collective-permute-start | bytes 98312 | tf_op jit(solution)/shard_map/ppermute | solution.py:416
  89.2 3.7 %collective-permute-start.22 = (bf16[128,128]{1,0:T(8,128)(2,1)S(1)}, bf16[128,128]{1,0:T(8,128)(2,1)S(1)}, u32[]{:S(2)}, u32[]{:S(2)}) collective-permute-start(bf16[128,128]{1,0:T(8,128)(2,1)S(1)} %get-tuple-element.45), channel_id=1, source_target_pairs={{0,16},{16,0},{32,48},{48,32},{1,17},{17,1},{33,49},{49,33},{2,18}... | collective-permute-start | bytes 98312 | tf_op jit(solution)/shard_map/ppermute | solution.py:416
  92.9 4.1 %collective-permute-start.27 = (bf16[128,128]{1,0:T(8,128)(2,1)S(1)}, bf16[128,128]{1,0:T(8,128)(2,1)S(1)}, u32[]{:S(2)}, u32[]{:S(2)}) collective-permute-start(bf16[128,128]{1,0:T(8,128)(2,1)S(1)} %add_convert_fusion.2.p0), channel_id=1, source_target_pairs={{0,192},{64,128},{128,64},{192,0},{1,193},{65,129},{129,65},{193,1... | collective-permute-start | bytes 98312 | tf_op jit(solution)/shard_map/ppermute | solution.py:416
  93.8 4.3 %collective-permute-start.26 = (bf16[128,128]{1,0:T(8,128)(2,1)S(1)}, bf16[128,128]{1,0:T(8,128)(2,1)S(1)}, u32[]{:S(2)}, u32[]{:S(2)}) collective-permute-start(bf16[128,128]{1,0:T(8,128)(2,1)S(1)} %add_convert_fusion.2.p0), channel_id=1, source_target_pairs={{0,128},{64,192},{128,0},{192,64},{1,129},{65,193},{129,1},{193,65... | collective-permute-start | bytes 98312 | tf_op jit(solution)/shard_map/ppermute | solution.py:416
  94.8 3.3 %collective-permute-start.25 = (bf16[128,128]{1,0:T(8,128)(2,1)S(1)}, bf16[128,128]{1,0:T(8,128)(2,1)S(1)}, u32[]{:S(2)}, u32[]{:S(2)}) collective-permute-start(bf16[128,128]{1,0:T(8,128)(2,1)S(1)} %add_convert_fusion.2.p0), channel_id=1, source_target_pairs={{0,64},{64,0},{128,192},{192,128},{1,65},{65,1},{129,193},{193,129... | collective-permute-start | bytes 98312 | tf_op jit(solution)/shard_map/ppermute | solution.py:416
  105.1 4.2 %collective-permute-start.30 = (bf16[176,128]{1,0:T(8,128)(2,1)S(1)}, bf16[176,128]{1,0:T(8,128)(2,1)S(1)}, u32[]{:S(2)}, u32[]{:S(2)}) collective-permute-start(bf16[176,128]{1,0:T(8,128)(2,1)S(1)} %constant_dynamic-update-slice_fusion), channel_id=1, source_target_pairs={{0,48},{16,32},{32,16},{48,0},{1,49},{17,33},{33,17},{49,1},{2,50}... | collective-permute-start | bytes 135176 | tf_op jit(solution)/shard_map/ppermute | solution.py:416
  106.8 4.4 %collective-permute-start.29 = (bf16[176,128]{1,0:T(8,128)(2,1)S(1)}, bf16[176,128]{1,0:T(8,128)(2,1)S(1)}, u32[]{:S(2)}, u32[]{:S(2)}) collective-permute-start(bf16[176,128]{1,0:T(8,128)(2,1)S(1)} %constant_dynamic-update-slice_fusion), channel_id=1, source_target_pairs={{0,32},{16,48},{32,0},{48,16},{1,33},{17,49},{33,1},{49,17},{2,34}... | collective-permute-start | bytes 135176 | tf_op jit(solution)/shard_map/ppermute | solution.py:416
  107.6 3.5 %collective-permute-start.28 = (bf16[176,128]{1,0:T(8,128)(2,1)S(1)}, bf16[176,128]{1,0:T(8,128)(2,1)S(1)}, u32[]{:S(2)}, u32[]{:S(2)}) collective-permute-start(bf16[176,128]{1,0:T(8,128)(2,1)S(1)} %constant_dynamic-update-slice_fusion), channel_id=1, source_target_pairs={{0,16},{16,0},{32,48},{48,32},{1,17},{17,1},{33,49},{49,33},{2,18}... | collective-permute-start | bytes 135176 | tf_op jit(solution)/shard_map/ppermute | solution.py:416
  111.2 4.2 %collective-permute-start.33 = (bf16[176,128]{1,0:T(8,128)(2,1)S(1)}, bf16[176,128]{1,0:T(8,128)(2,1)S(1)}, u32[]{:S(2)}, u32[]{:S(2)}) collective-permute-start(bf16[176,128]{1,0:T(8,128)(2,1)S(1)} %add_convert_fusion.p0), channel_id=1, source_target_pairs={{0,192},{64,128},{128,64},{192,0},{1,193},{65,129},{129,65},{193,1... | collective-permute-start | bytes 135176 | tf_op jit(solution)/shard_map/ppermute | solution.py:416
  113.3 4.4 %collective-permute-start.32 = (bf16[176,128]{1,0:T(8,128)(2,1)S(1)}, bf16[176,128]{1,0:T(8,128)(2,1)S(1)}, u32[]{:S(2)}, u32[]{:S(2)}) collective-permute-start(bf16[176,128]{1,0:T(8,128)(2,1)S(1)} %add_convert_fusion.p0), channel_id=1, source_target_pairs={{0,128},{64,192},{128,0},{192,64},{1,129},{65,193},{129,1},{193,65... | collective-permute-start | bytes 135176 | tf_op jit(solution)/shard_map/ppermute | solution.py:416
  114.1 3.6 %collective-permute-start.31 = (bf16[176,128]{1,0:T(8,128)(2,1)S(1)}, bf16[176,128]{1,0:T(8,128)(2,1)S(1)}, u32[]{:S(2)}, u32[]{:S(2)}) collective-permute-start(bf16[176,128]{1,0:T(8,128)(2,1)S(1)} %add_convert_fusion.p0), channel_id=1, source_target_pairs={{0,64},{64,0},{128,192},{192,128},{1,65},{65,1},{129,193},{193,129... | collective-permute-start | bytes 135176 | tf_op jit(solution)/shard_map/ppermute | solution.py:416
  118.3 6.9 %collective-permute-start.34 = (f32[40,128]{1,0:T(8,128)S(1)}, f32[40,128]{1,0:T(8,128)S(1)}, u32[]{:S(2)}, u32[]{:S(2)}) collective-permute-start(f32[40,128]{1,0:T(8,128)S(1)} %get-tuple-element.46), channel_id=1, source_target_pairs={{0,1},{1,0},{2,3},{3,2},{4,5},{5,4},{6,7},{7,6},{8,9},{9,8},{10,11... | collective-permute-start | bytes 61448 | tf_op jit(solution)/shard_map/ppermute | solution.py:412
